TPU v7x, 32 devices: a whole 2x2x4 slice. The times are simulated.
32 devices in a mesh: grp: 2 (over y), occ: 4 (over x, core), aux: 4 (over z).
Axes of the slice: x: 2, y: 2, z: 4, core: 2. Of those that a mesh axis runs over, the one named last changes fastest.
Arguments:
- bmat: bfloat16 [8, 6144, 1536], P(('grp', 'occ'), 'aux'), parts along dimension 0, may hold values from -0.625 to 0.625
- eps_occ: float32 [8], P('grp'), parts along dimension 0, may hold values from -1.5 to -0.5
- eps_vir: float32 [3072], P('grp'), parts along dimension 0, may hold values from 0.2 to 3
- occ_label: int32 [8], P('grp'), parts along dimension 0, may hold values from 0 to 3, each once
Outputs:
- gamma: bfloat16 [8, 6144, 1536], P(('grp', 'occ'), 'aux'), parts along dimension 0
- density: float32 [3072, 1536], P(('grp', 'aux'), 'occ'), parts along dimension 0
There are 2 independent parts, one for each index of `grp`. A program takes and returns all parts, laid end to end along the dimension named above; each array names one. Nothing has to cross between parts.
Inputs may be any that keep to these rules, and one draw needn't show every extreme that they name: `occ_label`: a permutation: each label appears once.
All inputs are finite; a program needn't handle non-finite values.
Results may differ from a plain program's by a relative error of at most 0.008.
Values may be sent and summed in bfloat16 or wider, within the bound.
No kernel may reach another device: no remote copies, remote signals or barrier semaphores. Data moves between devices by JAX's collectives and lax.ppermute only.
A program may use at most 128 MiB of HBM per device.

v0:
```python
import jax
import jax.numpy as jnp
from jax import lax
from jax.sharding import PartitionSpec as P


def shifted(shard, axis, by):
    devices = lax.axis_size(axis)
    return lax.ppermute(shard, axis, [(i, (i + by) % devices) for i in range(devices)])


def send_back(returned):
    return shifted(returned, "occ", -1)


def slab_total(received):
    return jnp.sum(received.astype(jnp.float32), axis=0)


def shards(bmat, eps_occ, eps_vir, occ_label):
    count = lax.axis_size("occ")
    slabs = lax.axis_size("aux")
    place = lax.axis_index("occ")
    slab_index = lax.axis_index("aux")
    nvirt = eps_vir.shape[0]
    rows = nvirt // slabs
    labels = jnp.arange(count, dtype=jnp.int32)
    energy = jnp.sum(
        eps_occ[None, :] * (occ_label[:, None] == labels[None, :]).astype(jnp.float32), axis=1
    )
    prev_place = (place + count - 1) % count
    energy_own = lax.dynamic_index_in_dim(energy, place, 0, keepdims=False)
    energy_prev = lax.dynamic_index_in_dim(energy, prev_place, 0, keepdims=False)
    mine = bmat[0]
    other = shifted(bmat, "occ", 1)[0]
    partial_value = lax.dot_general(
        mine, other, (((0,), (0,)), ((), ())), preferred_element_type=jnp.float32
    )
    blocks = partial_value.astype(jnp.bfloat16).reshape(slabs, rows, nvirt)
    summed = slab_total(lax.all_to_all(blocks, "aux", split_axis=0, concat_axis=0, tiled=True))
    eps_rows = lax.dynamic_slice_in_dim(eps_vir, slab_index * rows, rows)
    denom = eps_rows[:, None] + eps_vir[None, :] - energy_own - energy_prev
    amp_rows = (summed / denom).astype(jnp.bfloat16)
    amp_full = lax.all_gather(amp_rows, "aux", axis=0, tiled=True)
    amp_wide = amp_full.astype(jnp.float32)
    tilde = (2.0 * amp_wide - amp_wide.T).astype(jnp.bfloat16)
    contract = (((1,), (1,)), ((), ()))
    owned = lax.dot_general(other, tilde, contract, preferred_element_type=jnp.float32)
    returned = jnp.dot(mine, tilde, preferred_element_type=jnp.float32).astype(jnp.bfloat16)
    arrived = send_back(returned)
    gamma = (owned + arrived.astype(jnp.float32)).astype(jnp.bfloat16)[None]
    dens_rows = lax.dot_general(amp_rows, tilde, contract, preferred_element_type=jnp.float32)
    dens_rows = dens_rows * nvirt ** (-0.5)
    density = lax.psum_scatter(
        dens_rows.astype(jnp.bfloat16), "occ", scatter_dimension=1, tiled=True
    ).astype(jnp.float32)
    return (gamma, density)


def solution(mesh):
    return jax.shard_map(
        shards,
        mesh=mesh,
        in_specs=(P(("grp", "occ"), "aux", None), P("grp"), P("grp"), P("grp")),
        out_specs=(P(("grp", "occ"), "aux", None), P(("grp", "aux"), "occ")),
        check_vma=False,
    )
```

profile of v0, /device:TPU:1, one launch (start us, length us, event | category | flops | bytes accessed | tf_op | source)
XLA Modules:
  0.0 388.9 jit_solution(2708048333555516488)
XLA Ops:
  7.2 2.7 collective-permute-start
  9.8 51.4 %collective-permute-done = bf16[1,1536,1536]{2,1,0:T(8,128)(2,1)S(1)} collective-permute-done((bf16[1,1536,1536]{2,1,0:T(8,128)(2,1)}, bf16[1,1536,1536]{2,1,0:T(8,128)(2,1)S(1)}, u32[]{:S(2)}, u32[]{:S(2)}) %collective-permute-start) | collective-permute-done | bytes 4718624 | tf_op jit(solution)/shard_map/ppermute | solution.py:9
  61.2 13.2 %convolution_convert_fusion.1 = bf16[1536,1536]{1,0:T(8,128)(2,1)} fusion(bf16[1,1536,1536]{2,1,0:T(8,128)(2,1)S(1)} %collective-permute-done, bf16[1,1536,1536]{2,1,0:T(8,128)(2,1)} %param.4), kind=kOutput, calls=%fused_computation.6 | convolution fusion | flops 7250116608 | bytes 14155776 | tf_op jit(solution)/shard_map/dot_general | solution.py:36
  74.4 5.1 %all-to-all-start = ((bf16[4,384,1536]{2,1,0:T(8,128)(2,1)}), bf16[4,384,1536]{2,1,0:T(8,128)(2,1)}, u32[]{:S(2)}, u32[]{:S(2)}) async-start(bf16[4,384,1536]{2,1,0:T(8,128)(2,1)} %bitcast.33), calls=%async_computation | async-start | bytes 9437184 | tf_op jit(solution)/shard_map/all_to_all | solution.py:40
  79.5 0.0 all-gather.2.cloned.1.call-start
  79.6 0.1 dynamic_slice.10
  79.7 0.2 select_reduce_fusion
  79.9 0.7 fusion.9
  80.5 102.8 %all-to-all-done = bf16[4,384,1536]{2,1,0:T(8,128)(2,1)} async-done(((bf16[4,384,1536]{2,1,0:T(8,128)(2,1)}), bf16[4,384,1536]{2,1,0:T(8,128)(2,1)}, u32[]{:S(2)}, u32[]{:S(2)}) %all-to-all-start) | async-done | bytes 4718624 | tf_op jit(solution)/shard_map/all_to_all | solution.py:40
  183.4 3.4 convert_reduce_fusion
  186.7 2.8 divide_convert_fusion
  189.7 88.6 %all-gather.2.cloned.1.call-done = bf16[1536,1536]{1,0:T(8,128)(2,1)} async-done(((bf16[384,1536]{1,0:T(8,128)(2,1)}), bf16[1536,1536]{1,0:T(8,128)(2,1)}) %all-gather.2.cloned.1.call-update) | async-done | bytes 4718608 | tf_op jit(solution)/shard_map/all_gather | solution.py:44
  278.3 7.6 %copy.10 = f32[1536,1536]{0,1:T(8,128)} copy(bf16[1536,1536]{1,0:T(8,128)(2,1)} %all-gather.2.cloned.1.call-done) | data formatting | bytes 14155776 | tf_op jit(solution)/shard_map/convert_element_type | solution.py:45
  285.9 6.8 %fusion.1 = bf16[1536,1536]{0,1:T(8,128)(2,1)S(1)} fusion(f32[1536,1536]{0,1:T(8,128)} %copy.10, bf16[1536,1536]{1,0:T(8,128)(2,1)} %all-gather.2.cloned.1.call-done), kind=kLoop, calls=%fused_computation.3 | loop fusion | flops 9437184 | bytes 18874368 | tf_op jit(solution)/shard_map/convert_element_type | solution.py:46
  292.7 9.5 %fusion.3 = bf16[1536,1536]{0,1:T(8,128)(2,1)} fusion(bf16[1536,1536]{0,1:T(8,128)(2,1)S(1)} %fusion.1, bf16[1,1536,1536]{2,1,0:T(8,128)(2,1)S(1)} %bitcast.37), kind=kOutput, calls=%fused_computation.8 | convolution fusion | flops 7250116608 | bytes 14155776 | tf_op jit(solution)/shard_map/dot_general | solution.py:49
  302.1 0.6 collective-permute-start.1
  302.7 2.0 fusion.8
  304.7 1.4 copy.12
  306.2 27.2 %reduce-scatter.4.cloned.1.call-done = bf16[384,384]{1,0:T(8,128)(2,1)} async-done(((bf16[1536,384]{1,0:T(8,128)(2,1)}), bf16[384,384]{1,0:T(8,128)(2,1)}) %reduce-scatter.4.cloned.1.call-update) | async-done | bytes 294928
  333.4 1.2 copy.13
  334.6 0.9 convert_element_type.44
  335.4 26.9 %collective-permute-done.1 = bf16[1536,1536]{0,1:T(8,128)(2,1)} collective-permute-done((bf16[1536,1536]{0,1:T(8,128)(2,1)}, bf16[1536,1536]{0,1:T(8,128)(2,1)}, u32[]{:S(2)}, u32[]{:S(2)}) %collective-permute-start.1) | collective-permute-done | bytes 4718624 | tf_op jit(solution)/shard_map/ppermute | solution.py:9
  362.3 13.1 %fusion.2 = bf16[1,1536,1536]{1,2,0:T(8,128)(2,1)} fusion(bf16[1536,1536]{0,1:T(8,128)(2,1)} %collective-permute-done.1, bf16[1536,1536]{0,1:T(8,128)(2,1)} %copy-done.1, bf16[1,1536,1536]{2,1,0:T(8,128)(2,1)} %copy-done.3), kind=kOutput, calls=%fused_computation.7 | convolution fusion | flops 7254835200 | bytes 18874368 | tf_op jit(solution)/shard_map/dot_general | solution.py:48
  375.4 6.6 %copy.11 = bf16[1,1536,1536]{2,1,0:T(8,128)(2,1)} copy(bf16[1,1536,1536]{1,2,0:T(8,128)(2,1)} %fusion.2) | data formatting | bytes 9437184
  (20 shorter events, 0.1 us)
Async XLA Ops:
  7.2 54.0 %collective-permute-start = (bf16[1,1536,1536]{2,1,0:T(8,128)(2,1)}, bf16[1,1536,1536]{2,1,0:T(8,128)(2,1)S(1)}, u32[]{:S(2)}, u32[]{:S(2)}) collective-permute-start(bf16[1,1536,1536]{2,1,0:T(8,128)(2,1)} %param.4), channel_id=1, source_target_pairs={{0,4},{4,8},{8,12},{12,0},{1,5},{5,9},{9,13},{13,1},{2,6},{6,10},{... | collective-permute-start | bytes 14155784 | tf_op jit(solution)/shard_map/ppermute | solution.py:9
  61.2 13.2 %copy-start.3 = (bf16[1,1536,1536]{2,1,0:T(8,128)(2,1)}, bf16[1,1536,1536]{2,1,0:T(8,128)(2,1)S(1)}, u32[]{:S(2)}) copy-start(bf16[1,1536,1536]{2,1,0:T(8,128)(2,1)S(1)} %collective-permute-done) | copy-start | bytes 14155780
  74.4 5.2 %copy-start.2 = (f32[1536]{0:T(1024)S(1)}, f32[1536]{0:T(1024)}, u32[]{:S(2)}) copy-start(f32[1536]{0:T(1024)} %param.6) | copy-start | bytes 18436
  74.4 5.3 %copy-start.4 = (f32[4]{0:T(128)S(1)}, f32[4]{0:T(128)}, u32[]{:S(2)}) copy-start(f32[4]{0:T(128)} %param.5) | copy-start | bytes 52
  74.4 5.3 %copy-start.5 = (s32[4]{0:T(128)S(1)}, s32[4]{0:T(128)}, u32[]{:S(2)}) copy-start(s32[4]{0:T(128)} %param.7) | copy-start | bytes 52
  74.4 109.0 %all-to-all-start = ((bf16[4,384,1536]{2,1,0:T(8,128)(2,1)}), bf16[4,384,1536]{2,1,0:T(8,128)(2,1)}, u32[]{:S(2)}, u32[]{:S(2)}) async-start(bf16[4,384,1536]{2,1,0:T(8,128)(2,1)} %bitcast.33), calls=%async_computation | async-start | bytes 9437184 | tf_op jit(solution)/shard_map/all_to_all | solution.py:40
  79.5 198.8 %all-gather.2.cloned.1.call-start = ((), (), s32[]{:S(2)}) async-start(), calls=%async_computation.2 | async-start | bytes 5898240 | tf_op jit(solution)/shard_map/all_gather | solution.py:44
  189.6 143.8 %reduce-scatter.4.cloned.1.call-start = ((), (), s32[]{:S(2)}) async-start(), calls=%async_computation.3 | async-start | bytes 1474560
  278.3 14.3 %slice-start = ((s8[4718592]{0:T(1024)(128)(4,1)}), s8[524288]{0:T(1024)(128)(4,1)S(1)}, s32[]{:S(2)}) async-start(s8[4718592]{0:T(1024)(128)(4,1)} %bitcast.36), calls=%async_computation.4 | async-start | bytes 1048576
  285.8 6.8 %slice-start.1 = ((s8[4718592]{0:T(1024)(128)(4,1)}), s8[4194304]{0:T(1024)(128)(4,1)S(1)}, s32[]{:S(2)}) async-start(s8[4718592]{0:T(1024)(128)(4,1)} %bitcast.36), calls=%async_computation.5 | async-start | bytes 8388608
  292.7 10.1 %copy-start.1 = (bf16[1536,1536]{0,1:T(8,128)(2,1)}, bf16[1536,1536]{0,1:T(8,128)(2,1)S(1)}, u32[]{:S(2)}) copy-start(bf16[1536,1536]{0,1:T(8,128)(2,1)S(1)} %fusion.1) | copy-start | bytes 14155780
  292.7 10.1 %copy-start = (bf16[384,1536]{1,0:T(8,128)(2,1)S(1)}, bf16[384,1536]{1,0:T(8,128)(2,1)}, u32[]{:S(2)}) copy-start(bf16[384,1536]{1,0:T(8,128)(2,1)} %divide_convert_fusion) | copy-start | bytes 3538948
  302.1 60.2 %collective-permute-start.1 = (bf16[1536,1536]{0,1:T(8,128)(2,1)}, bf16[1536,1536]{0,1:T(8,128)(2,1)}, u32[]{:S(2)}, u32[]{:S(2)}) collective-permute-start(bf16[1536,1536]{0,1:T(8,128)(2,1)} %fusion.3), channel_id=1, source_target_pairs={{0,12},{4,0},{8,4},{12,8},{1,13},{5,1},{9,5},{13,9},{2,14},{6,2},{... | collective-permute-start | bytes 14155784 | tf_op jit(solution)/shard_map/ppermute | solution.py:9
Sparse Core Ops, SparseCore 0:
  189.7 88.5 all-gather.1
  306.3 27.0 reduce-scatter.3
where the time goes:
time: 390 us; the launch traced here: 389 us
  waiting for transfers between devices  297 us (76%)
  matrix products  37.8 us (10%)
  local copies, waits for them, and re-layouts  17.5 us (4%)
  between operations  14.2 us (4%)
  other arithmetic  14 us (4%)
  starting transfers between devices  8.42 us (2%)
    all_to_all x1, waiting for transfers between devices, shards(): lax.all_to_all(blocks, 'aux', split_axis=0, concat_axis=0, tiled=True)  103 us
    all_gather x1, waiting for transfers between devices, shards(): amp_full = lax.all_gather(amp_rows, 'aux', axis=0, tiled=True)  88.6 us
    ppermute x2, waiting for transfers between devices, shifted(): lax.ppermute(shard, axis, [(i, (i + by) % devices) for i in range(devices)])  78.3 us
    unnamed x3, waiting for transfers between devices  27.2 us
    dot_general x1, matrix products, shards(): lax.dot_general(mine, other, (((0,), (0,)), ((), ())), preferred_element_...  13.2 us
    dot_general x1, matrix products, shards(): lax.dot_general(other, tilde, contract, preferred_element_type=jnp.float32)  13.1 us
    dot_general x1, matrix products, shards(): jnp.dot(mine, tilde, preferred_element_type=jnp.float32)  9.46 us
    unnamed x19, local copies, waits for them, and re-layouts  9.22 us
  transfers between devices with their start and end apart: 5, of which 5 were waited for; matrix products, arithmetic and copies ran while one was open for 2% of the time, Pallas kernels for 0%

commit v1 on v0

v1 whole, which is shorter than its diff:
```python
import jax
import jax.numpy as jnp
from jax import lax
from jax.sharding import PartitionSpec as P

CHUNKS = 4
F32 = jnp.float32
BF16 = jnp.bfloat16


def contract(left, right, dim_left, dim_right):
    return lax.dot_general(
        left, right, (((dim_left,), (dim_right,)), ((), ())), preferred_element_type=F32
    )


def slab_sum_scale(part, denom, slabs, slab_index):
    if slabs != 4:
        rows, cols = part.shape
        blocks = part.reshape(slabs, rows // slabs, cols)
        blocks = lax.all_to_all(blocks, "aux", split_axis=0, concat_axis=0, tiled=True)
        total = jnp.sum(blocks.astype(F32), axis=0).astype(BF16)
        total = lax.all_gather(total, "aux", axis=0, tiled=True)
        return (total.astype(F32) / denom).astype(BF16)
    inner = (slab_index == 1) | (slab_index == 2)
    inward = lax.ppermute(part, "aux", [(0, 1), (3, 2)])
    half = (part.astype(F32) + inward.astype(F32)).astype(BF16)
    across = lax.ppermute(half, "aux", [(1, 2), (2, 1)])
    amp = ((half.astype(F32) + across.astype(F32)) / denom).astype(BF16)
    outward = lax.ppermute(amp, "aux", [(1, 0), (2, 3)])
    return jnp.where(inner, amp, outward)


def shards(bmat, eps_occ, eps_vir, occ_label):
    count = lax.axis_size("occ")
    slabs = lax.axis_size("aux")
    place = lax.axis_index("occ")
    slab_index = lax.axis_index("aux")
    chips = count // 2
    chip, core = place // 2, place % 2
    first = core == 0
    nvirt = eps_vir.shape[0]
    half = nvirt // 2
    width = half // CHUNKS
    labels = jnp.arange(count, dtype=jnp.int32)
    energy = jnp.sum(
        eps_occ[None, :] * (occ_label[:, None] == labels[None, :]).astype(F32), axis=1
    )
    swap_pairs = [(i, i ^ 1) for i in range(count)]

    def energy_at(row):
        return lax.dynamic_index_in_dim(energy, (row + count) % count, 0, keepdims=False)

    def swapped(value):
        return lax.ppermute(value, "occ", swap_pairs)

    energy_cross = energy_at(2 * chip), energy_at(2 * chip - 1)
    energy_local = energy_at(2 * chip + 1), energy_at(2 * chip)

    mine = bmat[0]
    partner = swapped(mine)
    even = jnp.where(first, mine, partner)
    odd = jnp.where(first, partner, mine)

    def arrived(j):
        start = j * width
        sent = jnp.where(
            first, partner[:, start : start + width], mine[:, half + start : half + start + width]
        )
        return lax.ppermute(sent, "occ", [(i, (i + 2) % count) for i in range(count)])

    incoming = [arrived(j) for j in range(CHUNKS)]

    def scaled(part, j, energies):
        eps_rows = lax.dynamic_slice_in_dim(eps_vir, core * half + j * width, width)
        denom = eps_rows[:, None] + eps_vir[None, :] - energies[0] - energies[1]
        return slab_sum_scale(part, denom, slabs, slab_index)

    def cross(j):
        return scaled(contract(incoming[j], even, 0, 0).astype(BF16), j, energy_cross)

    def local(j):
        cols = lax.dynamic_slice_in_dim(even, core * half + j * width, width, axis=1)
        return scaled(contract(cols, odd, 0, 0).astype(BF16), j, energy_local)

    local_parts = [local(0)]
    cross_parts = [cross(j) for j in range(CHUNKS)]
    local_parts += [local(j) for j in range(1, CHUNKS)]

    def whole(parts):
        mine_rows = jnp.concatenate(parts, axis=0)
        other_rows = swapped(mine_rows)
        return jnp.concatenate(
            [jnp.where(first, mine_rows, other_rows), jnp.where(first, other_rows, mine_rows)], axis=0
        )

    def mixed(amp_t, straight):
        wide = amp_t.astype(F32)
        turned = wide.T
        return jnp.where(straight, 2.0 * wide - turned, 2.0 * turned - wide).astype(BF16)

    def density_part(amp_t):
        rows = nvirt // slabs
        cols = nvirt // count
        amp_rows = lax.dynamic_slice_in_dim(amp_t, slab_index * rows, rows, axis=1)
        pieces = []
        for ahead in range(chips):
            start = (2 * ((chip + ahead) % chips) + core) * cols
            straight = lax.dynamic_slice_in_dim(amp_t, start, cols, axis=1).astype(F32)
            turned = lax.dynamic_slice_in_dim(amp_t, start, cols, axis=0).astype(F32).T
            tilde_t = (2.0 * straight - turned).astype(BF16)
            pieces.append(contract(amp_rows, tilde_t, 0, 0))
        return pieces

    cross_t = whole(cross_parts)
    cross_mix = mixed(cross_t, first)
    received = jnp.concatenate(incoming, axis=1)
    upper = swapped(received)
    left = jnp.where(first, jnp.concatenate([received, upper], axis=1), partner)
    step = nvirt // CHUNKS
    cross_out, returned = [], []
    back_pairs = [(i, (i - 2) % count) for i in range(1, count, 2)]
    for j in range(CHUNKS):
        out = jnp.dot(left, cross_mix[:, j * step : (j + 1) * step], preferred_element_type=F32)
        back = lax.ppermute(out.astype(BF16), "occ", back_pairs)
        cross_out.append(out)
        returned.append(back)
    cross_density = density_part(cross_t)

    local_t = whole(local_parts)
    local_mix = mixed(local_t, ~first)
    local_out = jnp.dot(partner, local_mix, preferred_element_type=F32)
    local_density = density_part(local_t)

    scale = nvirt ** (-0.5)
    pieces = [(a + b) * scale for a, b in zip(cross_density, local_density)]
    density = pieces[0]
    for ahead in range(1, chips):
        pairs = [(i, (i + 2 * ahead) % count) for i in range(count)]
        density = density + lax.ppermute(pieces[ahead].astype(BF16), "occ", pairs).astype(F32)

    gamma = []
    for j in range(CHUNKS):
        term = jnp.where(first, cross_out[j], returned[j].astype(F32))
        gamma.append((local_out[:, j * step : (j + 1) * step] + term).astype(BF16))
    return jnp.concatenate(gamma, axis=1)[None], density


def solution(mesh):
    return jax.shard_map(
        shards,
        mesh=mesh,
        in_specs=(P(("grp", "occ"), "aux", None), P("grp"), P("grp"), P("grp")),
        out_specs=(P(("grp", "occ"), "aux", None), P(("grp", "aux"), "occ")),
        check_vma=False,
    )
```

time: 390 us -> 530 us (1.36); the launches traced: 389 us -> 520 us
  starting transfers between devices: 8.42 us -> 65.2 us
  other arithmetic: 14 us -> 62.7 us
  local copies, waits for them, and re-layouts: 17.5 us -> 65.8 us
  waiting for transfers between devices: 297 us -> 266 us
  matrix products: 37.8 us -> 59.2 us
  between operations: 14.2 us -> 1.9 us
    ppermute x2 -> x37, waiting for transfers between devices: 78.3 us -> 266 us  [the longest x8 119 us: slab_sum_scale(): outward = lax.ppermute(amp, 'aux', [(1, 0), (2, 3)])]
    all_to_all x1 -> x0, waiting for transfers between devices: 103 us -> none  [shards(): lax.all_to_all(blocks, 'aux', split_axis=0, concat_axis=0, tiled=True)]
    all_gather x1 -> x0, waiting for transfers between devices: 88.6 us -> none  [shards(): amp_full = lax.all_gather(amp_rows, 'aux', axis=0, tiled=True)]
    ppermute x2 -> x37, starting transfers between devices: 3.24 us -> 65.2 us  [the longest x8 21.5 us: slab_sum_scale(): inward = lax.ppermute(part, 'aux', [(0, 1), (3, 2)])]
    unnamed x3 -> x0, waiting for transfers between devices: 27.2 us -> none
    dot_general x4 -> x17, matrix products: 37.8 us -> 59.2 us  [the longest x12 22.7 us: contract(): lax.dot_general(left, right, (((dim_left,), (dim_right,)), ((), ())), pre...]
    select_n x0 -> x12, other arithmetic: none -> 18.9 us  [the longest x1 6.82 us: shards(): even = jnp.where(first, mine, partner)]
    convert_element_type x3 -> x14, other arithmetic: 10.5 us -> 25.6 us  [the longest x2 7.76 us: slab_sum_scale(): amp = ((half.astype(F32) + across.astype(F32)) / denom).astype(BF16)]
  transfers between devices with their start and end apart: 5 -> 37, of which waited for: 5 -> 21; matrix products, arithmetic and copies ran while one was open for 2% -> 17% of each run, Pallas kernels for 0% -> 0%
where the time goes in v1:
time: 530 us; the launch traced here: 520 us
  waiting for transfers between devices  266 us (50%)
  local copies, waits for them, and re-layouts  65.8 us (12%)
  starting transfers between devices  65.2 us (12%)
  other arithmetic  62.7 us (12%)
  matrix products  59.2 us (11%)
    ppermute x8, waiting for transfers between devices, slab_sum_scale(): outward = lax.ppermute(amp, 'aux', [(1, 0), (2, 3)])  119 us
    ppermute x8, waiting for transfers between devices, slab_sum_scale(): inward = lax.ppermute(part, 'aux', [(0, 1), (3, 2)])  72.5 us
    ppermute x4, waiting for transfers between devices, arrived(): lax.ppermute(sent, 'occ', [(i, (i + 2) % count) for i in range(count)])  46 us
    dot_general x12, matrix products, contract(): lax.dot_general(left, right, (((dim_left,), (dim_right,)), ((), ())), pre...  22.7 us
    ppermute x8, starting transfers between devices, slab_sum_scale(): inward = lax.ppermute(part, 'aux', [(0, 1), (3, 2)])  21.5 us
    dot_general x1, matrix products, shards(): local_out = jnp.dot(partner, local_mix, preferred_element_type=F32)  18.5 us
    dot_general x4, matrix products, shards(): jnp.dot(left, cross_mix[:, j * step:(j + 1) * step], preferred_element_ty...  18 us
    ppermute x4, waiting for transfers between devices, shards(): back = lax.ppermute(out.astype(BF16), 'occ', back_pairs)  17.3 us
  transfers between devices with their start and end apart: 37, of which 21 were waited for; matrix products, arithmetic and copies ran while one was open for 17% of the time, Pallas kernels for 0%

profile of v1, /device:TPU:1, one launch (start us, length us, event | category | flops | bytes accessed | tf_op | source)
XLA Modules:
  0.0 520.5 jit_solution(3324510597824322127)
XLA Ops:
  0.8 8.2 %collective-permute-done = bf16[1536,1536]{1,0:T(8,128)(2,1)} collective-permute-done((bf16[1536,1536]{1,0:T(8,128)(2,1)}, bf16[1536,1536]{1,0:T(8,128)(2,1)}, u32[]{:S(2)}, u32[]{:S(2)}) %collective-permute-start) | collective-permute-done | bytes 4718624 | tf_op jit(solution)/shard_map/ppermute | solution.py:55
  21.8 9.9 %collective-permute-done.17 = bf16[1536,192]{0,1:T(8,128)(2,1)S(1)} collective-permute-done((bf16[1536,192]{0,1:T(8,128)(2,1)}, bf16[1536,192]{0,1:T(8,128)(2,1)S(1)}, u32[]{:S(2)}, u32[]{:S(2)}) %collective-permute-start.17) | collective-permute-done | bytes 589856 | tf_op jit(solution)/shard_map/ppermute | solution.py:70
  32.1 12.4 %collective-permute-done.15 = bf16[1536,192]{0,1:T(8,128)(2,1)S(1)} collective-permute-done((bf16[1536,192]{0,1:T(8,128)(2,1)}, bf16[1536,192]{0,1:T(8,128)(2,1)S(1)}, u32[]{:S(2)}, u32[]{:S(2)}) %collective-permute-start.15) | collective-permute-done | bytes 589856 | tf_op jit(solution)/shard_map/ppermute | solution.py:70
  45.2 11.8 %collective-permute-done.14 = bf16[1536,192]{0,1:T(8,128)(2,1)S(1)} collective-permute-done((bf16[1536,192]{0,1:T(8,128)(2,1)}, bf16[1536,192]{0,1:T(8,128)(2,1)S(1)}, u32[]{:S(2)}, u32[]{:S(2)}) %collective-permute-start.14) | collective-permute-done | bytes 589856 | tf_op jit(solution)/shard_map/ppermute | solution.py:70
  57.9 11.9 %collective-permute-done.16 = bf16[1536,192]{0,1:T(8,128)(2,1)} collective-permute-done((bf16[1536,192]{0,1:T(8,128)(2,1)}, bf16[1536,192]{0,1:T(8,128)(2,1)}, u32[]{:S(2)}, u32[]{:S(2)}) %collective-permute-start.16) | collective-permute-done | bytes 589856 | tf_op jit(solution)/shard_map/ppermute | solution.py:70
  79.2 8.4 %concatenate.25 = bf16[1536,1536]{1,0:T(8,128)(2,1)} concatenate(bf16[1536,192]{1,0:T(8,128)(2,1)S(1)} %copy.50, bf16[1536,192]{1,0:T(8,128)(2,1)S(1)} %copy.51, bf16[1536,192]{1,0:T(8,128)(2,1)S(1)} %copy.52, bf16[1536,192]{1,0:T(8,128)(2,1)S(1)} %copy.53, bf16[1536,768]{1,0:T(8,128)(2,1)} %collective-permute-done.18), dimensions={1} | concatenate | bytes 9437184 | tf_op jit(solution)/shard_map/concatenate | solution.py:119
  118.5 8.4 %collective-permute-done.4 = bf16[192,1536]{1,0:T(8,128)(2,1)S(1)} collective-permute-done((bf16[192,1536]{1,0:T(8,128)(2,1)S(1)}, bf16[192,1536]{1,0:T(8,128)(2,1)S(1)}, u32[]{:S(2)}, u32[]{:S(2)}) %collective-permute-start.4) | collective-permute-done | bytes 589856 | tf_op jit(solution)/shard_map/ppermute | solution.py:26
  131.1 8.4 %collective-permute-done.7 = bf16[192,1536]{1,0:T(8,128)(2,1)S(1)} collective-permute-done((bf16[192,1536]{1,0:T(8,128)(2,1)S(1)}, bf16[192,1536]{1,0:T(8,128)(2,1)S(1)}, u32[]{:S(2)}, u32[]{:S(2)}) %collective-permute-start.7) | collective-permute-done | bytes 589856 | tf_op jit(solution)/shard_map/ppermute | solution.py:26
  143.8 21.0 %collective-permute-done.19 = bf16[192,1536]{1,0:T(8,128)(2,1)S(1)} collective-permute-done((bf16[192,1536]{1,0:T(8,128)(2,1)S(1)}, bf16[192,1536]{1,0:T(8,128)(2,1)S(1)}, u32[]{:S(2)}, u32[]{:S(2)}) %collective-permute-start.19) | collective-permute-done | bytes 589856 | tf_op jit(solution)/shard_map/ppermute | solution.py:26
  165.6 11.8 %collective-permute-done.22 = bf16[192,1536]{1,0:T(8,128)(2,1)S(1)} collective-permute-done((bf16[192,1536]{1,0:T(8,128)(2,1)S(1)}, bf16[192,1536]{1,0:T(8,128)(2,1)S(1)}, u32[]{:S(2)}, u32[]{:S(2)}) %collective-permute-start.22) | collective-permute-done | bytes 589856 | tf_op jit(solution)/shard_map/ppermute | solution.py:26
  178.3 11.8 %collective-permute-done.25 = bf16[192,1536]{1,0:T(8,128)(2,1)S(1)} collective-permute-done((bf16[192,1536]{1,0:T(8,128)(2,1)S(1)}, bf16[192,1536]{1,0:T(8,128)(2,1)S(1)}, u32[]{:S(2)}, u32[]{:S(2)}) %collective-permute-start.25) | collective-permute-done | bytes 589856 | tf_op jit(solution)/shard_map/ppermute | solution.py:26
  191.6 11.1 %collective-permute-done.28 = bf16[192,1536]{1,0:T(8,128)(2,1)S(1)} collective-permute-done((bf16[192,1536]{1,0:T(8,128)(2,1)S(1)}, bf16[192,1536]{1,0:T(8,128)(2,1)S(1)}, u32[]{:S(2)}, u32[]{:S(2)}) %collective-permute-start.28) | collective-permute-done | bytes 589856 | tf_op jit(solution)/shard_map/ppermute | solution.py:26
  220.1 45.1 %collective-permute-done.3 = bf16[192,1536]{1,0:T(8,128)(2,1)S(1)} collective-permute-done((bf16[192,1536]{1,0:T(8,128)(2,1)S(1)}, bf16[192,1536]{1,0:T(8,128)(2,1)S(1)}, u32[]{:S(2)}, u32[]{:S(2)}) %collective-permute-start.3) | collective-permute-done | bytes 589856 | tf_op jit(solution)/shard_map/ppermute | solution.py:30
  266.6 11.1 %collective-permute-done.6 = bf16[192,1536]{1,0:T(8,128)(2,1)S(1)} collective-permute-done((bf16[192,1536]{1,0:T(8,128)(2,1)S(1)}, bf16[192,1536]{1,0:T(8,128)(2,1)S(1)}, u32[]{:S(2)}, u32[]{:S(2)}) %collective-permute-start.6) | collective-permute-done | bytes 589856 | tf_op jit(solution)/shard_map/ppermute | solution.py:30
  277.8 25.3 %collective-permute-done.9 = bf16[192,1536]{1,0:T(8,128)(2,1)S(1)} collective-permute-done((bf16[192,1536]{1,0:T(8,128)(2,1)S(1)}, bf16[192,1536]{1,0:T(8,128)(2,1)S(1)}, u32[]{:S(2)}, u32[]{:S(2)}) %collective-permute-start.9) | collective-permute-done | bytes 589856 | tf_op jit(solution)/shard_map/ppermute | solution.py:30
  303.2 12.5 %collective-permute-done.12 = bf16[192,1536]{1,0:T(8,128)(2,1)S(1)} collective-permute-done((bf16[192,1536]{1,0:T(8,128)(2,1)S(1)}, bf16[192,1536]{1,0:T(8,128)(2,1)S(1)}, u32[]{:S(2)}, u32[]{:S(2)}) %collective-permute-start.12) | collective-permute-done | bytes 589856 | tf_op jit(solution)/shard_map/ppermute | solution.py:30
  317.4 10.3 %collective-permute-start.13 = (bf16[768,1536]{1,0:T(8,128)(2,1)}, bf16[768,1536]{1,0:T(8,128)(2,1)}, u32[]{:S(2)}, u32[]{:S(2)}) collective-permute-start(bf16[768,1536]{1,0:T(8,128)(2,1)} %pad_maximum_fusion.2), channel_id=1, source_target_pairs={{0,4},{4,0},{8,12},{12,8},{1,5},{5,1},{9,13},{13,9},{2,6},{6,2},{1... | collective-permute-start | bytes 7077896 | tf_op jit(solution)/shard_map/ppermute | solution.py:55
  332.8 12.0 %collective-permute-done.27 = bf16[192,1536]{1,0:T(8,128)(2,1)S(1)} collective-permute-done((bf16[192,1536]{1,0:T(8,128)(2,1)}, bf16[192,1536]{1,0:T(8,128)(2,1)S(1)}, u32[]{:S(2)}, u32[]{:S(2)}) %collective-permute-start.27) | collective-permute-done | bytes 589856 | tf_op jit(solution)/shard_map/ppermute | solution.py:30
  344.8 12.6 %collective-permute-done.30 = bf16[192,1536]{1,0:T(8,128)(2,1)S(1)} collective-permute-done((bf16[192,1536]{1,0:T(8,128)(2,1)}, bf16[192,1536]{1,0:T(8,128)(2,1)S(1)}, u32[]{:S(2)}, u32[]{:S(2)}) %collective-permute-start.30) | collective-permute-done | bytes 589856 | tf_op jit(solution)/shard_map/ppermute | solution.py:30
  373.5 7.4 %copy.41 = f32[1536,1536]{1,0:T(8,128)} copy(bf16[1536,1536]{0,1:T(8,128)(2,1)} %copy.38) | data formatting | bytes 14155776 | tf_op jit(solution)/shard_map/convert_element_type | solution.py:98
  396.8 9.6 %copy.54 = f32[1536,1536]{0,1:T(8,128)} copy(f32[1536,1536]{1,0:T(8,128)} %fusion.6) | data formatting | bytes 18874368 | tf_op jit(solution)/shard_map/convert_element_type | solution.py:98
  441.9 9.6 %copy.40 = f32[1536,1536]{1,0:T(8,128)} copy(f32[1536,1536]{0,1:T(8,128)} %broadcast_multiply_fusion) | data formatting | bytes 18874368 | tf_op jit(solution)/shard_map/mul | solution.py:100
  462.1 18.5 %convolution_bitcast_fusion = f32[1536,1536]{0,1:T(8,128)} fusion(bf16[1536,1536]{1,0:T(8,128)(2,1)} %collective-permute-done, f32[1536,1536]{1,0:T(8,128)} %copy.40, f32[1536,1536]{1,0:T(8,128)} %copy.41, bf16[1536,1536]{0,1:T(8,128)(2,1)} %copy.38, pred[]{:T(512)S(6)} %not.3), kind=kOutput, calls=%fused_computation.10 | convolution fusion | flops 7261913088 | bytes 37748736 | tf_op jit(solution)/shard_map/dot_general | solution.py:132
  494.1 12.6 %collective-permute-done.32 = bf16[1536,384]{0,1:T(8,128)(2,1)} collective-permute-done((bf16[1536,384]{0,1:T(8,128)(2,1)}, bf16[1536,384]{0,1:T(8,128)(2,1)}, u32[]{:S(2)}, u32[]{:S(2)}) %collective-permute-start.32) | collective-permute-done | bytes 1179680 | tf_op jit(solution)/shard_map/ppermute | solution.py:125
  (188 shorter events, 196.9 us)
Async XLA Ops:
  19.2 37.8 %collective-permute-start.14 = (bf16[1536,192]{0,1:T(8,128)(2,1)}, bf16[1536,192]{0,1:T(8,128)(2,1)S(1)}, u32[]{:S(2)}, u32[]{:S(2)}) collective-permute-start(bf16[1536,192]{0,1:T(8,128)(2,1)} %copy.42), channel_id=1, source_target_pairs={{0,8},{4,12},{8,0},{12,4},{1,9},{5,13},{9,1},{13,5},{2,10},{6,14},... | collective-permute-start | bytes 1769480 | tf_op jit(solution)/shard_map/ppermute | solution.py:70
  21.8 48.0 %collective-permute-start.16 = (bf16[1536,192]{0,1:T(8,128)(2,1)}, bf16[1536,192]{0,1:T(8,128)(2,1)}, u32[]{:S(2)}, u32[]{:S(2)}) collective-permute-start(bf16[1536,192]{0,1:T(8,128)(2,1)} %copy.44), channel_id=1, source_target_pairs={{0,8},{4,12},{8,0},{12,4},{1,9},{5,13},{9,1},{13,5},{2,10},{6,14},... | collective-permute-start | bytes 1769480 | tf_op jit(solution)/shard_map/ppermute | solution.py:70
  104.3 35.2 %collective-permute-start.7 = (bf16[192,1536]{1,0:T(8,128)(2,1)S(1)}, bf16[192,1536]{1,0:T(8,128)(2,1)S(1)}, u32[]{:S(2)}, u32[]{:S(2)}) collective-permute-start(bf16[192,1536]{1,0:T(8,128)(2,1)S(1)} %convolution_convert_fusion.5), channel_id=1, source_target_pairs={{0,1},{3,2},{4,5},{7,6},{8,9},{11,10},{12,13},{15,14},{16,17},{19,... | collective-permute-start | bytes 1769480 | tf_op jit(solution)/shard_map/ppermute | solution.py:26
  105.6 85.2 %collective-permute-start.10 = (bf16[192,1536]{1,0:T(8,128)(2,1)S(1)}, bf16[192,1536]{1,0:T(8,128)(2,1)S(1)}, u32[]{:S(2)}, u32[]{:S(2)}) collective-permute-start(bf16[192,1536]{1,0:T(8,128)(2,1)S(1)} %convolution_convert_fusion.4), channel_id=1, source_target_pairs={{0,1},{3,2},{4,5},{7,6},{8,9},{11,10},{12,13},{15,14},{16,17},{19,... | collective-permute-start | bytes 1769480 | tf_op jit(solution)/shard_map/ppermute | solution.py:26
  108.1 56.7 %collective-permute-start.19 = (bf16[192,1536]{1,0:T(8,128)(2,1)S(1)}, bf16[192,1536]{1,0:T(8,128)(2,1)S(1)}, u32[]{:S(2)}, u32[]{:S(2)}) collective-permute-start(bf16[192,1536]{1,0:T(8,128)(2,1)S(1)} %convolution_convert_fusion.3), channel_id=1, source_target_pairs={{0,1},{3,2},{4,5},{7,6},{8,9},{11,10},{12,13},{15,14},{16,17},{19,... | collective-permute-start | bytes 1769480 | tf_op jit(solution)/shard_map/ppermute | solution.py:26
  114.2 63.2 %collective-permute-start.22 = (bf16[192,1536]{1,0:T(8,128)(2,1)S(1)}, bf16[192,1536]{1,0:T(8,128)(2,1)S(1)}, u32[]{:S(2)}, u32[]{:S(2)}) collective-permute-start(bf16[192,1536]{1,0:T(8,128)(2,1)S(1)} %convolution_convert_fusion.2), channel_id=1, source_target_pairs={{0,1},{3,2},{4,5},{7,6},{8,9},{11,10},{12,13},{15,14},{16,17},{19,... | collective-permute-start | bytes 1769480 | tf_op jit(solution)/shard_map/ppermute | solution.py:26
  126.8 63.2 %collective-permute-start.25 = (bf16[192,1536]{1,0:T(8,128)(2,1)S(1)}, bf16[192,1536]{1,0:T(8,128)(2,1)S(1)}, u32[]{:S(2)}, u32[]{:S(2)}) collective-permute-start(bf16[192,1536]{1,0:T(8,128)(2,1)S(1)} %convolution_convert_fusion.1), channel_id=1, source_target_pairs={{0,1},{3,2},{4,5},{7,6},{8,9},{11,10},{12,13},{15,14},{16,17},{19,... | collective-permute-start | bytes 1769480 | tf_op jit(solution)/shard_map/ppermute | solution.py:26
  139.5 63.2 %collective-permute-start.28 = (bf16[192,1536]{1,0:T(8,128)(2,1)S(1)}, bf16[192,1536]{1,0:T(8,128)(2,1)S(1)}, u32[]{:S(2)}, u32[]{:S(2)}) collective-permute-start(bf16[192,1536]{1,0:T(8,128)(2,1)S(1)} %convolution_convert_fusion), channel_id=1, source_target_pairs={{0,1},{3,2},{4,5},{7,6},{8,9},{11,10},{12,13},{15,14},{16,17},{19,... | collective-permute-start | bytes 1769480 | tf_op jit(solution)/shard_map/ppermute | solution.py:26
  164.8 38.6 %collective-permute-start.2 = (bf16[192,1536]{1,0:T(8,128)(2,1)S(1)}, bf16[192,1536]{1,0:T(8,128)(2,1)S(1)}, u32[]{:S(2)}, u32[]{:S(2)}) collective-permute-start(bf16[192,1536]{1,0:T(8,128)(2,1)S(1)} %add_convert_fusion.7), channel_id=1, source_target_pairs={{1,2},{2,1},{5,6},{6,5},{9,10},{10,9},{13,14},{14,13},{17,18},{18,... | collective-permute-start | bytes 1769480 | tf_op jit(solution)/shard_map/ppermute | solution.py:28
  177.4 27.0 %collective-permute-start.5 = (bf16[192,1536]{1,0:T(8,128)(2,1)S(1)}, bf16[192,1536]{1,0:T(8,128)(2,1)S(1)}, u32[]{:S(2)}, u32[]{:S(2)}) collective-permute-start(bf16[192,1536]{1,0:T(8,128)(2,1)S(1)} %add_convert_fusion.6), channel_id=1, source_target_pairs={{1,2},{2,1},{5,6},{6,5},{9,10},{10,9},{13,14},{14,13},{17,18},{18,... | collective-permute-start | bytes 1769480 | tf_op jit(solution)/shard_map/ppermute | solution.py:28
  210.4 120.1 %collective-permute-start.21 = (bf16[192,1536]{1,0:T(8,128)(2,1)S(1)}, bf16[192,1536]{1,0:T(8,128)(2,1)}, u32[]{:S(2)}, u32[]{:S(2)}) collective-permute-start(bf16[192,1536]{1,0:T(8,128)(2,1)S(1)} %get-tuple-element.25), channel_id=1, source_target_pairs={{1,0},{2,3},{5,4},{6,7},{9,8},{10,11},{13,12},{14,15},{17,16},{18,... | collective-permute-start | bytes 1769480 | tf_op jit(solution)/shard_map/ppermute | solution.py:30
  211.7 53.5 %collective-permute-start.3 = (bf16[192,1536]{1,0:T(8,128)(2,1)S(1)}, bf16[192,1536]{1,0:T(8,128)(2,1)S(1)}, u32[]{:S(2)}, u32[]{:S(2)}) collective-permute-start(bf16[192,1536]{1,0:T(8,128)(2,1)S(1)} %get-tuple-element.26), channel_id=1, source_target_pairs={{1,0},{2,3},{5,4},{6,7},{9,8},{10,11},{13,12},{14,15},{17,16},{18,... | collective-permute-start | bytes 1769480 | tf_op jit(solution)/shard_map/ppermute | solution.py:30
  213.0 64.8 %collective-permute-start.6 = (bf16[192,1536]{1,0:T(8,128)(2,1)S(1)}, bf16[192,1536]{1,0:T(8,128)(2,1)S(1)}, u32[]{:S(2)}, u32[]{:S(2)}) collective-permute-start(bf16[192,1536]{1,0:T(8,128)(2,1)S(1)} %get-tuple-element.33), channel_id=1, source_target_pairs={{1,0},{2,3},{5,4},{6,7},{9,8},{10,11},{13,12},{14,15},{17,16},{18,... | collective-permute-start | bytes 1769480 | tf_op jit(solution)/shard_map/ppermute | solution.py:30
  214.3 117.3 %collective-permute-start.24 = (bf16[192,1536]{1,0:T(8,128)(2,1)S(1)}, bf16[192,1536]{1,0:T(8,128)(2,1)}, u32[]{:S(2)}, u32[]{:S(2)}) collective-permute-start(bf16[192,1536]{1,0:T(8,128)(2,1)S(1)} %get-tuple-element.34), channel_id=1, source_target_pairs={{1,0},{2,3},{5,4},{6,7},{9,8},{10,11},{13,12},{14,15},{17,16},{18,... | collective-permute-start | bytes 1769480 | tf_op jit(solution)/shard_map/ppermute | solution.py:30
  215.6 87.5 %collective-permute-start.9 = (bf16[192,1536]{1,0:T(8,128)(2,1)S(1)}, bf16[192,1536]{1,0:T(8,128)(2,1)S(1)}, u32[]{:S(2)}, u32[]{:S(2)}) collective-permute-start(bf16[192,1536]{1,0:T(8,128)(2,1)S(1)} %get-tuple-element.35), channel_id=1, source_target_pairs={{1,0},{2,3},{5,4},{6,7},{9,8},{10,11},{13,12},{14,15},{17,16},{18,... | collective-permute-start | bytes 1769480 | tf_op jit(solution)/shard_map/ppermute | solution.py:30
  265.2 50.5 %collective-permute-start.12 = (bf16[192,1536]{1,0:T(8,128)(2,1)S(1)}, bf16[192,1536]{1,0:T(8,128)(2,1)S(1)}, u32[]{:S(2)}, u32[]{:S(2)}) collective-permute-start(bf16[192,1536]{1,0:T(8,128)(2,1)S(1)} %get-tuple-element.32), channel_id=1, source_target_pairs={{1,0},{2,3},{5,4},{6,7},{9,8},{10,11},{13,12},{14,15},{17,16},{18,... | collective-permute-start | bytes 1769480 | tf_op jit(solution)/shard_map/ppermute | solution.py:30
  317.4 42.5 %collective-permute-start.13 = (bf16[768,1536]{1,0:T(8,128)(2,1)}, bf16[768,1536]{1,0:T(8,128)(2,1)}, u32[]{:S(2)}, u32[]{:S(2)}) collective-permute-start(bf16[768,1536]{1,0:T(8,128)(2,1)} %pad_maximum_fusion.2), channel_id=1, source_target_pairs={{0,4},{4,0},{8,12},{12,8},{1,5},{5,1},{9,13},{13,9},{2,6},{6,2},{1... | collective-permute-start | bytes 7077896 | tf_op jit(solution)/shard_map/ppermute | solution.py:55
  329.0 28.4 %collective-permute-start.30 = (bf16[192,1536]{1,0:T(8,128)(2,1)}, bf16[192,1536]{1,0:T(8,128)(2,1)S(1)}, u32[]{:S(2)}, u32[]{:S(2)}) collective-permute-start(bf16[192,1536]{1,0:T(8,128)(2,1)} %get-tuple-element.31), channel_id=1, source_target_pairs={{1,0},{2,3},{5,4},{6,7},{9,8},{10,11},{13,12},{14,15},{17,16},{18,... | collective-permute-start | bytes 1769480 | tf_op jit(solution)/shard_map/ppermute | solution.py:30
  359.1 29.2 %collective-permute-start.31 = (bf16[768,1536]{1,0:T(8,128)(2,1)}, bf16[768,1536]{1,0:T(8,128)(2,1)}, u32[]{:S(2)}, u32[]{:S(2)}) collective-permute-start(bf16[768,1536]{1,0:T(8,128)(2,1)} %pad_maximum_fusion.4), channel_id=1, source_target_pairs={{0,4},{4,0},{8,12},{12,8},{1,5},{5,1},{9,13},{13,9},{2,6},{6,2},{1... | collective-permute-start | bytes 7077896 | tf_op jit(solution)/shard_map/ppermute | solution.py:55
  440.8 44.5 %collective-permute-start.36 = (bf16[384,384]{1,0:T(8,128)(2,1)}, bf16[384,384]{1,0:T(8,128)(2,1)}, u32[]{:S(2)}, u32[]{:S(2)}) collective-permute-start(bf16[384,384]{1,0:T(8,128)(2,1)} %fusion.22), channel_id=1, source_target_pairs={{0,8},{4,12},{8,0},{12,4},{1,9},{5,13},{9,1},{13,5},{2,10},{6,14},... | collective-permute-start | bytes 884744 | tf_op jit(solution)/shard_map/ppermute | solution.py:140
  451.5 37.9 %collective-permute-start.35 = (bf16[1536,384]{0,1:T(8,128)(2,1)}, bf16[1536,384]{0,1:T(8,128)(2,1)}, u32[]{:S(2)}, u32[]{:S(2)}) collective-permute-start(bf16[1536,384]{0,1:T(8,128)(2,1)} %get-tuple-element.46), channel_id=1, source_target_pairs={{4,12},{12,4},{5,13},{13,5},{6,14},{14,6},{7,15},{15,7},{20,28},{2... | collective-permute-start | bytes 3538952 | tf_op jit(solution)/shard_map/ppermute | solution.py:125
  453.7 35.7 %collective-permute-start.34 = (bf16[1536,384]{0,1:T(8,128)(2,1)}, bf16[1536,384]{0,1:T(8,128)(2,1)}, u32[]{:S(2)}, u32[]{:S(2)}) collective-permute-start(bf16[1536,384]{0,1:T(8,128)(2,1)} %get-tuple-element.48), channel_id=1, source_target_pairs={{4,12},{12,4},{5,13},{13,5},{6,14},{14,6},{7,15},{15,7},{20,28},{2... | collective-permute-start | bytes 3538952 | tf_op jit(solution)/shard_map/ppermute | solution.py:125
  456.8 37.2 %collective-permute-start.33 = (bf16[1536,384]{0,1:T(8,128)(2,1)}, bf16[1536,384]{0,1:T(8,128)(2,1)}, u32[]{:S(2)}, u32[]{:S(2)}) collective-permute-start(bf16[1536,384]{0,1:T(8,128)(2,1)} %get-tuple-element.50), channel_id=1, source_target_pairs={{4,12},{12,4},{5,13},{13,5},{6,14},{14,6},{7,15},{15,7},{20,28},{2... | collective-permute-start | bytes 3538952 | tf_op jit(solution)/shard_map/ppermute | solution.py:125
  459.0 47.7 %collective-permute-start.32 = (bf16[1536,384]{0,1:T(8,128)(2,1)}, bf16[1536,384]{0,1:T(8,128)(2,1)}, u32[]{:S(2)}, u32[]{:S(2)}) collective-permute-start(bf16[1536,384]{0,1:T(8,128)(2,1)} %get-tuple-element.44), channel_id=1, source_target_pairs={{4,12},{12,4},{5,13},{13,5},{6,14},{14,6},{7,15},{15,7},{20,28},{2... | collective-permute-start | bytes 3538952 | tf_op jit(solution)/shard_map/ppermute | solution.py:125
  (47 other events, 634.4 us)

commit v2 on v0

v2 whole, which is shorter than its diff:
```python
import functools

import jax
import jax.numpy as jnp
from jax import lax
from jax.experimental import pallas as pl
from jax.experimental.pallas import tpu as pltpu
from jax.sharding import PartitionSpec as P

F32 = jnp.float32
BF16 = jnp.bfloat16
PIECES = 3
LIMIT = 48 * 1024 * 1024


def contract(left, right, dim_left, dim_right):
    return lax.dot_general(
        left, right, (((dim_left,), (dim_right,)), ((), ())), preferred_element_type=F32
    )


class Order:
    def __init__(self, first):
        self.last = first

    def ready(self, *values):
        return lax.optimization_barrier((*values, self.last))[:-1]

    def step(self, work, *values):
        result = work(*self.ready(*values))
        self.last = result
        return result

    def send(self, value, axis, pairs, *others):
        return lax.ppermute(self.ready(value, *others)[0], axis, pairs)


def mix_kernel(half, band, rows, cols, straight_core, place, *refs):
    pieces, (mix, dens, amp_t, amp, sems) = refs[: 2 * PIECES], refs[2 * PIECES :]
    core, slab, chip = place[0], place[1], place[2]
    nvirt = 2 * half
    width = half // PIECES
    step = pl.program_id(0)

    @pl.when(step == 0)
    def _():
        copies = []
        for i, piece in enumerate(pieces):
            side = core if i < PIECES else 1 - core
            start = pl.multiple_of(side * half + (i % PIECES) * width, width)
            copies.append(pltpu.make_async_copy(piece, amp_t.at[pl.ds(start, width), :], sems.at[i]))
        for copy in copies:
            copy.start()
        for copy in copies:
            copy.wait()

    straight = core == straight_core
    here = jnp.where(straight, 2.0, -1.0).astype(F32)
    there = jnp.where(straight, -1.0, 2.0).astype(F32)
    start = pl.multiple_of(step * band, band)
    for j in range(nvirt // band):
        tile = amp_t[pl.ds(start, band), j * band : (j + 1) * band].astype(F32)
        turned = amp_t[j * band : (j + 1) * band, pl.ds(start, band)].astype(F32).T
        amp[pl.ds(start, band), j * band : (j + 1) * band] = turned.astype(BF16)
        mix[:, j * band : (j + 1) * band] = (here * tile + there * turned).astype(BF16)

    @pl.when(step == nvirt // band - 1)
    def _():
        chips = dens.shape[0]
        left = amp[pl.ds(pl.multiple_of(slab * rows, rows), rows), :]
        for ahead in range(chips):
            at = pl.multiple_of((2 * lax.rem(chip + ahead, chips) + core) * cols, cols)
            tilde = 2.0 * amp[pl.ds(at, cols), :].astype(F32) - amp_t[pl.ds(at, cols), :].astype(F32)
            dens[ahead] = contract(left, tilde.astype(BF16), 1, 1)


def mix(place, own, other, straight_core, slabs, count):
    width, nvirt = own[0].shape
    rows, cols, chips = nvirt // slabs, nvirt // count, count // 2
    band = 256
    return pl.pallas_call(
        functools.partial(mix_kernel, nvirt // 2, band, rows, cols, straight_core),
        grid_spec=pltpu.PrefetchScalarGridSpec(
            num_scalar_prefetch=1,
            grid=(nvirt // band,),
            in_specs=[pl.BlockSpec(memory_space=pl.ANY)] * (2 * PIECES),
            out_specs=[
                pl.BlockSpec((band, nvirt), lambda i, p: (i, 0)),
                pl.BlockSpec((chips, rows, cols), lambda i, p: (0, 0, 0)),
            ],
            scratch_shapes=[
                pltpu.VMEM((nvirt, nvirt), BF16),
                pltpu.VMEM((nvirt, nvirt), BF16),
                pltpu.SemaphoreType.DMA((2 * PIECES,)),
            ],
        ),
        out_shape=[
            jax.ShapeDtypeStruct((nvirt, nvirt), BF16),
            jax.ShapeDtypeStruct((chips, rows, cols), F32),
        ],
        compiler_params=pltpu.CompilerParams(vmem_limit_bytes=LIMIT),
        cost_estimate=pl.CostEstimate(
            flops=2 * rows * cols * chips * nvirt, bytes_accessed=4 * nvirt * nvirt, transcendentals=0
        ),
        name="mix",
    )(place, *own, *other)


def cross_kernel(place, *refs):
    pieces, (partner, weight, out) = refs[: 2 * PIECES], refs[2 * PIECES :]
    width = pieces[0].shape[1]

    @pl.when(place[0] == 0)
    def _():
        total = contract(pieces[0][...], weight[:width, :], 1, 0)
        for i in range(1, 2 * PIECES):
            total += contract(pieces[i][...], weight[i * width : (i + 1) * width, :], 1, 0)
        out[...] = total.astype(BF16)

    @pl.when(place[0] != 0)
    def _():
        out[...] = contract(partner[...], weight[...], 1, 0).astype(BF16)


def cross_columns(place, pieces, partner, weight, j, step):
    rows, nvirt = partner.shape
    width = pieces[0].shape[1]
    block = 256 if rows % 256 == 0 else 128
    return pl.pallas_call(
        cross_kernel,
        grid_spec=pltpu.PrefetchScalarGridSpec(
            num_scalar_prefetch=1,
            grid=(rows // block,),
            in_specs=[pl.BlockSpec((block, width), lambda i, p: (jnp.where(p[0] == 0, i, 0), 0))]
            * (2 * PIECES)
            + [
                pl.BlockSpec((block, nvirt), lambda i, p: (jnp.where(p[0] == 0, 0, i), 0)),
                pl.BlockSpec((nvirt, step), lambda i, p: (0, j)),
            ],
            out_specs=pl.BlockSpec((block, step), lambda i, p: (i, 0)),
        ),
        out_shape=jax.ShapeDtypeStruct((rows, step), BF16),
        compiler_params=pltpu.CompilerParams(vmem_limit_bytes=LIMIT),
        cost_estimate=pl.CostEstimate(
            flops=2 * rows * nvirt * step, bytes_accessed=2 * rows * (nvirt + step), transcendentals=0
        ),
        name="cross_term",
    )(place, *pieces, partner, weight)


def final_kernel(place, partner, weight, kept, arrived, *refs):
    out = refs[-1]
    total = contract(partner[...], weight[...], 1, 0)

    @pl.when(place[0] == 0)
    def _():
        out[0] = (total.astype(BF16).astype(F32) + kept[...].astype(F32)).astype(BF16)

    @pl.when(place[0] != 0)
    def _():
        out[0] = (total + arrived[...].astype(F32)).astype(BF16)


def final_columns(place, partner, weight, kept, arrived, j, step, gamma):
    rows, nvirt = partner.shape
    block = 256 if rows % 256 == 0 else 128
    before = [] if gamma is None else [gamma]
    return pl.pallas_call(
        final_kernel,
        grid_spec=pltpu.PrefetchScalarGridSpec(
            num_scalar_prefetch=1,
            grid=(rows // block,),
            in_specs=[
                pl.BlockSpec((block, nvirt), lambda i, p: (i, 0)),
                pl.BlockSpec((nvirt, step), lambda i, p: (0, j)),
                pl.BlockSpec((block, step), lambda i, p: (jnp.where(p[0] == 0, i, 0), 0)),
                pl.BlockSpec((block, step), lambda i, p: (jnp.where(p[0] == 0, 0, i), 0)),
            ]
            + [pl.BlockSpec(memory_space=pl.ANY)] * len(before),
            out_specs=pl.BlockSpec((1, block, step), lambda i, p: (0, i, j)),
        ),
        out_shape=jax.ShapeDtypeStruct((1, rows, nvirt), BF16),
        input_output_aliases={5: 0} if before else {},
        compiler_params=pltpu.CompilerParams(vmem_limit_bytes=LIMIT),
        cost_estimate=pl.CostEstimate(
            flops=2 * rows * nvirt * step, bytes_accessed=2 * rows * (nvirt + step), transcendentals=0
        ),
        name="local_term",
    )(place, partner, weight, kept, arrived, *before)


def shards(bmat, eps_occ, eps_vir, occ_label):
    count = lax.axis_size("occ")
    slabs = lax.axis_size("aux")
    place = lax.axis_index("occ")
    slab_index = lax.axis_index("aux")
    chips = count // 2
    chip, core = place // 2, place % 2
    first = core == 0
    where = jnp.stack([core, slab_index, chip]).astype(jnp.int32)
    nvirt = eps_vir.shape[0]
    half = nvirt // 2
    width = half // PIECES
    labels = jnp.arange(count, dtype=jnp.int32)
    energy = jnp.sum(
        eps_occ[None, :] * (occ_label[:, None] == labels[None, :]).astype(F32), axis=1
    )
    swap_pairs = [(i, i ^ 1) for i in range(count)]
    next_pairs = [(i, (i + 2) % count) for i in range(count)]
    down_pairs = [(i, i - 1) for i in range(1, count, 2)]
    back_pairs = [(i, (i - 2) % count) for i in range(1, count, 2)]
    inner = (slab_index == 1) | (slab_index == 2)

    def energy_at(row):
        return lax.dynamic_index_in_dim(energy, (row + count) % count, 0, keepdims=False)

    energies = {
        "cross": (energy_at(2 * chip), energy_at(2 * chip - 1)),
        "local": (energy_at(2 * chip + 1), energy_at(2 * chip)),
    }

    mine = bmat[0]
    partner = lax.ppermute(mine, "occ", swap_pairs)
    order = Order(partner)
    incoming, upper = {}, {}

    def ship(j, *others):
        sent = order.step(
            lambda p, m: jnp.where(
                first,
                p[:, j * width : (j + 1) * width],
                m[:, half + j * width : half + (j + 1) * width],
            ),
            partner,
            mine,
        )
        incoming[j] = order.send(sent, "occ", next_pairs, *others)

    ship(0)
    ship(1)
    even = order.step(lambda m, p: jnp.where(first, m, p), mine, partner)
    odd = order.step(lambda m, p: jnp.where(first, p, m), mine, partner)

    def product(kind, j):
        if kind == "cross":
            part = order.step(lambda a, b: contract(a, b, 0, 0).astype(BF16), incoming[j], even)
            if j + 2 < PIECES:
                ship(j + 2)
            upper[j] = order.send(incoming[j], "occ", down_pairs)
            return part
        return order.step(
            lambda a, b: contract(
                lax.dynamic_slice_in_dim(a, core * half + j * width, width, axis=1), b, 0, 0
            ).astype(BF16),
            even,
            odd,
        )

    def scaled(kind, j, mine_sum, other_sum):
        eps_rows = lax.dynamic_slice_in_dim(eps_vir, core * half + j * width, width)
        denom = eps_rows[:, None] + eps_vir[None, :] - energies[kind][0] - energies[kind][1]
        return ((mine_sum.astype(F32) + other_sum.astype(F32)) / denom).astype(BF16)

    own, other = {"cross": [], "local": []}, {"cross": [], "local": []}
    jobs = [("local",0),("cross",0),("cross",1),("cross",2),("local",1),("local",2)]
    n = len(jobs)
    part, inward, summed, across, amp, outward = ({} for _ in range(6))

    def feed(s):
        part[s] = product(*jobs[s])
        inward[s] = order.send(part[s], "aux", [(0, 1), (3, 2)])

    results = {}

    def finish_cross():
        weight, dens = order.step(
            lambda *v: mix(where, v[:PIECES], v[PIECES:], 0, slabs, count), *own["cross"], *other["cross"]
        )
        results["cross_density"] = dens
        kept, arrived = [], []
        pieces = [incoming[j] for j in range(PIECES)] + [upper[j] for j in range(PIECES)]
        step = nvirt // PIECES
        for j in range(PIECES):
            kept.append(
                order.step(lambda w, p, *v: cross_columns(where, v, p, w, j, step), weight, partner, *pieces)
            )
            arrived.append(order.send(kept[j], "occ", back_pairs))
        results["kept"], results["arrived"] = kept, arrived

    done = None
    for s in range(-1, n + 2):
        if s + 1 < n:
            feed(s + 1)
        if done is not None:
            order.last = (order.last, done)
        if 0 <= s < n:
            summed[s] = order.step(
                lambda a, b: (a.astype(F32) + b.astype(F32)).astype(BF16), part[s], inward[s]
            )
        t = s - 1
        if 0 <= t < n:
            amp[t] = order.step(lambda a, b: scaled(*jobs[t], a, b), summed[t], across[t])
        if 0 <= s < n:
            across[s] = order.send(summed[s], "aux", [(1, 2), (2, 1)])
        t = s - 2
        if 0 <= t < n:
            full = order.step(lambda a, b: jnp.where(inner, a, b), amp[t], outward[t])
            kind = jobs[t][0]
            own[kind].append(full)
            done = order.send(full, "occ", swap_pairs)
            other[kind].append(done)
        t = s - 1
        if 0 <= t < n:
            outward[t] = order.send(amp[t], "aux", [(1, 0), (2, 3)])
        if len(own["cross"]) == PIECES and "kept" not in results:
            finish_cross()

    weight, dens = order.step(
        lambda *v: mix(where, v[:PIECES], v[PIECES:], 1, slabs, count), *own["local"], *other["local"]
    )
    total = order.step(lambda a, b: (a + b) * nvirt ** (-0.5), results["cross_density"], dens)
    density = total[0]
    for ahead in range(1, chips):
        pairs = [(i, (i + 2 * ahead) % count) for i in range(count)]
        density = density + order.send(total[ahead].astype(BF16), "occ", pairs).astype(F32)
    gamma = None
    step = nvirt // PIECES
    for j in range(PIECES):
        gamma = order.step(
            lambda p, w, k, a, *g: final_columns(where, p, w, k, a, j, step, *g),
            partner, weight, results["kept"][j], results["arrived"][j], *([None] if gamma is None else [gamma]),
        )
    return gamma, density


def solution(mesh):
    return jax.shard_map(
        shards,
        mesh=mesh,
        in_specs=(P(("grp", "occ"), "aux", None), P("grp"), P("grp"), P("grp")),
        out_specs=(P(("grp", "occ"), "aux", None), P(("grp", "aux"), "occ")),
        check_vma=False,
    )
```

time: 390 us -> 301 us (0.77)
  waiting for transfers between devices: 297 us -> 145 us
  Pallas kernels: 0 us -> 61.1 us
  starting transfers between devices: 8.42 us -> 58.9 us
  matrix products: 37.8 us -> 8.44 us
  local copies, waits for them, and re-layouts: 17.5 us -> 1.52 us
  between operations: 14.2 us -> 1.32 us
  other arithmetic: 14 us -> 21.8 us
    all_to_all x1 -> x0, waiting for transfers between devices: 103 us -> none  [shards(): lax.all_to_all(blocks, 'aux', split_axis=0, concat_axis=0, tiled=True)]
    all_gather x1 -> x0, waiting for transfers between devices: 88.6 us -> none  [shards(): amp_full = lax.all_gather(amp_rows, 'aux', axis=0, tiled=True)]
    ppermute x2 -> x35, waiting for transfers between devices: 78.3 us -> 145 us  [the longest x34 140 us: send(): return lax.ppermute(self.ready(value, *others)[0], axis, pairs)]
    pallas_call x0 -> x8, Pallas kernels: none -> 61.1 us  [the longest x3 24.1 us: final_columns(): pl.pallas_call(final_kernel, grid_spec=pltpu.PrefetchScalarGridSpec(num_s...]
    ppermute x2 -> x35, starting transfers between devices: 3.24 us -> 58.9 us  [the longest x34 58.8 us: send(): return lax.ppermute(self.ready(value, *others)[0], axis, pairs)]
    dot_general x4 -> x6, matrix products: 37.8 us -> 8.44 us  [contract(): lax.dot_general(left, right, (((dim_left,), (dim_right,)), ((), ())), pre...]
    unnamed x3 -> x0, waiting for transfers between devices: 27.2 us -> none
    unnamed x19 -> x14, local copies, waits for them, and re-layouts: 9.22 us -> 0.03 us
  transfers between devices with their start and end apart: 5 -> 35, of which waited for: 5 -> 12; matrix products, arithmetic and copies ran while one was open for 2% -> 9% of each run, Pallas kernels for 0% -> 20%
where the time goes in v2:
time: 301 us; the launch traced here: 298 us
  waiting for transfers between devices  145 us (48%)
  Pallas kernels  61.1 us (20%)
  starting transfers between devices  58.9 us (20%)
  other arithmetic  21.8 us (7%)
  matrix products  8.44 us (3%)
    ppermute x34, waiting for transfers between devices, send(): return lax.ppermute(self.ready(value, *others)[0], axis, pairs)  140 us
    ppermute x34, starting transfers between devices, send(): return lax.ppermute(self.ready(value, *others)[0], axis, pairs)  58.8 us
    pallas_call x3, Pallas kernels, final_columns(): pl.pallas_call(final_kernel, grid_spec=pltpu.PrefetchScalarGridSpec(num_s...  24.1 us
    pallas_call x3, Pallas kernels, cross_columns(): pl.pallas_call(cross_kernel, grid_spec=pltpu.PrefetchScalarGridSpec(num_s...  23.6 us
    pallas_call x2, Pallas kernels, mix(): pl.pallas_call(functools.partial(mix_kernel, nvirt // 2, band, rows, cols...  13.4 us
    convert_element_type x6, other arithmetic, scaled(): return ((mine_sum.astype(F32) + other_sum.astype(F32)) / denom).astype(BF16)  10.2 us
    dot_general x6, matrix products, contract(): lax.dot_general(left, right, (((dim_left,), (dim_right,)), ((), ())), pre...  8.44 us
  transfers between devices with their start and end apart: 35, of which 12 were waited for; matrix products, arithmetic and copies ran while one was open for 9% of the time, Pallas kernels for 20%

profile of v2, /device:TPU:1, one launch (start us, length us, event | category | flops | bytes accessed | tf_op | source)
XLA Modules:
  0.0 298.4 jit_solution(6657675956624471110)
XLA Ops:
  3.1 5.8 %collective-permute-done.refs_6_.partner = bf16[1536,1536]{1,0:T(8,128)(2,1)} collective-permute-done((bf16[1536,1536]{1,0:T(8,128)(2,1)}, bf16[1536,1536]{1,0:T(8,128)(2,1)}, u32[]{:S(2)}, u32[]{:S(2)}) %collective-permute-start) | collective-permute-done | bytes 4718624 | tf_op jit(solution)/shard_map/ppermute | solution.py:223
  19.6 3.4 %collective-permute-start.1 = (bf16[256,1536]{1,0:T(8,128)(2,1)S(1)}, bf16[256,1536]{1,0:T(8,128)(2,1)S(1)}, u32[]{:S(2)}, u32[]{:S(2)}) collective-permute-start(bf16[256,1536]{1,0:T(8,128)(2,1)S(1)} %convolution_convert_fusion.5), channel_id=1, source_target_pairs={{0,1},{3,2},{4,5},{7,6},{8,9},{11,10},{12,13},{15,14},{16,17},{19,... | collective-permute-start | bytes 2359304 | tf_op jit(solution)/shard_map/ppermute | solution.py:35
  23.0 26.2 %collective-permute-done.2.refs_0_ = bf16[1536,256]{1,0:T(8,128)(2,1)S(1)} collective-permute-done((bf16[1536,256]{1,0:T(8,128)(2,1)S(1)}, bf16[1536,256]{1,0:T(8,128)(2,1)S(1)}, u32[]{:S(2)}, u32[]{:S(2)}) %collective-permute-start.2) | collective-permute-done | bytes 786464 | tf_op jit(solution)/shard_map/ppermute | solution.py:35
  51.8 3.2 %collective-permute-start.4 = (bf16[256,1536]{1,0:T(8,128)(2,1)S(1)}, bf16[256,1536]{1,0:T(8,128)(2,1)S(1)}, u32[]{:S(2)}, u32[]{:S(2)}) collective-permute-start(bf16[256,1536]{1,0:T(8,128)(2,1)S(1)} %convolution_convert_fusion.4), channel_id=1, source_target_pairs={{0,1},{3,2},{4,5},{7,6},{8,9},{11,10},{12,13},{15,14},{16,17},{19,... | collective-permute-start | bytes 2359304 | tf_op jit(solution)/shard_map/ppermute | solution.py:35
  58.6 3.8 %collective-permute-start.8 = (bf16[256,1536]{1,0:T(8,128)(2,1)S(1)}, bf16[256,1536]{1,0:T(8,128)(2,1)S(1)}, u32[]{:S(2)}, u32[]{:S(2)}) collective-permute-start(bf16[256,1536]{1,0:T(8,128)(2,1)S(1)} %convolution_convert_fusion.3), channel_id=1, source_target_pairs={{0,1},{3,2},{4,5},{7,6},{8,9},{11,10},{12,13},{15,14},{16,17},{19,... | collective-permute-start | bytes 2359304 | tf_op jit(solution)/shard_map/ppermute | solution.py:35
  62.4 8.2 %collective-permute-done.4 = bf16[256,1536]{1,0:T(8,128)(2,1)S(1)} collective-permute-done((bf16[256,1536]{1,0:T(8,128)(2,1)S(1)}, bf16[256,1536]{1,0:T(8,128)(2,1)S(1)}, u32[]{:S(2)}, u32[]{:S(2)}) %collective-permute-start.4) | collective-permute-done | bytes 786464 | tf_op jit(solution)/shard_map/ppermute | solution.py:35
  74.7 12.7 %collective-permute-done.8 = bf16[256,1536]{1,0:T(8,128)(2,1)S(1)} collective-permute-done((bf16[256,1536]{1,0:T(8,128)(2,1)S(1)}, bf16[256,1536]{1,0:T(8,128)(2,1)S(1)}, u32[]{:S(2)}, u32[]{:S(2)}) %collective-permute-start.8) | collective-permute-done | bytes 786464 | tf_op jit(solution)/shard_map/ppermute | solution.py:35
  87.4 4.1 %collective-permute-start.13 = (bf16[256,1536]{1,0:T(8,128)(2,1)S(1)}, bf16[256,1536]{1,0:T(8,128)(2,1)S(1)}, u32[]{:S(2)}, u32[]{:S(2)}) collective-permute-start(bf16[256,1536]{1,0:T(8,128)(2,1)S(1)} %convolution_convert_fusion.2), channel_id=1, source_target_pairs={{0,1},{3,2},{4,5},{7,6},{8,9},{11,10},{12,13},{15,14},{16,17},{19,... | collective-permute-start | bytes 2359304 | tf_op jit(solution)/shard_map/ppermute | solution.py:35
  94.8 15.3 %collective-permute-done.6 = bf16[256,1536]{1,0:T(8,128)(2,1)S(1)} collective-permute-done((bf16[256,1536]{1,0:T(8,128)(2,1)S(1)}, bf16[256,1536]{1,0:T(8,128)(2,1)S(1)}, u32[]{:S(2)}, u32[]{:S(2)}) %collective-permute-start.6) | collective-permute-done | bytes 786464 | tf_op jit(solution)/shard_map/ppermute | solution.py:35
  110.2 3.4 %collective-permute-start.14 = (bf16[256,1536]{1,0:T(8,128)(2,1)S(1)}, bf16[256,1536]{1,0:T(8,128)(2,1)S(1)}, u32[]{:S(2)}, u32[]{:S(2)}) collective-permute-start(bf16[256,1536]{1,0:T(8,128)(2,1)S(1)} %broadcast_select_fusion.7.refs_0_), channel_id=1, source_target_pairs={{0,4},{4,0},{8,12},{12,8},{1,5},{5,1},{9,13},{13,9},{2,6},{6,2},{1... | collective-permute-start | bytes 2359304 | tf_op jit(solution)/shard_map/ppermute | solution.py:35
  115.7 3.7 %collective-permute-start.10 = (bf16[256,1536]{1,0:T(8,128)(2,1)S(1)}, bf16[256,1536]{1,0:T(8,128)(2,1)S(1)}, u32[]{:S(2)}, u32[]{:S(2)}) collective-permute-start(bf16[256,1536]{1,0:T(8,128)(2,1)S(1)} %convolution_convert_fusion.1), channel_id=1, source_target_pairs={{0,1},{3,2},{4,5},{7,6},{8,9},{11,10},{12,13},{15,14},{16,17},{19,... | collective-permute-start | bytes 2359304 | tf_op jit(solution)/shard_map/ppermute | solution.py:35
  122.7 17.1 %collective-permute-done.11 = bf16[256,1536]{1,0:T(8,128)(2,1)S(1)} collective-permute-done((bf16[256,1536]{1,0:T(8,128)(2,1)S(1)}, bf16[256,1536]{1,0:T(8,128)(2,1)S(1)}, u32[]{:S(2)}, u32[]{:S(2)}) %collective-permute-start.11) | collective-permute-done | bytes 786464 | tf_op jit(solution)/shard_map/ppermute | solution.py:35
  149.6 17.0 %collective-permute-done.19 = bf16[256,1536]{1,0:T(8,128)(2,1)S(1)} collective-permute-done((bf16[256,1536]{1,0:T(8,128)(2,1)S(1)}, bf16[256,1536]{1,0:T(8,128)(2,1)S(1)}, u32[]{:S(2)}, u32[]{:S(2)}) %collective-permute-start.19) | collective-permute-done | bytes 786464 | tf_op jit(solution)/shard_map/ppermute | solution.py:35
  172.1 17.9 %collective-permute-done.21 = bf16[256,1536]{1,0:T(8,128)(2,1)S(1)} collective-permute-done((bf16[256,1536]{1,0:T(8,128)(2,1)S(1)}, bf16[256,1536]{1,0:T(8,128)(2,1)S(1)}, u32[]{:S(2)}, u32[]{:S(2)}) %collective-permute-start.21) | collective-permute-done | bytes 786464 | tf_op jit(solution)/shard_map/ppermute | solution.py:35
  197.7 6.6 %mix.2 = (bf16[1536,1536]{1,0:T(8,128)(2,1)}, f32[2,384,384]{2,1,0:T(8,128)S(1)}) custom-call(s32[3]{0:T(128)S(1)} %pad_add_fusion.place, bf16[256,1536]{1,0:T(8,128)(2,1)S(1)} %broadcast_select_fusion.6.refs_0_, bf16[256,1536]{1,0:T(8,128)(2,1)S(1)} %broadcast_select_fusion.5.refs_1_, bf16[256,1536]{1,0:T(8,128)(2,1)S(1)} %broadcast_select_fusion.4.refs_2_, ...), custom_call_target="tpu_custom_call" | custom-call | flops 905969664 | bytes 9437184 | tf_op jit(solution)/shard_map/mix/pallas_call | solution.py:81
  204.3 7.9 %cross_term.3.kept = bf16[1536,512]{1,0:T(8,128)(2,1)} custom-call(s32[3]{0:T(128)S(1)} %pad_add_fusion.place, bf16[1536,256]{1,0:T(8,128)(2,1)S(1)} %collective-permute-done.2.refs_0_, bf16[1536,256]{1,0:T(8,128)(2,1)S(1)} %collective-permute-done.5.refs_1_, bf16[1536,256]{1,0:T(8,128)(2,1)S(1)} %collective-permute-done.9.refs_2_, ...), custom_call_target="tpu_custom_call" | custom-call | flops 2415919104 | bytes 6291456 | tf_op jit(solution)/shard_map/cross_term/pallas_call | solution.py:129
  212.2 7.9 %cross_term.4.kept = bf16[1536,512]{1,0:T(8,128)(2,1)} custom-call(s32[3]{0:T(128)S(1)} %pad_add_fusion.place, bf16[1536,256]{1,0:T(8,128)(2,1)S(1)} %collective-permute-done.2.refs_0_, bf16[1536,256]{1,0:T(8,128)(2,1)S(1)} %collective-permute-done.5.refs_1_, bf16[1536,256]{1,0:T(8,128)(2,1)S(1)} %collective-permute-done.9.refs_2_, ...), custom_call_target="tpu_custom_call" | custom-call | flops 2415919104 | bytes 6291456 | tf_op jit(solution)/shard_map/cross_term/pallas_call | solution.py:129
  220.1 7.8 %cross_term.5.kept = bf16[1536,512]{1,0:T(8,128)(2,1)} custom-call(s32[3]{0:T(128)S(1)} %pad_add_fusion.place, bf16[1536,256]{1,0:T(8,128)(2,1)S(1)} %collective-permute-done.2.refs_0_, bf16[1536,256]{1,0:T(8,128)(2,1)S(1)} %collective-permute-done.5.refs_1_, bf16[1536,256]{1,0:T(8,128)(2,1)S(1)} %collective-permute-done.9.refs_2_, ...), custom_call_target="tpu_custom_call" | custom-call | flops 2415919104 | bytes 6291456 | tf_op jit(solution)/shard_map/cross_term/pallas_call | solution.py:129
  234.5 13.6 %collective-permute-done.28 = bf16[256,1536]{1,0:T(8,128)(2,1)S(1)} collective-permute-done((bf16[256,1536]{1,0:T(8,128)(2,1)S(1)}, bf16[256,1536]{1,0:T(8,128)(2,1)S(1)}, u32[]{:S(2)}, u32[]{:S(2)}) %collective-permute-start.28) | collective-permute-done | bytes 786464 | tf_op jit(solution)/shard_map/ppermute | solution.py:35
  253.8 6.7 %mix.3 = (bf16[1536,1536]{1,0:T(8,128)(2,1)}, f32[2,384,384]{2,1,0:T(8,128)S(1)}) custom-call(s32[3]{0:T(128)S(1)} %pad_add_fusion.place, bf16[256,1536]{1,0:T(8,128)(2,1)S(1)} %broadcast_select_fusion.7.refs_0_, bf16[256,1536]{1,0:T(8,128)(2,1)S(1)} %broadcast_select_fusion.3.refs_1_, bf16[256,1536]{1,0:T(8,128)(2,1)S(1)} %broadcast_select_fusion.2.refs_2_, ...), custom_call_target="tpu_custom_call" | custom-call | flops 905969664 | bytes 9437184 | tf_op jit(solution)/shard_map/mix/pallas_call | solution.py:81
  261.9 8.0 %local_term.3.refs_0_ = bf16[1,1536,1536]{2,1,0:T(8,128)(2,1)} custom-call(s32[3]{0:T(128)S(1)} %pad_add_fusion.place, bf16[1536,1536]{1,0:T(8,128)(2,1)} %collective-permute-done.refs_6_.partner, bf16[1536,1536]{1,0:T(8,128)(2,1)} %get-tuple-element.293.weight, bf16[1536,512]{1,0:T(8,128)(2,1)S(1)} %copy-done.2, ...), custom_call_target="tpu_custom_call" | custom-call | flops 2415919104 | bytes 6291456 | tf_op jit(solution)/shard_map/local_term/pallas_call | solution.py:168
  272.6 8.0 %local_term.4.refs_0_ = bf16[1,1536,1536]{2,1,0:T(8,128)(2,1)} custom-call(s32[3]{0:T(128)S(1)} %pad_add_fusion.place, bf16[1536,1536]{1,0:T(8,128)(2,1)} %collective-permute-done.refs_6_.partner, bf16[1536,1536]{1,0:T(8,128)(2,1)} %get-tuple-element.293.weight, bf16[1536,512]{1,0:T(8,128)(2,1)S(1)} %copy-done.1, ...), custom_call_target="tpu_custom_call", output_to_operand_aliasing={{}: (5, {})} | custom-call | flops 2415919104 | bytes 6291456 | tf_op jit(solution)/shard_map/local_term/pallas_call | solution.py:168
  280.7 8.8 %collective-permute-done.31.arrived = bf16[1536,512]{1,0:T(8,128)(2,1)S(1)} collective-permute-done((bf16[1536,512]{1,0:T(8,128)(2,1)S(1)}, bf16[1536,512]{1,0:T(8,128)(2,1)S(1)}, u32[]{:S(2)}, u32[]{:S(2)}) %collective-permute-start.31) | collective-permute-done | bytes 1572896 | tf_op jit(solution)/shard_map/ppermute | solution.py:35
  289.5 8.0 %local_term.5 = bf16[1,1536,1536]{2,1,0:T(8,128)(2,1)} custom-call(s32[3]{0:T(128)S(1)} %pad_add_fusion.place, bf16[1536,1536]{1,0:T(8,128)(2,1)} %collective-permute-done.refs_6_.partner, bf16[1536,1536]{1,0:T(8,128)(2,1)} %get-tuple-element.293.weight, bf16[1536,512]{1,0:T(8,128)(2,1)S(1)} %copy-done, ...), custom_call_target="tpu_custom_call", output_to_operand_aliasing={{}: (5, {})} | custom-call | flops 2415919104 | bytes 6291456 | tf_op jit(solution)/shard_map/local_term/pallas_call | solution.py:168
  (104 shorter events, 71.9 us)
Async XLA Ops:
  12.3 44.1 %collective-permute-start.5 = (bf16[1536,256]{1,0:T(8,128)(2,1)S(1)}, bf16[1536,256]{1,0:T(8,128)(2,1)S(1)}, u32[]{:S(2)}, u32[]{:S(2)}) collective-permute-start(bf16[1536,256]{1,0:T(8,128)(2,1)S(1)} %slice_select_fusion.1), channel_id=1, source_target_pairs={{0,8},{4,12},{8,0},{12,4},{1,9},{5,13},{9,1},{13,5},{2,10},{6,14},... | collective-permute-start | bytes 2359304 | tf_op jit(solution)/shard_map/ppermute | solution.py:35
  14.7 34.5 %collective-permute-start.2 = (bf16[1536,256]{1,0:T(8,128)(2,1)S(1)}, bf16[1536,256]{1,0:T(8,128)(2,1)S(1)}, u32[]{:S(2)}, u32[]{:S(2)}) collective-permute-start(bf16[1536,256]{1,0:T(8,128)(2,1)S(1)} %slice_select_fusion.2), channel_id=1, source_target_pairs={{0,8},{4,12},{8,0},{12,4},{1,9},{5,13},{9,1},{13,5},{2,10},{6,14},... | collective-permute-start | bytes 2359304 | tf_op jit(solution)/shard_map/ppermute | solution.py:35
  19.6 36.7 %collective-permute-start.1 = (bf16[256,1536]{1,0:T(8,128)(2,1)S(1)}, bf16[256,1536]{1,0:T(8,128)(2,1)S(1)}, u32[]{:S(2)}, u32[]{:S(2)}) collective-permute-start(bf16[256,1536]{1,0:T(8,128)(2,1)S(1)} %convolution_convert_fusion.5), channel_id=1, source_target_pairs={{0,1},{3,2},{4,5},{7,6},{8,9},{11,10},{12,13},{15,14},{16,17},{19,... | collective-permute-start | bytes 2359304 | tf_op jit(solution)/shard_map/ppermute | solution.py:35
  51.8 18.8 %collective-permute-start.4 = (bf16[256,1536]{1,0:T(8,128)(2,1)S(1)}, bf16[256,1536]{1,0:T(8,128)(2,1)S(1)}, u32[]{:S(2)}, u32[]{:S(2)}) collective-permute-start(bf16[256,1536]{1,0:T(8,128)(2,1)S(1)} %convolution_convert_fusion.4), channel_id=1, source_target_pairs={{0,1},{3,2},{4,5},{7,6},{8,9},{11,10},{12,13},{15,14},{16,17},{19,... | collective-permute-start | bytes 2359304 | tf_op jit(solution)/shard_map/ppermute | solution.py:35
  55.0 17.6 %collective-permute-start.9 = (bf16[1536,256]{1,0:T(8,128)(2,1)S(1)}, bf16[1536,256]{1,0:T(8,128)(2,1)S(1)}, u32[]{:S(2)}, u32[]{:S(2)}) collective-permute-start(bf16[1536,256]{1,0:T(8,128)(2,1)S(1)} %slice_select_fusion), channel_id=1, source_target_pairs={{0,8},{4,12},{8,0},{12,4},{1,9},{5,13},{9,1},{13,5},{2,10},{6,14},... | collective-permute-start | bytes 2359304 | tf_op jit(solution)/shard_map/ppermute | solution.py:35
  56.5 14.3 %collective-permute-start.3 = (bf16[256,1536]{1,0:T(8,128)(2,1)S(1)}, bf16[256,1536]{1,0:T(8,128)(2,1)S(1)}, u32[]{:S(2)}, u32[]{:S(2)}) collective-permute-start(bf16[256,1536]{1,0:T(8,128)(2,1)S(1)} %add_convert_fusion.5), channel_id=1, source_target_pairs={{1,2},{2,1},{5,6},{6,5},{9,10},{10,9},{13,14},{14,13},{17,18},{18,... | collective-permute-start | bytes 2359304 | tf_op jit(solution)/shard_map/ppermute | solution.py:35
  58.6 28.8 %collective-permute-start.8 = (bf16[256,1536]{1,0:T(8,128)(2,1)S(1)}, bf16[256,1536]{1,0:T(8,128)(2,1)S(1)}, u32[]{:S(2)}, u32[]{:S(2)}) collective-permute-start(bf16[256,1536]{1,0:T(8,128)(2,1)S(1)} %convolution_convert_fusion.3), channel_id=1, source_target_pairs={{0,1},{3,2},{4,5},{7,6},{8,9},{11,10},{12,13},{15,14},{16,17},{19,... | collective-permute-start | bytes 2359304 | tf_op jit(solution)/shard_map/ppermute | solution.py:35
  72.6 20.5 %collective-permute-start.7 = (bf16[256,1536]{1,0:T(8,128)(2,1)S(1)}, bf16[256,1536]{1,0:T(8,128)(2,1)S(1)}, u32[]{:S(2)}, u32[]{:S(2)}) collective-permute-start(bf16[256,1536]{1,0:T(8,128)(2,1)S(1)} %add_convert_fusion.4), channel_id=1, source_target_pairs={{1,2},{2,1},{5,6},{6,5},{9,10},{10,9},{13,14},{14,13},{17,18},{18,... | collective-permute-start | bytes 2359304 | tf_op jit(solution)/shard_map/ppermute | solution.py:35
  87.4 33.3 %collective-permute-start.13 = (bf16[256,1536]{1,0:T(8,128)(2,1)S(1)}, bf16[256,1536]{1,0:T(8,128)(2,1)S(1)}, u32[]{:S(2)}, u32[]{:S(2)}) collective-permute-start(bf16[256,1536]{1,0:T(8,128)(2,1)S(1)} %convolution_convert_fusion.2), channel_id=1, source_target_pairs={{0,1},{3,2},{4,5},{7,6},{8,9},{11,10},{12,13},{15,14},{16,17},{19,... | collective-permute-start | bytes 2359304 | tf_op jit(solution)/shard_map/ppermute | solution.py:35
  91.6 18.5 %collective-permute-start.6 = (bf16[256,1536]{1,0:T(8,128)(2,1)S(1)}, bf16[256,1536]{1,0:T(8,128)(2,1)S(1)}, u32[]{:S(2)}, u32[]{:S(2)}) collective-permute-start(bf16[256,1536]{1,0:T(8,128)(2,1)S(1)} %fusion.17), channel_id=1, source_target_pairs={{1,0},{2,3},{5,4},{6,7},{9,8},{10,11},{13,12},{14,15},{17,16},{18,... | collective-permute-start | bytes 2359304 | tf_op jit(solution)/shard_map/ppermute | solution.py:35
  115.7 31.9 %collective-permute-start.10 = (bf16[256,1536]{1,0:T(8,128)(2,1)S(1)}, bf16[256,1536]{1,0:T(8,128)(2,1)S(1)}, u32[]{:S(2)}, u32[]{:S(2)}) collective-permute-start(bf16[256,1536]{1,0:T(8,128)(2,1)S(1)} %convolution_convert_fusion.1), channel_id=1, source_target_pairs={{0,1},{3,2},{4,5},{7,6},{8,9},{11,10},{12,13},{15,14},{16,17},{19,... | collective-permute-start | bytes 2359304 | tf_op jit(solution)/shard_map/ppermute | solution.py:35
  119.4 20.4 %collective-permute-start.11 = (bf16[256,1536]{1,0:T(8,128)(2,1)S(1)}, bf16[256,1536]{1,0:T(8,128)(2,1)S(1)}, u32[]{:S(2)}, u32[]{:S(2)}) collective-permute-start(bf16[256,1536]{1,0:T(8,128)(2,1)S(1)} %fusion.16), channel_id=1, source_target_pairs={{1,0},{2,3},{5,4},{6,7},{9,8},{10,11},{13,12},{14,15},{17,16},{18,... | collective-permute-start | bytes 2359304 | tf_op jit(solution)/shard_map/ppermute | solution.py:35
  143.6 26.6 %collective-permute-start.18 = (bf16[256,1536]{1,0:T(8,128)(2,1)S(1)}, bf16[256,1536]{1,0:T(8,128)(2,1)S(1)}, u32[]{:S(2)}, u32[]{:S(2)}) collective-permute-start(bf16[256,1536]{1,0:T(8,128)(2,1)S(1)} %convolution_convert_fusion), channel_id=1, source_target_pairs={{0,1},{3,2},{4,5},{7,6},{8,9},{11,10},{12,13},{15,14},{16,17},{19,... | collective-permute-start | bytes 2359304 | tf_op jit(solution)/shard_map/ppermute | solution.py:35
  146.2 20.4 %collective-permute-start.19 = (bf16[256,1536]{1,0:T(8,128)(2,1)S(1)}, bf16[256,1536]{1,0:T(8,128)(2,1)S(1)}, u32[]{:S(2)}, u32[]{:S(2)}) collective-permute-start(bf16[256,1536]{1,0:T(8,128)(2,1)S(1)} %fusion.15), channel_id=1, source_target_pairs={{1,0},{2,3},{5,4},{6,7},{9,8},{10,11},{13,12},{14,15},{17,16},{18,... | collective-permute-start | bytes 2359304 | tf_op jit(solution)/shard_map/ppermute | solution.py:35
  168.9 21.0 %collective-permute-start.21 = (bf16[256,1536]{1,0:T(8,128)(2,1)S(1)}, bf16[256,1536]{1,0:T(8,128)(2,1)S(1)}, u32[]{:S(2)}, u32[]{:S(2)}) collective-permute-start(bf16[256,1536]{1,0:T(8,128)(2,1)S(1)} %fusion.13), channel_id=1, source_target_pairs={{1,0},{2,3},{5,4},{6,7},{9,8},{10,11},{13,12},{14,15},{17,16},{18,... | collective-permute-start | bytes 2359304 | tf_op jit(solution)/shard_map/ppermute | solution.py:35
  190.9 13.4 %collective-permute-start.25 = (bf16[1536,256]{1,0:T(8,128)(2,1)S(1)}, bf16[1536,256]{1,0:T(8,128)(2,1)S(1)}, u32[]{:S(2)}, u32[]{:S(2)}) collective-permute-start(bf16[1536,256]{1,0:T(8,128)(2,1)S(1)} %collective-permute-done.2.refs_0_), channel_id=1, source_target_pairs={{4,0},{12,8},{5,1},{13,9},{6,2},{14,10},{7,3},{15,11},{20,16},{28,... | collective-permute-start | bytes 2359304 | tf_op jit(solution)/shard_map/ppermute | solution.py:35
  195.6 32.3 %collective-permute-start.23 = (bf16[256,1536]{1,0:T(8,128)(2,1)S(1)}, bf16[256,1536]{1,0:T(8,128)(2,1)S(1)}, u32[]{:S(2)}, u32[]{:S(2)}) collective-permute-start(bf16[256,1536]{1,0:T(8,128)(2,1)S(1)} %add_convert_fusion), channel_id=1, source_target_pairs={{1,2},{2,1},{5,6},{6,5},{9,10},{10,9},{13,14},{14,13},{17,18},{18,... | collective-permute-start | bytes 2359304 | tf_op jit(solution)/shard_map/ppermute | solution.py:35
  196.4 33.3 %collective-permute-start.22 = (bf16[256,1536]{1,0:T(8,128)(2,1)S(1)}, bf16[256,1536]{1,0:T(8,128)(2,1)S(1)}, u32[]{:S(2)}, u32[]{:S(2)}) collective-permute-start(bf16[256,1536]{1,0:T(8,128)(2,1)S(1)} %fusion.14), channel_id=1, source_target_pairs={{1,0},{2,3},{5,4},{6,7},{9,8},{10,11},{13,12},{14,15},{17,16},{18,... | collective-permute-start | bytes 2359304 | tf_op jit(solution)/shard_map/ppermute | solution.py:35
  229.8 18.3 %collective-permute-start.28 = (bf16[256,1536]{1,0:T(8,128)(2,1)S(1)}, bf16[256,1536]{1,0:T(8,128)(2,1)S(1)}, u32[]{:S(2)}, u32[]{:S(2)}) collective-permute-start(bf16[256,1536]{1,0:T(8,128)(2,1)S(1)} %fusion.12), channel_id=1, source_target_pairs={{1,0},{2,3},{5,4},{6,7},{9,8},{10,11},{13,12},{14,15},{17,16},{18,... | collective-permute-start | bytes 2359304 | tf_op jit(solution)/shard_map/ppermute | solution.py:35
  231.3 16.7 %collective-permute-start.29 = (bf16[256,1536]{1,0:T(8,128)(2,1)S(1)}, bf16[256,1536]{1,0:T(8,128)(2,1)S(1)}, u32[]{:S(2)}, u32[]{:S(2)}) collective-permute-start(bf16[256,1536]{1,0:T(8,128)(2,1)S(1)} %broadcast_select_fusion.3.refs_1_), channel_id=1, source_target_pairs={{0,4},{4,0},{8,12},{12,8},{1,5},{5,1},{9,13},{13,9},{2,6},{6,2},{1... | collective-permute-start | bytes 2359304 | tf_op jit(solution)/shard_map/ppermute | solution.py:35
  231.4 30.5 %collective-permute-start.33 = (bf16[1536,512]{1,0:T(8,128)(2,1)S(1)}, bf16[1536,512]{1,0:T(8,128)(2,1)S(1)}, u32[]{:S(2)}, u32[]{:S(2)}) collective-permute-start(bf16[1536,512]{1,0:T(8,128)(2,1)S(1)} %copy-done.2), channel_id=1, source_target_pairs={{4,12},{12,4},{5,13},{13,5},{6,14},{14,6},{7,15},{15,7},{20,28},{2... | collective-permute-start | bytes 4718600 | tf_op jit(solution)/shard_map/ppermute | solution.py:35
  248.2 24.4 %collective-permute-start.32 = (bf16[1536,512]{1,0:T(8,128)(2,1)S(1)}, bf16[1536,512]{1,0:T(8,128)(2,1)S(1)}, u32[]{:S(2)}, u32[]{:S(2)}) collective-permute-start(bf16[1536,512]{1,0:T(8,128)(2,1)S(1)} %copy-done.1), channel_id=1, source_target_pairs={{4,12},{12,4},{5,13},{13,5},{6,14},{14,6},{7,15},{15,7},{20,28},{2... | collective-permute-start | bytes 4718600 | tf_op jit(solution)/shard_map/ppermute | solution.py:35
  251.3 38.2 %collective-permute-start.31 = (bf16[1536,512]{1,0:T(8,128)(2,1)S(1)}, bf16[1536,512]{1,0:T(8,128)(2,1)S(1)}, u32[]{:S(2)}, u32[]{:S(2)}) collective-permute-start(bf16[1536,512]{1,0:T(8,128)(2,1)S(1)} %copy-done), channel_id=1, source_target_pairs={{4,12},{12,4},{5,13},{13,5},{6,14},{14,6},{7,15},{15,7},{20,28},{2... | collective-permute-start | bytes 4718600 | tf_op jit(solution)/shard_map/ppermute | solution.py:35
  260.7 36.8 %collective-permute-start.34 = (bf16[384,384]{1,0:T(8,128)(2,1)S(1)}, bf16[384,384]{1,0:T(8,128)(2,1)S(1)}, u32[]{:S(2)}, u32[]{:S(2)}) collective-permute-start(bf16[384,384]{1,0:T(8,128)(2,1)S(1)} %fusion.22), channel_id=1, source_target_pairs={{0,8},{4,12},{8,0},{12,4},{1,9},{5,13},{9,1},{13,5},{2,10},{6,14},... | collective-permute-start | bytes 884744 | tf_op jit(solution)/shard_map/ppermute | solution.py:35
  (18 other events, 167.4 us)

commit v3 on v2

v3 whole, which is shorter than its diff:
```python
import functools

import jax
import jax.numpy as jnp
from jax import lax
from jax.experimental import pallas as pl
from jax.experimental.pallas import tpu as pltpu
from jax.sharding import PartitionSpec as P

F32 = jnp.float32
BF16 = jnp.bfloat16
PIECES = 3
LIMIT = 24 * 1024 * 1024
LIGHT = pl.CostEstimate(flops=10**9, bytes_accessed=10**6, transcendentals=0)

TINY = pl.CostEstimate(flops=10**7, bytes_accessed=10**4, transcendentals=0)


def contract(left, right, dim_left, dim_right):
    return lax.dot_general(
        left, right, (((dim_left,), (dim_right,)), ((), ())), preferred_element_type=F32
    )


class Order:
    def __init__(self, first):
        self.last = first

    def ready(self, *values):
        return lax.optimization_barrier((*values, self.last))[:-1]

    def step(self, work, *values):
        result = work(*self.ready(*values))
        self.last = result
        return result

    def send(self, value, axis, pairs, *others):
        return lax.ppermute(self.ready(value, *others)[0], axis, pairs)


def product_kernel(place, left, right, out):
    out[...] = contract(left[...], right[...], 0, 0).astype(BF16)


def product_rows(place, left, right, width, j):
    rows, nvirt = right.shape
    whole_left = left.shape[1] == width
    step = nvirt // 3
    return pl.pallas_call(
        product_kernel,
        grid_spec=pltpu.PrefetchScalarGridSpec(
            num_scalar_prefetch=1,
            grid=(nvirt // step,),
            in_specs=[
                pl.BlockSpec(
                    (rows, width), lambda i, p: (0, 0 if whole_left else p[0] * PIECES + j)
                ),
                pl.BlockSpec((rows, step), lambda i, p: (0, i)),
            ],
            out_specs=pl.BlockSpec((width, step), lambda i, p: (0, i)),
        ),
        out_shape=jax.ShapeDtypeStruct((width, nvirt), BF16),
        compiler_params=pltpu.CompilerParams(vmem_limit_bytes=LIMIT),
        cost_estimate=LIGHT,
        name="slab_product",
    )(place, left, right)


def add_kernel(left, right, out):
    out[...] = (left[...].astype(F32) + right[...].astype(F32)).astype(BF16)


def added(left, right):
    return pl.pallas_call(
        add_kernel,
        out_shape=jax.ShapeDtypeStruct(left.shape, BF16),
        compiler_params=pltpu.CompilerParams(vmem_limit_bytes=LIMIT),
        cost_estimate=LIGHT,
        name="half_sum",
    )(left, right)


def pick_kernel(hop, slabs, place, left, right, *refs):
    out = refs[-1]
    outer = (place[1] == hop) | (place[1] == slabs - 1 - hop)

    @pl.when(outer)
    def _():
        out[...] = right[...]

    @pl.when(jnp.logical_not(outer))
    def _():
        out[...] = left[...]


def picked(place, left, right, hop, slabs, start, rows, before):
    width, nvirt = left.shape
    return pl.pallas_call(
        functools.partial(pick_kernel, hop, slabs),
        grid=(1,),
        in_specs=[pl.BlockSpec(memory_space=pltpu.SMEM)]
        + [pl.BlockSpec((width, nvirt), lambda i: (0, 0))] * 2
        + [pl.BlockSpec(memory_space=pl.ANY)] * len(before),
        out_specs=pl.BlockSpec((width, nvirt), lambda i: (start // width, 0)),
        out_shape=jax.ShapeDtypeStruct((rows, nvirt), BF16),
        input_output_aliases={3: 0} if before else {},
        compiler_params=pltpu.CompilerParams(vmem_limit_bytes=LIMIT),
        cost_estimate=LIGHT,
        name="amp_of_slab",
    )(place, left, right, *before)


def amp_kernel(place, energy, eps_rows, eps_cols, left, right, out):
    denom = eps_rows[...] + eps_cols[...] - energy[0] - energy[1]
    out[...] = ((left[...].astype(F32) + right[...].astype(F32)) / denom).astype(BF16)


def amplitude(place, energy, eps_rows, eps_cols, left, right, start, half):
    width, nvirt = left.shape
    return pl.pallas_call(
        amp_kernel,
        grid_spec=pltpu.PrefetchScalarGridSpec(
            num_scalar_prefetch=1,
            grid=(1,),
            in_specs=[
                pl.BlockSpec(memory_space=pltpu.SMEM),
                pl.BlockSpec((width, 1), lambda i, p: (p[0] * (half // width) + start // width, 0)),
                pl.BlockSpec((1, nvirt), lambda i, p: (0, 0)),
                pl.BlockSpec((width, nvirt), lambda i, p: (0, 0)),
                pl.BlockSpec((width, nvirt), lambda i, p: (0, 0)),
            ],
            out_specs=pl.BlockSpec((width, nvirt), lambda i, p: (0, 0)),
        ),
        out_shape=jax.ShapeDtypeStruct(left.shape, BF16),
        compiler_params=pltpu.CompilerParams(vmem_limit_bytes=LIMIT),
        cost_estimate=LIGHT,
        name="amplitude",
    )(place, energy, eps_rows, eps_cols, left, right)


def mix_kernel(half, band, rows, cols, straight_core, place, *refs):
    own, other, mix, dens, amp_t, amp, sems = refs
    core, slab, chip = place[0], place[1], place[2]
    nvirt = 2 * half
    step = pl.program_id(0)

    @pl.when(step == 0)
    def _():
        copies = []
        for i, (piece, side) in enumerate(((own, core), (other, 1 - core))):
            start = pl.multiple_of(side * half, 128)
            copies.append(pltpu.make_async_copy(piece, amp_t.at[pl.ds(start, half), :], sems.at[i]))
        for copy in copies:
            copy.start()
        for copy in copies:
            copy.wait()

    straight = core == straight_core
    here = jnp.where(straight, 2.0, -1.0).astype(F32)
    there = jnp.where(straight, -1.0, 2.0).astype(F32)
    start = pl.multiple_of(step * band, band)
    for j in range(nvirt // band):
        tile = amp_t[pl.ds(start, band), j * band : (j + 1) * band].astype(F32)
        turned = amp_t[j * band : (j + 1) * band, pl.ds(start, band)].astype(F32).T
        amp[pl.ds(start, band), j * band : (j + 1) * band] = turned.astype(BF16)
        mix[:, j * band : (j + 1) * band] = (here * tile + there * turned).astype(BF16)

    @pl.when(step == nvirt // band - 1)
    def _():
        chips = dens.shape[0]
        left = amp[pl.ds(pl.multiple_of(slab * rows, rows), rows), :]
        for ahead in range(chips):
            at = pl.multiple_of((2 * lax.rem(chip + ahead, chips) + core) * cols, cols)
            tilde = 2.0 * amp[pl.ds(at, cols), :].astype(F32) - amp_t[pl.ds(at, cols), :].astype(F32)
            dens[ahead] = contract(left, tilde.astype(BF16), 1, 1)


def mix(place, own, other, straight_core, slabs, count):
    nvirt = own.shape[1]
    rows, cols, chips = nvirt // slabs, nvirt // count, count // 2
    band = 256
    return pl.pallas_call(
        functools.partial(mix_kernel, nvirt // 2, band, rows, cols, straight_core),
        grid_spec=pltpu.PrefetchScalarGridSpec(
            num_scalar_prefetch=1,
            grid=(nvirt // band,),
            in_specs=[pl.BlockSpec(memory_space=pl.ANY)] * 2,
            out_specs=[
                pl.BlockSpec((band, nvirt), lambda i, p: (i, 0)),
                pl.BlockSpec((chips, rows, cols), lambda i, p: (0, 0, 0)),
            ],
            scratch_shapes=[
                pltpu.VMEM((nvirt, nvirt), BF16),
                pltpu.VMEM((nvirt, nvirt), BF16),
                pltpu.SemaphoreType.DMA((2,)),
            ],
        ),
        out_shape=[
            jax.ShapeDtypeStruct((nvirt, nvirt), BF16),
            jax.ShapeDtypeStruct((chips, rows, cols), F32),
        ],
        compiler_params=pltpu.CompilerParams(vmem_limit_bytes=LIMIT),
        cost_estimate=TINY,
        name="mix",
    )(place, own, other)


def block_of(rows):
    return 768 if rows % 768 == 0 else 128


def cross_kernel(place, lower, upper, partner, weight, out):
    half = lower.shape[1]

    @pl.when(place[0] == 0)
    def _():
        total = contract(lower[...], weight[:half, :], 1, 0)
        out[...] = (total + contract(upper[...], weight[half:, :], 1, 0)).astype(BF16)

    @pl.when(place[0] != 0)
    def _():
        out[...] = contract(partner[...], weight[...], 1, 0).astype(BF16)


def cross_columns(place, lower, upper, partner, weight, start, step):
    rows, nvirt = partner.shape
    block = block_of(rows)
    return pl.pallas_call(
        cross_kernel,
        grid_spec=pltpu.PrefetchScalarGridSpec(
            num_scalar_prefetch=1,
            grid=(rows // block,),
            in_specs=[
                pl.BlockSpec((block, nvirt // 2), lambda i, p: (jnp.where(p[0] == 0, i, 0), 0)),
                pl.BlockSpec((block, nvirt // 2), lambda i, p: (jnp.where(p[0] == 0, i, 0), 0)),
                pl.BlockSpec((block, nvirt), lambda i, p: (jnp.where(p[0] == 0, 0, i), 0)),
                pl.BlockSpec((nvirt, step), lambda i, p: (0, start // step)),
            ],
            out_specs=pl.BlockSpec((block, step), lambda i, p: (i, 0)),
        ),
        out_shape=jax.ShapeDtypeStruct((rows, step), BF16),
        compiler_params=pltpu.CompilerParams(vmem_limit_bytes=LIMIT),
        cost_estimate=TINY,
        name="cross_term",
    )(place, lower, upper, partner, weight)


def final_kernel(place, partner, weight, kept, arrived, *refs):
    out = refs[-1]
    total = contract(partner[...], weight[...], 1, 0)

    @pl.when(place[0] == 0)
    def _():
        out[0] = (total.astype(BF16).astype(F32) + kept[...].astype(F32)).astype(BF16)

    @pl.when(place[0] != 0)
    def _():
        out[0] = (total + arrived[...].astype(F32)).astype(BF16)


def final_columns(place, partner, weight, kept, arrived, start, step, gamma=None):
    rows, nvirt = partner.shape
    block = block_of(rows)
    before = [] if gamma is None else [gamma]
    return pl.pallas_call(
        final_kernel,
        grid_spec=pltpu.PrefetchScalarGridSpec(
            num_scalar_prefetch=1,
            grid=(rows // block,),
            in_specs=[
                pl.BlockSpec((block, nvirt), lambda i, p: (i, 0)),
                pl.BlockSpec((nvirt, step), lambda i, p: (0, start // step)),
                pl.BlockSpec((block, step), lambda i, p: (jnp.where(p[0] == 0, i, 0), 0)),
                pl.BlockSpec((block, step), lambda i, p: (jnp.where(p[0] == 0, 0, i), 0)),
            ]
            + [pl.BlockSpec(memory_space=pl.ANY)] * len(before),
            out_specs=pl.BlockSpec((1, block, step), lambda i, p: (0, i, start // step)),
        ),
        out_shape=jax.ShapeDtypeStruct((1, rows, nvirt), BF16),
        input_output_aliases={5: 0} if before else {},
        compiler_params=pltpu.CompilerParams(vmem_limit_bytes=LIMIT),
        cost_estimate=TINY,
        name="local_term",
    )(place, partner, weight, kept, arrived, *before)


def shards(bmat, eps_occ, eps_vir, occ_label):
    count = lax.axis_size("occ")
    slabs = lax.axis_size("aux")
    place = lax.axis_index("occ")
    slab_index = lax.axis_index("aux")
    chips = count // 2
    chip, core = place // 2, place % 2
    first = core == 0
    where = jnp.stack([core, slab_index, chip]).astype(jnp.int32)
    nvirt = eps_vir.shape[0]
    half = nvirt // 2
    width = half // PIECES
    labels = jnp.arange(count, dtype=jnp.int32)
    energy = jnp.sum(
        eps_occ[None, :] * (occ_label[:, None] == labels[None, :]).astype(F32), axis=1
    )
    swap_pairs = [(i, i ^ 1) for i in range(count)]
    next_pairs = [(i, (i + 2) % count) for i in range(count)]
    down_pairs = [(i, i - 1) for i in range(1, count, 2)]
    back_pairs = [(i, (i - 2) % count) for i in range(1, count, 2)]

    def energy_at(row):
        return lax.dynamic_index_in_dim(energy, (row + count) % count, 0, keepdims=False)

    energies = {
        "cross": jnp.stack([energy_at(2 * chip), energy_at(2 * chip - 1)]),
        "local": jnp.stack([energy_at(2 * chip + 1), energy_at(2 * chip)]),
    }
    eps_rows, eps_cols = eps_vir.reshape(nvirt, 1), eps_vir.reshape(1, nvirt)

    mine = bmat[0]
    partner = lax.ppermute(mine, "occ", swap_pairs)
    order = Order(partner)
    incoming = {}

    def ship(j, *others):
        sent = order.step(
            lambda p, m: jnp.where(
                first,
                p[:, j * width : (j + 1) * width],
                m[:, half + j * width : half + (j + 1) * width],
            ),
            partner,
            mine,
        )
        incoming[j] = order.send(sent, "occ", next_pairs, *others)

    ship(0)
    odd = order.step(lambda m, p: jnp.where(first, p, m), mine, partner)
    even = order.step(lambda m, p: jnp.where(first, m, p), mine, partner)
    ship(1)

    def product(kind, j):
        if kind == "cross":
            part = order.step(lambda a, b: product_rows(where, a, b, width, j), incoming[j], even)
            if j + 2 < PIECES:
                ship(j + 2)
            return part
        return order.step(lambda a, b: product_rows(where, a, b, width, j), even, odd)

    def scaled(kind, j, mine_sum, other_sum):
        return amplitude(
            where, energies[kind], eps_rows, eps_cols, mine_sum, other_sum, j * width, half
        )

    jobs = [("local", 0)] + [("cross", j) for j in range(PIECES)] + [("local", j) for j in range(1, PIECES)]
    n = len(jobs)
    left = {kind: sum(job[0] == kind for job in jobs) for kind in ("cross", "local")}
    own = {"cross": [], "local": []}
    part, inward, summed, across, amp, outward = ({} for _ in range(6))

    def settle(*values):
        order.last = (order.last, *values)

    hops = slabs // 2 - 1
    middle = [(hops, hops + 1), (hops + 1, hops)]

    def towards_middle(hop):
        return [(hop, hop + 1), (slabs - 1 - hop, slabs - 2 - hop)]

    def towards_ends(hop):
        return [(b, a) for a, b in towards_middle(hop)]

    def feed(s):
        value = product(*jobs[s])
        for hop in range(hops - 1):
            value = order.step(added, value, order.send(value, "aux", towards_middle(hop)))
        part[s] = value
        inward[s] = order.send(value, "aux", towards_middle(hops - 1))

    def pass_across(s):
        if 0 <= s < n:
            summed[s] = order.step(added, part[s], inward[s])
            across[s] = order.send(summed[s], "aux", middle)

    def pass_out(s):
        if 0 <= s < n:
            value = order.step(lambda a, b: scaled(*jobs[s], a, b), summed[s], across[s])
            for hop in reversed(range(1, hops)):
                value = order.step(
                    lambda a, b: picked(where, a, b, hop, slabs, 0, width, ()),
                    value, order.send(value, "aux", towards_ends(hop)),
                )
            amp[s] = value
            outward[s] = order.send(value, "aux", towards_ends(0))

    def collect(s):
        if 0 <= s < n:
            kind, j = jobs[s]
            own[kind] = [
                order.step(
                    lambda a, b, *c: picked(where, a, b, 0, slabs, j * width, half, c), amp[s], outward[s], *own[kind]
                )
            ]
            left[kind] -= 1

    third = nvirt // 3
    spans = [(0, 2 * third), (2 * third, third)]
    kept, arrived = [], []

    def cross_term():
        j = len(kept)
        if j < len(spans) and cross_mix:
            kept.append(
                order.step(
                    lambda w, p, a, b: cross_columns(where, a, b, p, w, *spans[j]),
                    cross_mix[0], partner, received, upper,
                )
            )
            arrived.append(order.send(kept[j], "occ", back_pairs))

    cross_mix = []
    received = upper = None
    for s in range(-1, n + 2):
        if s + 1 < n:
            feed(s + 1)
        pass_across(s)
        if s < n:
            pass_out(s - 1)
            collect(s - 2)
        elif s == n:
            collect(s - 2)
            pass_out(s - 1)
            cross_term()
        else:
            settle(arrived[0])
            collect(s - 2)
        if not left["cross"] and not cross_mix:
            other = order.send(own["cross"][0], "occ", swap_pairs)
            received = order.step(lambda *v: jnp.concatenate(v, axis=1), *incoming.values())
            upper = order.send(received, "occ", down_pairs)
            cross_mix = order.step(lambda a, b: mix(where, a, b, 0, slabs, count), own["cross"][0], other)
            cross_term()
    other = order.send(own["local"][0], "occ", swap_pairs)
    weight, dens = order.step(lambda a, b: mix(where, a, b, 1, slabs, count), own["local"][0], other)
    total = order.step(lambda a, b: (a + b) * nvirt ** (-0.5), cross_mix[1], dens)
    density = total[0]
    for ahead in range(1, chips):
        pairs = [(i, (i + 2 * ahead) % count) for i in range(count)]
        density = density + order.send(total[ahead].astype(BF16), "occ", pairs).astype(F32)
    gamma = None
    for j in range(len(spans)):
        gamma = order.step(
            lambda p, w, k, a, *g: final_columns(where, p, w, k, a, *spans[j], *g),
            partner, weight, kept[j], arrived[j], *([] if gamma is None else [gamma]),
        )
    return gamma, density


def solution(mesh):
    return jax.shard_map(
        shards,
        mesh=mesh,
        in_specs=(P(("grp", "occ"), "aux", None), P("grp"), P("grp"), P("grp")),
        out_specs=(P(("grp", "occ"), "aux", None), P(("grp", "aux"), "occ")),
        check_vma=False,
    )
```

time: 301 us -> 245 us (0.81)
  waiting for transfers between devices: 145 us -> 99.1 us
  Pallas kernels: 61.1 us -> 71.3 us
  matrix products: 8.44 us -> 0 us
  starting transfers between devices: 58.9 us -> 50.5 us
  other arithmetic: 21.8 us -> 17.5 us
    ppermute x34 -> x27, waiting for transfers between devices: 140 us -> 91 us  [send(): return lax.ppermute(self.ready(value, *others)[0], axis, pairs)]
    pallas_call x0 -> x24, Pallas kernels: none -> 33.9 us  [the longest x6 16.6 us: product_rows(): pl.pallas_call(product_kernel, grid_spec=pltpu.PrefetchScalarGridSpec(num...]
    convert_element_type x12 -> x0, other arithmetic: 11.4 us -> none  [the longest x6 10.2 us: scaled(): return ((mine_sum.astype(F32) + other_sum.astype(F32)) / denom).astype(BF16)]
    pallas_call x3 -> x2, Pallas kernels: 23.6 us -> 12.5 us  [cross_columns(): pl.pallas_call(cross_kernel, grid_spec=pltpu.PrefetchScalarGridSpec(num_s...]
    pallas_call x3 -> x2, Pallas kernels: 24.1 us -> 15.4 us  [final_columns(): pl.pallas_call(final_kernel, grid_spec=pltpu.PrefetchScalarGridSpec(num_s...]
    dot_general x6 -> x0, matrix products: 8.44 us -> none  [contract(): lax.dot_general(left, right, (((dim_left,), (dim_right,)), ((), ())), pre...]
    ppermute x34 -> x27, starting transfers between devices: 58.8 us -> 50.4 us  [send(): return lax.ppermute(self.ready(value, *others)[0], axis, pairs)]
    pallas_call x2, Pallas kernels: 13.4 us -> 9.52 us  [mix(): pl.pallas_call(functools.partial(mix_kernel, nvirt // 2, band, rows, cols...]
  transfers between devices with their start and end apart: 35 -> 28, of which waited for: 12 -> 15; matrix products, arithmetic and copies ran while one was open for 9% -> 4% of each run, Pallas kernels for 20% -> 26%
where the time goes in v3:
time: 245 us; the launch traced here: 244 us
  waiting for transfers between devices  99.1 us (40%)
  Pallas kernels  71.3 us (29%)
  starting transfers between devices  50.5 us (21%)
  other arithmetic  17.5 us (7%)
  local copies, waits for them, and re-layouts  4.38 us (2%)
    ppermute x27, waiting for transfers between devices, send(): return lax.ppermute(self.ready(value, *others)[0], axis, pairs)  91 us
    ppermute x27, starting transfers between devices, send(): return lax.ppermute(self.ready(value, *others)[0], axis, pairs)  50.4 us
    pallas_call x6, Pallas kernels, product_rows(): pl.pallas_call(product_kernel, grid_spec=pltpu.PrefetchScalarGridSpec(num...  16.6 us
    pallas_call x2, Pallas kernels, final_columns(): pl.pallas_call(final_kernel, grid_spec=pltpu.PrefetchScalarGridSpec(num_s...  15.4 us
    pallas_call x2, Pallas kernels, cross_columns(): pl.pallas_call(cross_kernel, grid_spec=pltpu.PrefetchScalarGridSpec(num_s...  12.5 us
    pallas_call x6, Pallas kernels, amplitude(): pl.pallas_call(amp_kernel, grid_spec=pltpu.PrefetchScalarGridSpec(num_sca...  10.2 us
    pallas_call x2, Pallas kernels, mix(): pl.pallas_call(functools.partial(mix_kernel, nvirt // 2, band, rows, cols...  9.52 us
    ppermute x1, waiting for transfers between devices, shards(): partner = lax.ppermute(mine, 'occ', swap_pairs)  8.12 us
  transfers between devices with their start and end apart: 28, of which 15 were waited for; matrix products, arithmetic and copies ran while one was open for 4% of the time, Pallas kernels for 26%

profile of v3, /device:TPU:1, one launch (start us, length us, event | category | flops | bytes accessed | tf_op | source)
XLA Modules:
  0.0 244.0 jit_solution(945775349734606407)
XLA Ops:
  0.8 8.1 %collective-permute-done.partner = bf16[1536,1536]{1,0:T(8,128)(2,1)} collective-permute-done((bf16[1536,1536]{1,0:T(8,128)(2,1)}, bf16[1536,1536]{1,0:T(8,128)(2,1)}, u32[]{:S(2)}, u32[]{:S(2)}) %collective-permute-start) | collective-permute-done | bytes 4718624 | tf_op jit(solution)/shard_map/ppermute | solution.py:318
  10.6 3.0 %broadcast_select_fusion.1.right = bf16[1536,1536]{1,0:T(8,128)(2,1)S(1)} fusion(bf16[1536,1536]{1,0:T(8,128)(2,1)} %collective-permute-done.partner, bf16[1536,1536]{1,0:T(8,128)(2,1)} %bitcast.14, pred[]{:T(512)S(6)} %eq.25), kind=kLoop, calls=%fused_computation.1 | loop fusion | flops 2359296 | bytes 14155777 | tf_op jit(solution)/shard_map/jit(_where)/select_n | solution.py:335
  13.6 4.5 %broadcast_select_fusion.left.right = bf16[1536,1536]{1,0:T(8,128)(2,1)S(1)} fusion(bf16[1536,1536]{1,0:T(8,128)(2,1)S(1)} %bitcast.17, bf16[1536,1536]{1,0:T(8,128)(2,1)} %collective-permute-done.partner, pred[]{:T(512)S(6)} %eq.25), kind=kLoop, calls=%fused_computation | loop fusion | flops 2359296 | bytes 14155777 | tf_op jit(solution)/shard_map/jit(_where)/select_n | solution.py:336
  25.5 3.6 %collective-permute-start.4 = (bf16[256,1536]{1,0:T(8,128)(2,1)S(1)}, bf16[256,1536]{1,0:T(8,128)(2,1)S(1)}, u32[]{:S(2)}, u32[]{:S(2)}) collective-permute-start(bf16[256,1536]{1,0:T(8,128)(2,1)S(1)} %slab_product.6.left), channel_id=1, source_target_pairs={{0,1},{3,2},{4,5},{7,6},{8,9},{11,10},{12,13},{15,14},{16,17},{19,... | collective-permute-start | bytes 2359304 | tf_op jit(solution)/shard_map/ppermute | solution.py:38
  29.7 9.0 %collective-permute-done.1.left = bf16[1536,256]{1,0:T(8,128)(2,1)S(1)} collective-permute-done((bf16[1536,256]{1,0:T(8,128)(2,1)S(1)}, bf16[1536,256]{1,0:T(8,128)(2,1)S(1)}, u32[]{:S(2)}, u32[]{:S(2)}) %collective-permute-start.1) | collective-permute-done | bytes 786464 | tf_op jit(solution)/shard_map/ppermute | solution.py:38
  43.8 5.0 %collective-permute-start.2 = (bf16[256,1536]{1,0:T(8,128)(2,1)S(1)}, bf16[256,1536]{1,0:T(8,128)(2,1)}, u32[]{:S(2)}, u32[]{:S(2)}) collective-permute-start(bf16[256,1536]{1,0:T(8,128)(2,1)S(1)} %slab_product.7.left), channel_id=1, source_target_pairs={{0,1},{3,2},{4,5},{7,6},{8,9},{11,10},{12,13},{15,14},{16,17},{19,... | collective-permute-start | bytes 2359304 | tf_op jit(solution)/shard_map/ppermute | solution.py:38
  74.1 6.7 %collective-permute-start.11 = (bf16[256,1536]{1,0:T(8,128)(2,1)S(1)}, bf16[256,1536]{1,0:T(8,128)(2,1)S(1)}, u32[]{:S(2)}, u32[]{:S(2)}) collective-permute-start(bf16[256,1536]{1,0:T(8,128)(2,1)S(1)} %slab_product.9.left), channel_id=1, source_target_pairs={{0,1},{3,2},{4,5},{7,6},{8,9},{11,10},{12,13},{15,14},{16,17},{19,... | collective-permute-start | bytes 2359304 | tf_op jit(solution)/shard_map/ppermute | solution.py:38
  84.8 7.0 %collective-permute-done.12.right = bf16[256,1536]{1,0:T(8,128)(2,1)S(1)} collective-permute-done((bf16[256,1536]{1,0:T(8,128)(2,1)S(1)}, bf16[256,1536]{1,0:T(8,128)(2,1)S(1)}, u32[]{:S(2)}, u32[]{:S(2)}) %collective-permute-start.12) | collective-permute-done | bytes 786464 | tf_op jit(solution)/shard_map/ppermute | solution.py:38
  96.6 4.1 %collective-permute-start.16 = (bf16[256,1536]{1,0:T(8,128)(2,1)S(1)}, bf16[256,1536]{1,0:T(8,128)(2,1)S(1)}, u32[]{:S(2)}, u32[]{:S(2)}) collective-permute-start(bf16[256,1536]{1,0:T(8,128)(2,1)S(1)} %slab_product.10.left), channel_id=1, source_target_pairs={{0,1},{3,2},{4,5},{7,6},{8,9},{11,10},{12,13},{15,14},{16,17},{19,... | collective-permute-start | bytes 2359304 | tf_op jit(solution)/shard_map/ppermute | solution.py:38
  104.5 8.8 %collective-permute-done.9.right = bf16[256,1536]{1,0:T(8,128)(2,1)S(1)} collective-permute-done((bf16[256,1536]{1,0:T(8,128)(2,1)S(1)}, bf16[256,1536]{1,0:T(8,128)(2,1)S(1)}, u32[]{:S(2)}, u32[]{:S(2)}) %collective-permute-start.9) | collective-permute-done | bytes 786464 | tf_op jit(solution)/shard_map/ppermute | solution.py:38
  113.9 2.8 %slab_product.11.left = bf16[256,1536]{1,0:T(8,128)(2,1)S(1)} custom-call(s32[3]{0:T(128)S(1)} %pad_add_fusion.place, bf16[1536,1536]{1,0:T(8,128)(2,1)S(1)} %copy-done.2, bf16[1536,1536]{1,0:T(8,128)(2,1)S(1)} %bitcast.11), custom_call_target="tpu_custom_call" | custom-call | flops 1000000000 | bytes 1000000 | tf_op jit(solution)/shard_map/slab_product/pallas_call | solution.py:49
  117.4 4.1 %collective-permute-start.13 = (bf16[256,1536]{1,0:T(8,128)(2,1)S(1)}, bf16[256,1536]{1,0:T(8,128)(2,1)S(1)}, u32[]{:S(2)}, u32[]{:S(2)}) collective-permute-start(bf16[256,1536]{1,0:T(8,128)(2,1)S(1)} %slab_product.11.left), channel_id=1, source_target_pairs={{0,1},{3,2},{4,5},{7,6},{8,9},{11,10},{12,13},{15,14},{16,17},{19,... | collective-permute-start | bytes 2359304 | tf_op jit(solution)/shard_map/ppermute | solution.py:38
  125.3 3.7 %collective-permute-done.14.right = bf16[256,1536]{1,0:T(8,128)(2,1)S(1)} collective-permute-done((bf16[256,1536]{1,0:T(8,128)(2,1)S(1)}, bf16[256,1536]{1,0:T(8,128)(2,1)S(1)}, u32[]{:S(2)}, u32[]{:S(2)}) %collective-permute-start.14) | collective-permute-done | bytes 786464 | tf_op jit(solution)/shard_map/ppermute | solution.py:38
  129.6 8.9 %collective-permute-done.13.right = bf16[256,1536]{1,0:T(8,128)(2,1)S(1)} collective-permute-done((bf16[256,1536]{1,0:T(8,128)(2,1)S(1)}, bf16[256,1536]{1,0:T(8,128)(2,1)S(1)}, u32[]{:S(2)}, u32[]{:S(2)}) %collective-permute-start.13) | collective-permute-done | bytes 786464 | tf_op jit(solution)/shard_map/ppermute | solution.py:38
  140.3 5.9 %collective-permute-done.20.right = bf16[256,1536]{1,0:T(8,128)(2,1)S(1)} collective-permute-done((bf16[256,1536]{1,0:T(8,128)(2,1)S(1)}, bf16[256,1536]{1,0:T(8,128)(2,1)S(1)}, u32[]{:S(2)}, u32[]{:S(2)}) %collective-permute-start.20) | collective-permute-done | bytes 786464 | tf_op jit(solution)/shard_map/ppermute | solution.py:38
  151.6 4.8 %mix.2 = (bf16[1536,1536]{1,0:T(8,128)(2,1)S(1)}, f32[2,384,384]{2,1,0:T(8,128)S(1)}) custom-call(s32[3]{0:T(128)S(1)} %pad_add_fusion.place, bf16[768,1536]{1,0:T(8,128)(2,1)S(1)} %amp_of_slab.9.refs_0_, bf16[768,1536]{1,0:T(8,128)(2,1)S(1)} %collective-permute-done.21.refs_1_), custom_call_target="tpu_custom_call" | custom-call | flops 10000000 | bytes 10000 | tf_op jit(solution)/shard_map/mix/pallas_call | solution.py:182
  156.4 7.5 %cross_term.2.kept = bf16[1536,1024]{1,0:T(8,128)(2,1)S(1)} custom-call(s32[3]{0:T(128)S(1)} %pad_add_fusion.place, bf16[1536,768]{1,0:T(8,128)(2,1)S(1)} %constant_dynamic-update-slice_fusion.lower, bf16[1536,768]{1,0:T(8,128)(2,1)S(1)} %collective-permute-done.22.upper, bf16[1536,1536]{1,0:T(8,128)(2,1)} %collective-permute-done.partner, ...), custom_call_target="tpu_custom_call" | custom-call | flops 10000000 | bytes 10000 | tf_op jit(solution)/shard_map/cross_term/pallas_call | solution.py:228
  167.8 19.1 %collective-permute-done.19.right = bf16[256,1536]{1,0:T(8,128)(2,1)S(1)} collective-permute-done((bf16[256,1536]{1,0:T(8,128)(2,1)S(1)}, bf16[256,1536]{1,0:T(8,128)(2,1)S(1)}, u32[]{:S(2)}, u32[]{:S(2)}) %collective-permute-start.19) | collective-permute-done | bytes 786464 | tf_op jit(solution)/shard_map/ppermute | solution.py:38
  190.4 5.0 %cross_term.3.kept = bf16[1536,512]{1,0:T(8,128)(2,1)S(1)} custom-call(s32[3]{0:T(128)S(1)} %pad_add_fusion.place, bf16[1536,768]{1,0:T(8,128)(2,1)S(1)} %constant_dynamic-update-slice_fusion.lower, bf16[1536,768]{1,0:T(8,128)(2,1)S(1)} %collective-permute-done.22.upper, bf16[1536,1536]{1,0:T(8,128)(2,1)} %collective-permute-done.partner, ...), custom_call_target="tpu_custom_call" | custom-call | flops 10000000 | bytes 10000 | tf_op jit(solution)/shard_map/cross_term/pallas_call | solution.py:228
  195.5 15.4 %collective-permute-done.23.right = bf16[256,1536]{1,0:T(8,128)(2,1)S(1)} collective-permute-done((bf16[256,1536]{1,0:T(8,128)(2,1)S(1)}, bf16[256,1536]{1,0:T(8,128)(2,1)S(1)}, u32[]{:S(2)}, u32[]{:S(2)}) %collective-permute-start.23) | collective-permute-done | bytes 786464 | tf_op jit(solution)/shard_map/ppermute | solution.py:38
  216.7 4.8 %mix.3 = (bf16[1536,1536]{1,0:T(8,128)(2,1)S(1)}, f32[2,384,384]{2,1,0:T(8,128)S(1)}) custom-call(s32[3]{0:T(128)S(1)} %pad_add_fusion.place, bf16[768,1536]{1,0:T(8,128)(2,1)S(1)} %amp_of_slab.11.refs_0_, bf16[768,1536]{1,0:T(8,128)(2,1)S(1)} %collective-permute-done.25.refs_1_), custom_call_target="tpu_custom_call" | custom-call | flops 10000000 | bytes 10000 | tf_op jit(solution)/shard_map/mix/pallas_call | solution.py:182
  221.7 9.2 %local_term.2.refs_0_ = bf16[1,1536,1536]{2,1,0:T(8,128)(2,1)} custom-call(s32[3]{0:T(128)S(1)} %pad_add_fusion.place, bf16[1536,1536]{1,0:T(8,128)(2,1)} %collective-permute-done.partner, bf16[1536,1536]{1,0:T(8,128)(2,1)S(1)} %get-tuple-element.235.weight, bf16[1536,1024]{1,0:T(8,128)(2,1)S(1)} %cross_term.2.kept, ...), custom_call_target="tpu_custom_call" | custom-call | flops 10000000 | bytes 10000 | tf_op jit(solution)/shard_map/local_term/pallas_call | solution.py:265
  230.9 5.9 %collective-permute-done.26.arrived = bf16[1536,512]{1,0:T(8,128)(2,1)S(1)} collective-permute-done((bf16[1536,512]{1,0:T(8,128)(2,1)S(1)}, bf16[1536,512]{1,0:T(8,128)(2,1)S(1)}, u32[]{:S(2)}, u32[]{:S(2)}) %collective-permute-start.26) | collective-permute-done | bytes 1572896 | tf_op jit(solution)/shard_map/ppermute | solution.py:38
  236.9 6.2 %local_term.3 = bf16[1,1536,1536]{2,1,0:T(8,128)(2,1)} custom-call(s32[3]{0:T(128)S(1)} %pad_add_fusion.place, bf16[1536,1536]{1,0:T(8,128)(2,1)} %collective-permute-done.partner, bf16[1536,1536]{1,0:T(8,128)(2,1)S(1)} %get-tuple-element.235.weight, bf16[1536,512]{1,0:T(8,128)(2,1)S(1)} %cross_term.3.kept, ...), custom_call_target="tpu_custom_call", output_to_operand_aliasing={{}: (5, {})} | custom-call | flops 10000000 | bytes 10000 | tf_op jit(solution)/shard_map/local_term/pallas_call | solution.py:265
  (106 shorter events, 79.8 us)
Async XLA Ops:
  18.1 20.6 %collective-permute-start.1 = (bf16[1536,256]{1,0:T(8,128)(2,1)S(1)}, bf16[1536,256]{1,0:T(8,128)(2,1)S(1)}, u32[]{:S(2)}, u32[]{:S(2)}) collective-permute-start(bf16[1536,256]{1,0:T(8,128)(2,1)S(1)} %slice_select_fusion.2), channel_id=1, source_target_pairs={{0,8},{4,12},{8,0},{12,4},{1,9},{5,13},{9,1},{13,5},{2,10},{6,14},... | collective-permute-start | bytes 2359304 | tf_op jit(solution)/shard_map/ppermute | solution.py:38
  25.5 18.2 %collective-permute-start.4 = (bf16[256,1536]{1,0:T(8,128)(2,1)S(1)}, bf16[256,1536]{1,0:T(8,128)(2,1)S(1)}, u32[]{:S(2)}, u32[]{:S(2)}) collective-permute-start(bf16[256,1536]{1,0:T(8,128)(2,1)S(1)} %slab_product.6.left), channel_id=1, source_target_pairs={{0,1},{3,2},{4,5},{7,6},{8,9},{11,10},{12,13},{15,14},{16,17},{19,... | collective-permute-start | bytes 2359304 | tf_op jit(solution)/shard_map/ppermute | solution.py:38
  29.1 26.2 %collective-permute-start.3 = (bf16[1536,256]{1,0:T(8,128)(2,1)}, bf16[1536,256]{1,0:T(8,128)(2,1)S(1)}, u32[]{:S(2)}, u32[]{:S(2)}) collective-permute-start(bf16[1536,256]{1,0:T(8,128)(2,1)} %slice_select_fusion.1), channel_id=1, source_target_pairs={{0,8},{4,12},{8,0},{12,4},{1,9},{5,13},{9,1},{13,5},{2,10},{6,14},... | collective-permute-start | bytes 2359304 | tf_op jit(solution)/shard_map/ppermute | solution.py:38
  43.8 21.5 %collective-permute-start.2 = (bf16[256,1536]{1,0:T(8,128)(2,1)S(1)}, bf16[256,1536]{1,0:T(8,128)(2,1)}, u32[]{:S(2)}, u32[]{:S(2)}) collective-permute-start(bf16[256,1536]{1,0:T(8,128)(2,1)S(1)} %slab_product.7.left), channel_id=1, source_target_pairs={{0,1},{3,2},{4,5},{7,6},{8,9},{11,10},{12,13},{15,14},{16,17},{19,... | collective-permute-start | bytes 2359304 | tf_op jit(solution)/shard_map/ppermute | solution.py:38
  49.8 16.9 %collective-permute-start.8 = (bf16[256,1536]{1,0:T(8,128)(2,1)}, bf16[256,1536]{1,0:T(8,128)(2,1)}, u32[]{:S(2)}, u32[]{:S(2)}) collective-permute-start(bf16[256,1536]{1,0:T(8,128)(2,1)} %half_sum.6.left), channel_id=1, source_target_pairs={{1,2},{2,1},{5,6},{6,5},{9,10},{10,9},{13,14},{14,13},{17,18},{18,... | collective-permute-start | bytes 2359304 | tf_op jit(solution)/shard_map/ppermute | solution.py:38
  51.4 19.9 %collective-permute-start.7 = (bf16[1536,256]{1,0:T(8,128)(2,1)}, bf16[1536,256]{1,0:T(8,128)(2,1)S(1)}, u32[]{:S(2)}, u32[]{:S(2)}) collective-permute-start(bf16[1536,256]{1,0:T(8,128)(2,1)} %slice_select_fusion), channel_id=1, source_target_pairs={{0,8},{4,12},{8,0},{12,4},{1,9},{5,13},{9,1},{13,5},{2,10},{6,14},... | collective-permute-start | bytes 2359304 | tf_op jit(solution)/shard_map/ppermute | solution.py:38
  60.4 21.8 %collective-permute-start.6 = (bf16[256,1536]{1,0:T(8,128)(2,1)S(1)}, bf16[256,1536]{1,0:T(8,128)(2,1)S(1)}, u32[]{:S(2)}, u32[]{:S(2)}) collective-permute-start(bf16[256,1536]{1,0:T(8,128)(2,1)S(1)} %slab_product.8.left), channel_id=1, source_target_pairs={{0,1},{3,2},{4,5},{7,6},{8,9},{11,10},{12,13},{15,14},{16,17},{19,... | collective-permute-start | bytes 2359304 | tf_op jit(solution)/shard_map/ppermute | solution.py:38
  66.7 16.5 %collective-permute-start.5 = (bf16[256,1536]{1,0:T(8,128)(2,1)S(1)}, bf16[256,1536]{1,0:T(8,128)(2,1)S(1)}, u32[]{:S(2)}, u32[]{:S(2)}) collective-permute-start(bf16[256,1536]{1,0:T(8,128)(2,1)S(1)} %half_sum.7.left), channel_id=1, source_target_pairs={{1,2},{2,1},{5,6},{6,5},{9,10},{10,9},{13,14},{14,13},{17,18},{18,... | collective-permute-start | bytes 2359304 | tf_op jit(solution)/shard_map/ppermute | solution.py:38
  70.0 21.8 %collective-permute-start.12 = (bf16[256,1536]{1,0:T(8,128)(2,1)S(1)}, bf16[256,1536]{1,0:T(8,128)(2,1)S(1)}, u32[]{:S(2)}, u32[]{:S(2)}) collective-permute-start(bf16[256,1536]{1,0:T(8,128)(2,1)S(1)} %amplitude.6.left), channel_id=1, source_target_pairs={{1,0},{2,3},{5,4},{6,7},{9,8},{10,11},{13,12},{14,15},{17,16},{18,... | collective-permute-start | bytes 2359304 | tf_op jit(solution)/shard_map/ppermute | solution.py:38
  74.1 26.6 %collective-permute-start.11 = (bf16[256,1536]{1,0:T(8,128)(2,1)S(1)}, bf16[256,1536]{1,0:T(8,128)(2,1)S(1)}, u32[]{:S(2)}, u32[]{:S(2)}) collective-permute-start(bf16[256,1536]{1,0:T(8,128)(2,1)S(1)} %slab_product.9.left), channel_id=1, source_target_pairs={{0,1},{3,2},{4,5},{7,6},{8,9},{11,10},{12,13},{15,14},{16,17},{19,... | collective-permute-start | bytes 2359304 | tf_op jit(solution)/shard_map/ppermute | solution.py:38
  82.4 19.2 %collective-permute-start.10 = (bf16[256,1536]{1,0:T(8,128)(2,1)S(1)}, bf16[256,1536]{1,0:T(8,128)(2,1)S(1)}, u32[]{:S(2)}, u32[]{:S(2)}) collective-permute-start(bf16[256,1536]{1,0:T(8,128)(2,1)S(1)} %half_sum.8.left), channel_id=1, source_target_pairs={{1,2},{2,1},{5,6},{6,5},{9,10},{10,9},{13,14},{14,13},{17,18},{18,... | collective-permute-start | bytes 2359304 | tf_op jit(solution)/shard_map/ppermute | solution.py:38
  91.8 21.4 %collective-permute-start.9 = (bf16[256,1536]{1,0:T(8,128)(2,1)S(1)}, bf16[256,1536]{1,0:T(8,128)(2,1)S(1)}, u32[]{:S(2)}, u32[]{:S(2)}) collective-permute-start(bf16[256,1536]{1,0:T(8,128)(2,1)S(1)} %amplitude.7.left), channel_id=1, source_target_pairs={{1,0},{2,3},{5,4},{6,7},{9,8},{10,11},{13,12},{14,15},{17,16},{18,... | collective-permute-start | bytes 2359304 | tf_op jit(solution)/shard_map/ppermute | solution.py:38
  96.6 20.8 %collective-permute-start.16 = (bf16[256,1536]{1,0:T(8,128)(2,1)S(1)}, bf16[256,1536]{1,0:T(8,128)(2,1)S(1)}, u32[]{:S(2)}, u32[]{:S(2)}) collective-permute-start(bf16[256,1536]{1,0:T(8,128)(2,1)S(1)} %slab_product.10.left), channel_id=1, source_target_pairs={{0,1},{3,2},{4,5},{7,6},{8,9},{11,10},{12,13},{15,14},{16,17},{19,... | collective-permute-start | bytes 2359304 | tf_op jit(solution)/shard_map/ppermute | solution.py:38
  100.9 20.9 %collective-permute-start.15 = (bf16[256,1536]{1,0:T(8,128)(2,1)S(1)}, bf16[256,1536]{1,0:T(8,128)(2,1)S(1)}, u32[]{:S(2)}, u32[]{:S(2)}) collective-permute-start(bf16[256,1536]{1,0:T(8,128)(2,1)S(1)} %half_sum.9.left), channel_id=1, source_target_pairs={{1,2},{2,1},{5,6},{6,5},{9,10},{10,9},{13,14},{14,13},{17,18},{18,... | collective-permute-start | bytes 2359304 | tf_op jit(solution)/shard_map/ppermute | solution.py:38
  103.2 25.8 %collective-permute-start.14 = (bf16[256,1536]{1,0:T(8,128)(2,1)S(1)}, bf16[256,1536]{1,0:T(8,128)(2,1)S(1)}, u32[]{:S(2)}, u32[]{:S(2)}) collective-permute-start(bf16[256,1536]{1,0:T(8,128)(2,1)S(1)} %amplitude.8.left), channel_id=1, source_target_pairs={{1,0},{2,3},{5,4},{6,7},{9,8},{10,11},{13,12},{14,15},{17,16},{18,... | collective-permute-start | bytes 2359304 | tf_op jit(solution)/shard_map/ppermute | solution.py:38
  117.4 21.1 %collective-permute-start.13 = (bf16[256,1536]{1,0:T(8,128)(2,1)S(1)}, bf16[256,1536]{1,0:T(8,128)(2,1)S(1)}, u32[]{:S(2)}, u32[]{:S(2)}) collective-permute-start(bf16[256,1536]{1,0:T(8,128)(2,1)S(1)} %slab_product.11.left), channel_id=1, source_target_pairs={{0,1},{3,2},{4,5},{7,6},{8,9},{11,10},{12,13},{15,14},{16,17},{19,... | collective-permute-start | bytes 2359304 | tf_op jit(solution)/shard_map/ppermute | solution.py:38
  121.7 16.9 %collective-permute-start.18 = (bf16[256,1536]{1,0:T(8,128)(2,1)S(1)}, bf16[256,1536]{1,0:T(8,128)(2,1)S(1)}, u32[]{:S(2)}, u32[]{:S(2)}) collective-permute-start(bf16[256,1536]{1,0:T(8,128)(2,1)S(1)} %half_sum.10.left), channel_id=1, source_target_pairs={{1,2},{2,1},{5,6},{6,5},{9,10},{10,9},{13,14},{14,13},{17,18},{18,... | collective-permute-start | bytes 2359304 | tf_op jit(solution)/shard_map/ppermute | solution.py:38
  124.0 22.1 %collective-permute-start.20 = (bf16[256,1536]{1,0:T(8,128)(2,1)S(1)}, bf16[256,1536]{1,0:T(8,128)(2,1)S(1)}, u32[]{:S(2)}, u32[]{:S(2)}) collective-permute-start(bf16[256,1536]{1,0:T(8,128)(2,1)S(1)} %amplitude.9.left), channel_id=1, source_target_pairs={{1,0},{2,3},{5,4},{6,7},{9,8},{10,11},{13,12},{14,15},{17,16},{18,... | collective-permute-start | bytes 2359304 | tf_op jit(solution)/shard_map/ppermute | solution.py:38
  163.9 47.0 %collective-permute-start.24 = (bf16[1536,1024]{1,0:T(8,128)(2,1)S(1)}, bf16[1536,1024]{1,0:T(8,128)(2,1)S(1)}, u32[]{:S(2)}, u32[]{:S(2)}) collective-permute-start(bf16[1536,1024]{1,0:T(8,128)(2,1)S(1)} %cross_term.2.kept), channel_id=1, source_target_pairs={{4,12},{12,4},{5,13},{13,5},{6,14},{14,6},{7,15},{15,7},{20,28},{2... | collective-permute-start | bytes 9437192 | tf_op jit(solution)/shard_map/ppermute | solution.py:38
  165.8 21.2 %collective-permute-start.19 = (bf16[256,1536]{1,0:T(8,128)(2,1)S(1)}, bf16[256,1536]{1,0:T(8,128)(2,1)S(1)}, u32[]{:S(2)}, u32[]{:S(2)}) collective-permute-start(bf16[256,1536]{1,0:T(8,128)(2,1)S(1)} %amplitude.10.left), channel_id=1, source_target_pairs={{1,0},{2,3},{5,4},{6,7},{9,8},{10,11},{13,12},{14,15},{17,16},{18,... | collective-permute-start | bytes 2359304 | tf_op jit(solution)/shard_map/ppermute | solution.py:38
  167.1 20.5 %collective-permute-start.17 = (bf16[256,1536]{1,0:T(8,128)(2,1)S(1)}, bf16[256,1536]{1,0:T(8,128)(2,1)S(1)}, u32[]{:S(2)}, u32[]{:S(2)}) collective-permute-start(bf16[256,1536]{1,0:T(8,128)(2,1)S(1)} %half_sum.11.left), channel_id=1, source_target_pairs={{1,2},{2,1},{5,6},{6,5},{9,10},{10,9},{13,14},{14,13},{17,18},{18,... | collective-permute-start | bytes 2359304 | tf_op jit(solution)/shard_map/ppermute | solution.py:38
  189.1 21.7 %collective-permute-start.23 = (bf16[256,1536]{1,0:T(8,128)(2,1)S(1)}, bf16[256,1536]{1,0:T(8,128)(2,1)S(1)}, u32[]{:S(2)}, u32[]{:S(2)}) collective-permute-start(bf16[256,1536]{1,0:T(8,128)(2,1)S(1)} %amplitude.11.left), channel_id=1, source_target_pairs={{1,0},{2,3},{5,4},{6,7},{9,8},{10,11},{13,12},{14,15},{17,16},{18,... | collective-permute-start | bytes 2359304 | tf_op jit(solution)/shard_map/ppermute | solution.py:38
  212.6 24.3 %collective-permute-start.26 = (bf16[1536,512]{1,0:T(8,128)(2,1)S(1)}, bf16[1536,512]{1,0:T(8,128)(2,1)S(1)}, u32[]{:S(2)}, u32[]{:S(2)}) collective-permute-start(bf16[1536,512]{1,0:T(8,128)(2,1)S(1)} %cross_term.3.kept), channel_id=1, source_target_pairs={{4,12},{12,4},{5,13},{13,5},{6,14},{14,6},{7,15},{15,7},{20,28},{2... | collective-permute-start | bytes 4718600 | tf_op jit(solution)/shard_map/ppermute | solution.py:38
  221.7 21.4 %collective-permute-start.27 = (bf16[384,384]{1,0:T(8,128)(2,1)S(1)}, bf16[384,384]{1,0:T(8,128)(2,1)S(1)}, u32[]{:S(2)}, u32[]{:S(2)}) collective-permute-start(bf16[384,384]{1,0:T(8,128)(2,1)S(1)} %fusion.1), channel_id=1, source_target_pairs={{0,8},{4,12},{8,0},{12,4},{1,9},{5,13},{9,1},{13,5},{2,10},{6,14},... | collective-permute-start | bytes 884744 | tf_op jit(solution)/shard_map/ppermute | solution.py:38
  (16 other events, 130.2 us)

commit v4 on v3

--- a/solution.py
+++ b/solution.py
@@ -139,7 +139,7 @@
 
 
 def mix_kernel(half, band, rows, cols, straight_core, place, *refs):
-    own, other, mix, dens, amp_t, amp, sems = refs
+    own, *other, mix, dens, amp_t, amp, sems = refs
     core, slab, chip = place[0], place[1], place[2]
     nvirt = 2 * half
     step = pl.program_id(0)
@@ -147,9 +147,11 @@
     @pl.when(step == 0)
     def _():
         copies = []
-        for i, (piece, side) in enumerate(((own, core), (other, 1 - core))):
-            start = pl.multiple_of(side * half, 128)
-            copies.append(pltpu.make_async_copy(piece, amp_t.at[pl.ds(start, half), :], sems.at[i]))
+        for i, piece in enumerate((own, *other)):
+            width = piece.shape[0]
+            start = core * half if i == 0 else (1 - core) * half + (i - 1) * width
+            rows_at = pl.ds(pl.multiple_of(start, 128), width)
+            copies.append(pltpu.make_async_copy(piece, amp_t.at[rows_at, :], sems.at[i]))
         for copy in copies:
             copy.start()
         for copy in copies:
@@ -184,7 +186,7 @@
         grid_spec=pltpu.PrefetchScalarGridSpec(
             num_scalar_prefetch=1,
             grid=(nvirt // band,),
-            in_specs=[pl.BlockSpec(memory_space=pl.ANY)] * 2,
+            in_specs=[pl.BlockSpec(memory_space=pl.ANY)] * (1 + len(other)),
             out_specs=[
                 pl.BlockSpec((band, nvirt), lambda i, p: (i, 0)),
                 pl.BlockSpec((chips, rows, cols), lambda i, p: (0, 0, 0)),
@@ -192,7 +194,7 @@
             scratch_shapes=[
                 pltpu.VMEM((nvirt, nvirt), BF16),
                 pltpu.VMEM((nvirt, nvirt), BF16),
-                pltpu.SemaphoreType.DMA((2,)),
+                pltpu.SemaphoreType.DMA((1 + len(other),)),
             ],
         ),
         out_shape=[
@@ -202,7 +204,7 @@
         compiler_params=pltpu.CompilerParams(vmem_limit_bytes=LIMIT),
         cost_estimate=TINY,
         name="mix",
-    )(place, own, other)
+    )(place, own, *other)
 
 
 def block_of(rows):
@@ -225,18 +227,19 @@
 def cross_columns(place, lower, upper, partner, weight, start, step):
     rows, nvirt = partner.shape
     block = block_of(rows)
+    part = nvirt // 3
     return pl.pallas_call(
         cross_kernel,
         grid_spec=pltpu.PrefetchScalarGridSpec(
             num_scalar_prefetch=1,
-            grid=(rows // block,),
+            grid=(step // part, rows // block),
             in_specs=[
-                pl.BlockSpec((block, nvirt // 2), lambda i, p: (jnp.where(p[0] == 0, i, 0), 0)),
-                pl.BlockSpec((block, nvirt // 2), lambda i, p: (jnp.where(p[0] == 0, i, 0), 0)),
-                pl.BlockSpec((block, nvirt), lambda i, p: (jnp.where(p[0] == 0, 0, i), 0)),
-                pl.BlockSpec((nvirt, step), lambda i, p: (0, start // step)),
+                pl.BlockSpec((block, nvirt // 2), lambda j, i, p: (jnp.where(p[0] == 0, i, 0), 0)),
+                pl.BlockSpec((block, nvirt // 2), lambda j, i, p: (jnp.where(p[0] == 0, i, 0), 0)),
+                pl.BlockSpec((block, nvirt), lambda j, i, p: (jnp.where(p[0] == 0, 0, i), 0)),
+                pl.BlockSpec((nvirt, part), lambda j, i, p: (0, start // part + j)),
             ],
-            out_specs=pl.BlockSpec((block, step), lambda i, p: (i, 0)),
+            out_specs=pl.BlockSpec((block, part), lambda j, i, p: (i, j)),
         ),
         out_shape=jax.ShapeDtypeStruct((rows, step), BF16),
         compiler_params=pltpu.CompilerParams(vmem_limit_bytes=LIMIT),
@@ -282,6 +285,63 @@
         cost_estimate=TINY,
         name="local_term",
     )(place, partner, weight, kept, arrived, *before)
+
+
+def local_kernel(partner, weight, out):
+    out[...] = contract(partner[...], weight[...], 1, 0).astype(BF16)
+
+
+def local_columns(partner, weight, start, step):
+    rows, nvirt = partner.shape
+    block = block_of(rows)
+    part = nvirt // 3
+    return pl.pallas_call(
+        local_kernel,
+        grid=(step // part, rows // block),
+        in_specs=[
+            pl.BlockSpec((block, nvirt), lambda j, i: (i, 0)),
+            pl.BlockSpec((nvirt, part), lambda j, i: (0, start // part + j)),
+        ],
+        out_specs=pl.BlockSpec((block, part), lambda j, i: (i, j)),
+        out_shape=jax.ShapeDtypeStruct((rows, step), BF16),
+        compiler_params=pltpu.CompilerParams(vmem_limit_bytes=LIMIT),
+        cost_estimate=TINY,
+        name="local_rest",
+    )(partner, weight)
+
+
+def closing_kernel(place, rest, kept, arrived, gamma, out):
+    @pl.when(place[0] == 0)
+    def _():
+        out[0] = (rest[...].astype(F32) + kept[...].astype(F32)).astype(BF16)
+
+    @pl.when(place[0] != 0)
+    def _():
+        out[0] = (rest[...].astype(F32) + arrived[...].astype(F32)).astype(BF16)
+
+
+def closing_columns(place, rest, kept, arrived, start, step, gamma):
+    rows = rest.shape[0]
+    part = 256
+    return pl.pallas_call(
+        closing_kernel,
+        grid_spec=pltpu.PrefetchScalarGridSpec(
+            num_scalar_prefetch=1,
+            grid=(step // part,),
+            in_specs=[
+                pl.BlockSpec((rows, part), lambda i, p: (0, i)),
+                pl.BlockSpec((rows, part), lambda i, p: (0, jnp.where(p[0] == 0, i, 0))),
+                pl.BlockSpec((rows, part), lambda i, p: (0, jnp.where(p[0] == 0, 0, i))),
+                pl.BlockSpec(memory_space=pl.ANY),
+            ],
+            out_specs=pl.BlockSpec((1, rows, part), lambda i, p: (0, 0, start // part + i)),
+        ),
+        out_shape=jax.ShapeDtypeStruct(gamma.shape, BF16),
+        input_output_aliases={4: 0},
+        compiler_params=pltpu.CompilerParams(vmem_limit_bytes=LIMIT),
+        cost_estimate=TINY,
+        name="closing_sum",
+    )(place, rest, kept, arrived, gamma)
 
 
 def shards(bmat, eps_occ, eps_vir, occ_label):
@@ -315,32 +375,27 @@
     eps_rows, eps_cols = eps_vir.reshape(nvirt, 1), eps_vir.reshape(1, nvirt)
 
     mine = bmat[0]
-    partner = lax.ppermute(mine, "occ", swap_pairs)
-    order = Order(partner)
+    order = Order(where)
     incoming = {}
 
-    def ship(j, *others):
-        sent = order.step(
-            lambda p, m: jnp.where(
-                first,
-                p[:, j * width : (j + 1) * width],
-                m[:, half + j * width : half + (j + 1) * width],
-            ),
-            partner,
-            mine,
-        )
-        incoming[j] = order.send(sent, "occ", next_pairs, *others)
-
-    ship(0)
+    def ship(j, low, high):
+        sent = order.step(lambda a, b: jnp.where(first, a, b), low, high)
+        incoming[j] = order.send(sent, "occ", next_pairs)
+
+    def columns(value, start):
+        return lax.slice_in_dim(value, start, start + width, axis=1)
+
+    ship(0, order.send(columns(mine, 0), "occ", down_pairs), columns(mine, half))
+    partner = order.send(mine, "occ", swap_pairs)
+    ship(1, columns(partner, width), columns(mine, half + width))
     odd = order.step(lambda m, p: jnp.where(first, p, m), mine, partner)
     even = order.step(lambda m, p: jnp.where(first, m, p), mine, partner)
-    ship(1)
 
     def product(kind, j):
         if kind == "cross":
             part = order.step(lambda a, b: product_rows(where, a, b, width, j), incoming[j], even)
             if j + 2 < PIECES:
-                ship(j + 2)
+                ship(j + 2, columns(partner, (j + 2) * width), columns(mine, half + (j + 2) * width))
             return part
         return order.step(lambda a, b: product_rows(where, a, b, width, j), even, odd)
 
@@ -349,7 +404,7 @@
             where, energies[kind], eps_rows, eps_cols, mine_sum, other_sum, j * width, half
         )
 
-    jobs = [("local", 0)] + [("cross", j) for j in range(PIECES)] + [("local", j) for j in range(1, PIECES)]
+    jobs = [("local", 0), ("cross", 0), ("cross", 1), ("cross", 2), ("local", 1), ("local", 2)]
     n = len(jobs)
     left = {kind: sum(job[0] == kind for job in jobs) for kind in ("cross", "local")}
     own = {"cross": [], "local": []}
@@ -401,7 +456,7 @@
             left[kind] -= 1
 
     third = nvirt // 3
-    spans = [(0, 2 * third), (2 * third, third)]
+    spans = [(0, third), (third, 2 * third)]
     kept, arrived = [], []
 
     def cross_term():
@@ -416,40 +471,51 @@
             arrived.append(order.send(kept[j], "occ", back_pairs))
 
     cross_mix = []
-    received = upper = None
     for s in range(-1, n + 2):
         if s + 1 < n:
             feed(s + 1)
         pass_across(s)
-        if s < n:
+        if not cross_mix:
             pass_out(s - 1)
             collect(s - 2)
-        elif s == n:
+        else:
+            if s == n + 1:
+                settle(arrived[0])
             collect(s - 2)
             pass_out(s - 1)
             cross_term()
-        else:
-            settle(arrived[0])
-            collect(s - 2)
         if not left["cross"] and not cross_mix:
             other = order.send(own["cross"][0], "occ", swap_pairs)
             received = order.step(lambda *v: jnp.concatenate(v, axis=1), *incoming.values())
             upper = order.send(received, "occ", down_pairs)
-            cross_mix = order.step(lambda a, b: mix(where, a, b, 0, slabs, count), own["cross"][0], other)
+            cross_mix = order.step(
+                lambda a, b: mix(where, a, (b,), 0, slabs, count), own["cross"][0], other
+            )
             cross_term()
-    other = order.send(own["local"][0], "occ", swap_pairs)
-    weight, dens = order.step(lambda a, b: mix(where, a, b, 1, slabs, count), own["local"][0], other)
+    while len(kept) < len(spans):
+        cross_term()
+
+    other = [
+        order.send(lax.slice_in_dim(own["local"][0], j * width, (j + 1) * width), "occ", swap_pairs)
+        for j in range(PIECES)
+    ]
+    weight, dens = order.step(
+        lambda a, *b: mix(where, a, b, 1, slabs, count), own["local"][0], *other
+    )
     total = order.step(lambda a, b: (a + b) * nvirt ** (-0.5), cross_mix[1], dens)
     density = total[0]
+    moved = []
     for ahead in range(1, chips):
         pairs = [(i, (i + 2 * ahead) % count) for i in range(count)]
-        density = density + order.send(total[ahead].astype(BF16), "occ", pairs).astype(F32)
-    gamma = None
-    for j in range(len(spans)):
-        gamma = order.step(
-            lambda p, w, k, a, *g: final_columns(where, p, w, k, a, *spans[j], *g),
-            partner, weight, kept[j], arrived[j], *([] if gamma is None else [gamma]),
-        )
+        moved.append(order.send(total[ahead].astype(BF16), "occ", pairs))
+    gamma = order.step(
+        lambda p, w, k, a: final_columns(where, p, w, k, a, *spans[0]), partner, weight, kept[0], arrived[0]
+    )
+    rest = order.step(lambda p, w: local_columns(p, w, *spans[1]), partner, weight)
+    gamma = order.step(
+        lambda r, k, a, g: closing_columns(where, r, k, a, *spans[1], g), rest, kept[1], arrived[1], gamma
+    )
+    density = order.step(lambda d, *m: d + sum(v.astype(F32) for v in m), density, *moved)
     return gamma, density
 
 

time: 245 us -> 226 us (0.922)
  waiting for transfers between devices: 99.1 us -> 74.2 us
  starting transfers between devices: 50.5 us -> 65.3 us
  other arithmetic: 17.5 us -> 7.47 us
  local copies, waits for them, and re-layouts: 4.38 us -> 8.15 us
  Pallas kernels: 71.3 us -> 68.1 us
    ppermute x27 -> x31, waiting for transfers between devices: 91 us -> 74.2 us  [send(): return lax.ppermute(self.ready(value, *others)[0], axis, pairs)]
    ppermute x27 -> x31, starting transfers between devices: 50.4 us -> 65.3 us  [send(): return lax.ppermute(self.ready(value, *others)[0], axis, pairs)]
    pallas_call x2 -> x1, Pallas kernels: 15.4 us -> 4.58 us  [final_columns(): pl.pallas_call(final_kernel, grid_spec=pltpu.PrefetchScalarGridSpec(num_s...]
    pallas_call x0 -> x2, Pallas kernels: none -> 9.74 us  [the longest x1 5.99 us: local_columns(): pl.pallas_call(local_kernel, grid=(step // part, rows // block), in_specs...]
    ppermute x1 -> x0, waiting for transfers between devices: 8.12 us -> none  [shards(): partner = lax.ppermute(mine, 'occ', swap_pairs)]
    select_n x1, other arithmetic: 4.51 us -> 0.46 us  [shards(): even = order.step(lambda m, p: jnp.where(first, m, p), mine, partner)]
    select_n x3, other arithmetic: 5.95 us -> 2.41 us  [ship(): sent = order.step(lambda a, b: jnp.where(first, a, b), low, high)]
    select_n x1, other arithmetic: 2.99 us -> 0.49 us  [shards(): odd = order.step(lambda m, p: jnp.where(first, p, m), mine, partner)]
  transfers between devices with their start and end apart: 28 -> 31, of which waited for: 15 -> 18; matrix products, arithmetic and copies ran while one was open for 4% -> 3% of each run, Pallas kernels for 26% -> 30%
where the time goes in v4:
time: 226 us; the launch traced here: 225 us
  waiting for transfers between devices  74.2 us (33%)
  Pallas kernels  68.1 us (30%)
  starting transfers between devices  65.3 us (29%)
  local copies, waits for them, and re-layouts  8.15 us (4%)
  other arithmetic  7.47 us (3%)
    ppermute x31, waiting for transfers between devices, send(): return lax.ppermute(self.ready(value, *others)[0], axis, pairs)  74.2 us
    ppermute x31, starting transfers between devices, send(): return lax.ppermute(self.ready(value, *others)[0], axis, pairs)  65.3 us
    pallas_call x6, Pallas kernels, product_rows(): pl.pallas_call(product_kernel, grid_spec=pltpu.PrefetchScalarGridSpec(num...  16.6 us
    pallas_call x6, Pallas kernels, amplitude(): pl.pallas_call(amp_kernel, grid_spec=pltpu.PrefetchScalarGridSpec(num_sca...  10.2 us
    pallas_call x2, Pallas kernels, cross_columns(): pl.pallas_call(cross_kernel, grid_spec=pltpu.PrefetchScalarGridSpec(num_s...  10.2 us
    pallas_call x2, Pallas kernels, mix(): pl.pallas_call(functools.partial(mix_kernel, nvirt // 2, band, rows, cols...  9.55 us
    pallas_call x1, Pallas kernels, local_columns(): pl.pallas_call(local_kernel, grid=(step // part, rows // block), in_specs...  5.99 us
    unnamed x30, local copies, waits for them, and re-layouts  4.76 us
  transfers between devices with their start and end apart: 31, of which 18 were waited for; matrix products, arithmetic and copies ran while one was open for 3% of the time, Pallas kernels for 30%

profile of v4, /device:TPU:1, one launch (start us, length us, event | category | flops | bytes accessed | tf_op | source)
XLA Modules:
  0.0 224.5 jit_solution(4978131479309547311)
XLA Ops:
  11.2 5.1 %collective-permute-done.1.partner = bf16[1536,1536]{1,0:T(8,128)(2,1)S(1)} collective-permute-done((bf16[1536,1536]{1,0:T(8,128)(2,1)}, bf16[1536,1536]{1,0:T(8,128)(2,1)S(1)}, u32[]{:S(2)}, u32[]{:S(2)}) %collective-permute-start.1) | collective-permute-done | bytes 4718624 | tf_op jit(solution)/shard_map/ppermute | solution.py:38
  23.7 4.7 %collective-permute-start.5 = (bf16[256,1536]{1,0:T(8,128)(2,1)S(1)}, bf16[256,1536]{1,0:T(8,128)(2,1)S(1)}, u32[]{:S(2)}, u32[]{:S(2)}) collective-permute-start(bf16[256,1536]{1,0:T(8,128)(2,1)S(1)} %slab_product.6.left), channel_id=1, source_target_pairs={{0,1},{3,2},{4,5},{7,6},{8,9},{11,10},{12,13},{15,14},{16,17},{19,... | collective-permute-start | bytes 2359304 | tf_op jit(solution)/shard_map/ppermute | solution.py:38
  34.1 4.2 %collective-permute-start.3 = (bf16[256,1536]{1,0:T(8,128)(2,1)S(1)}, bf16[256,1536]{1,0:T(8,128)(2,1)}, u32[]{:S(2)}, u32[]{:S(2)}) collective-permute-start(bf16[256,1536]{1,0:T(8,128)(2,1)S(1)} %slab_product.7.left), channel_id=1, source_target_pairs={{0,1},{3,2},{4,5},{7,6},{8,9},{11,10},{12,13},{15,14},{16,17},{19,... | collective-permute-start | bytes 2359304 | tf_op jit(solution)/shard_map/ppermute | solution.py:38
  38.3 4.1 %collective-permute-done.5.right = bf16[256,1536]{1,0:T(8,128)(2,1)S(1)} collective-permute-done((bf16[256,1536]{1,0:T(8,128)(2,1)S(1)}, bf16[256,1536]{1,0:T(8,128)(2,1)S(1)}, u32[]{:S(2)}, u32[]{:S(2)}) %collective-permute-start.5) | collective-permute-done | bytes 786464 | tf_op jit(solution)/shard_map/ppermute | solution.py:38
  53.8 5.5 %collective-permute-done.3.right = bf16[256,1536]{1,0:T(8,128)(2,1)} collective-permute-done((bf16[256,1536]{1,0:T(8,128)(2,1)S(1)}, bf16[256,1536]{1,0:T(8,128)(2,1)}, u32[]{:S(2)}, u32[]{:S(2)}) %collective-permute-start.3) | collective-permute-done | bytes 786464 | tf_op jit(solution)/shard_map/ppermute | solution.py:38
  59.3 4.2 %collective-permute-start.7 = (bf16[256,1536]{1,0:T(8,128)(2,1)S(1)}, bf16[256,1536]{1,0:T(8,128)(2,1)S(1)}, u32[]{:S(2)}, u32[]{:S(2)}) collective-permute-start(bf16[256,1536]{1,0:T(8,128)(2,1)S(1)} %slab_product.8.left), channel_id=1, source_target_pairs={{0,1},{3,2},{4,5},{7,6},{8,9},{11,10},{12,13},{15,14},{16,17},{19,... | collective-permute-start | bytes 2359304 | tf_op jit(solution)/shard_map/ppermute | solution.py:38
  72.4 4.1 %collective-permute-start.12 = (bf16[256,1536]{1,0:T(8,128)(2,1)S(1)}, bf16[256,1536]{1,0:T(8,128)(2,1)S(1)}, u32[]{:S(2)}, u32[]{:S(2)}) collective-permute-start(bf16[256,1536]{1,0:T(8,128)(2,1)S(1)} %slab_product.9.left), channel_id=1, source_target_pairs={{0,1},{3,2},{4,5},{7,6},{8,9},{11,10},{12,13},{15,14},{16,17},{19,... | collective-permute-start | bytes 2359304 | tf_op jit(solution)/shard_map/ppermute | solution.py:38
  81.9 3.5 %collective-permute-done.13.right = bf16[256,1536]{1,0:T(8,128)(2,1)S(1)} collective-permute-done((bf16[256,1536]{1,0:T(8,128)(2,1)S(1)}, bf16[256,1536]{1,0:T(8,128)(2,1)S(1)}, u32[]{:S(2)}, u32[]{:S(2)}) %collective-permute-start.13) | collective-permute-done | bytes 786464 | tf_op jit(solution)/shard_map/ppermute | solution.py:38
  88.8 5.1 %collective-permute-done.12.right = bf16[256,1536]{1,0:T(8,128)(2,1)S(1)} collective-permute-done((bf16[256,1536]{1,0:T(8,128)(2,1)S(1)}, bf16[256,1536]{1,0:T(8,128)(2,1)S(1)}, u32[]{:S(2)}, u32[]{:S(2)}) %collective-permute-start.12) | collective-permute-done | bytes 786464 | tf_op jit(solution)/shard_map/ppermute | solution.py:38
  93.9 4.1 %collective-permute-start.17 = (bf16[256,1536]{1,0:T(8,128)(2,1)S(1)}, bf16[256,1536]{1,0:T(8,128)(2,1)S(1)}, u32[]{:S(2)}, u32[]{:S(2)}) collective-permute-start(bf16[256,1536]{1,0:T(8,128)(2,1)S(1)} %slab_product.10.left), channel_id=1, source_target_pairs={{0,1},{3,2},{4,5},{7,6},{8,9},{11,10},{12,13},{15,14},{16,17},{19,... | collective-permute-start | bytes 2359304 | tf_op jit(solution)/shard_map/ppermute | solution.py:38
  105.7 4.1 %collective-permute-start.14 = (bf16[256,1536]{1,0:T(8,128)(2,1)S(1)}, bf16[256,1536]{1,0:T(8,128)(2,1)S(1)}, u32[]{:S(2)}, u32[]{:S(2)}) collective-permute-start(bf16[256,1536]{1,0:T(8,128)(2,1)S(1)} %slab_product.11.left), channel_id=1, source_target_pairs={{0,1},{3,2},{4,5},{7,6},{8,9},{11,10},{12,13},{15,14},{16,17},{19,... | collective-permute-start | bytes 2359304 | tf_op jit(solution)/shard_map/ppermute | solution.py:38
  117.7 9.7 %collective-permute-done.14.right = bf16[256,1536]{1,0:T(8,128)(2,1)S(1)} collective-permute-done((bf16[256,1536]{1,0:T(8,128)(2,1)S(1)}, bf16[256,1536]{1,0:T(8,128)(2,1)S(1)}, u32[]{:S(2)}, u32[]{:S(2)}) %collective-permute-start.14) | collective-permute-done | bytes 786464 | tf_op jit(solution)/shard_map/ppermute | solution.py:38
  129.2 4.8 %collective-permute-done.21.right = bf16[256,1536]{1,0:T(8,128)(2,1)S(1)} collective-permute-done((bf16[256,1536]{1,0:T(8,128)(2,1)S(1)}, bf16[256,1536]{1,0:T(8,128)(2,1)S(1)}, u32[]{:S(2)}, u32[]{:S(2)}) %collective-permute-start.21) | collective-permute-done | bytes 786464 | tf_op jit(solution)/shard_map/ppermute | solution.py:38
  134.7 6.8 %collective-permute-start.22 = (bf16[768,1536]{1,0:T(8,128)(2,1)S(1)}, bf16[768,1536]{1,0:T(8,128)(2,1)S(1)}, u32[]{:S(2)}, u32[]{:S(2)}) collective-permute-start(bf16[768,1536]{1,0:T(8,128)(2,1)S(1)} %amp_of_slab.9.refs_0_), channel_id=1, source_target_pairs={{0,4},{4,0},{8,12},{12,8},{1,5},{5,1},{9,13},{13,9},{2,6},{6,2},{1... | collective-permute-start | bytes 7077896 | tf_op jit(solution)/shard_map/ppermute | solution.py:38
  145.9 4.8 %mix.2 = (bf16[1536,1536]{1,0:T(8,128)(2,1)S(1)}, f32[2,384,384]{2,1,0:T(8,128)S(1)}) custom-call(s32[3]{0:T(128)S(1)} %pad_add_fusion.place, bf16[768,1536]{1,0:T(8,128)(2,1)S(1)} %amp_of_slab.9.refs_0_, bf16[768,1536]{1,0:T(8,128)(2,1)S(1)} %collective-permute-done.22.refs_1_), custom_call_target="tpu_custom_call" | custom-call | flops 10000000 | bytes 10000 | tf_op jit(solution)/shard_map/mix/pallas_call | solution.py:184
  150.7 3.5 %cross_term.2.kept = bf16[1536,512]{1,0:T(8,128)(2,1)S(1)} custom-call(s32[3]{0:T(128)S(1)} %pad_add_fusion.place, bf16[1536,768]{1,0:T(8,128)(2,1)S(1)} %constant_dynamic-update-slice_fusion.lower, bf16[1536,768]{1,0:T(8,128)(2,1)S(1)} %collective-permute-done.23.upper, bf16[1536,1536]{1,0:T(8,128)(2,1)S(1)} %bitcast.11, ...), custom_call_target="tpu_custom_call" | custom-call | flops 10000000 | bytes 10000 | tf_op jit(solution)/shard_map/cross_term/pallas_call | solution.py:231
  157.3 7.4 %collective-permute-done.20.right = bf16[256,1536]{1,0:T(8,128)(2,1)S(1)} collective-permute-done((bf16[256,1536]{1,0:T(8,128)(2,1)S(1)}, bf16[256,1536]{1,0:T(8,128)(2,1)S(1)}, u32[]{:S(2)}, u32[]{:S(2)}) %collective-permute-start.20) | collective-permute-done | bytes 786464 | tf_op jit(solution)/shard_map/ppermute | solution.py:38
  166.9 6.7 %cross_term.3.kept = bf16[1536,1024]{1,0:T(8,128)(2,1)S(1)} custom-call(s32[3]{0:T(128)S(1)} %pad_add_fusion.place, bf16[1536,768]{1,0:T(8,128)(2,1)S(1)} %constant_dynamic-update-slice_fusion.lower, bf16[1536,768]{1,0:T(8,128)(2,1)S(1)} %collective-permute-done.23.upper, bf16[1536,1536]{1,0:T(8,128)(2,1)S(1)} %bitcast.11, ...), custom_call_target="tpu_custom_call" | custom-call | flops 10000000 | bytes 10000 | tf_op jit(solution)/shard_map/cross_term/pallas_call | solution.py:231
  173.6 3.1 %collective-permute-start.29 = (bf16[1536,1024]{1,0:T(8,128)(2,1)S(1)}, bf16[1536,1024]{1,0:T(8,128)(2,1)S(1)}, u32[]{:S(2)}, u32[]{:S(2)}) collective-permute-start(bf16[1536,1024]{1,0:T(8,128)(2,1)S(1)} %cross_term.3.kept), channel_id=1, source_target_pairs={{4,12},{12,4},{5,13},{13,5},{6,14},{14,6},{7,15},{15,7},{20,28},{2... | collective-permute-start | bytes 9437192 | tf_op jit(solution)/shard_map/ppermute | solution.py:38
  178.0 19.3 %collective-permute-done.24.right = bf16[256,1536]{1,0:T(8,128)(2,1)S(1)} collective-permute-done((bf16[256,1536]{1,0:T(8,128)(2,1)S(1)}, bf16[256,1536]{1,0:T(8,128)(2,1)S(1)}, u32[]{:S(2)}, u32[]{:S(2)}) %collective-permute-start.24) | collective-permute-done | bytes 786464 | tf_op jit(solution)/shard_map/ppermute | solution.py:38
  202.9 4.8 %mix.3 = (bf16[1536,1536]{1,0:T(8,128)(2,1)S(1)}, f32[2,384,384]{2,1,0:T(8,128)S(1)}) custom-call(s32[3]{0:T(128)S(1)} %pad_add_fusion.place, bf16[768,1536]{1,0:T(8,128)(2,1)S(1)} %amp_of_slab.11.refs_0_, bf16[256,1536]{1,0:T(8,128)(2,1)S(1)} %collective-permute-done.26.refs_1_, bf16[256,1536]{1,0:T(8,128)(2,1)S(1)} %collective-permute-done.27.refs_2_, ...), custom_call_target="tpu_custom_call" | custom-call | flops 10000000 | bytes 10000 | tf_op jit(solution)/shard_map/mix/pallas_call | solution.py:184
  209.2 4.6 %local_term.1.gamma = bf16[1,1536,1536]{2,1,0:T(8,128)(2,1)} custom-call(s32[3]{0:T(128)S(1)} %pad_add_fusion.place, bf16[1536,1536]{1,0:T(8,128)(2,1)S(1)} %bitcast.11, bf16[1536,1536]{1,0:T(8,128)(2,1)S(1)} %get-tuple-element.249.weight, bf16[1536,512]{1,0:T(8,128)(2,1)S(1)} %cross_term.2.kept, bf16[1536,512]{1,0:T(8,128)(2,1)S(1)} %collective-permute-done.25.arrived), custom_call_target="tpu_custom_call" | custom-call | flops 10000000 | bytes 10000 | tf_op jit(solution)/shard_map/local_term/pallas_call | solution.py:268
  213.8 6.0 %local_rest.1.rest = bf16[1536,1024]{1,0:T(8,128)(2,1)S(1)} custom-call(bf16[1536,1536]{1,0:T(8,128)(2,1)S(1)} %bitcast.11, bf16[1536,1536]{1,0:T(8,128)(2,1)S(1)} %get-tuple-element.249.weight), custom_call_target="tpu_custom_call" | custom-call | flops 10000000 | bytes 10000 | tf_op jit(solution)/shard_map/local_rest/pallas_call | solution.py:298
  219.9 3.7 %closing_sum.1 = bf16[1,1536,1536]{2,1,0:T(8,128)(2,1)} custom-call(s32[3]{0:T(128)S(1)} %pad_add_fusion.place, bf16[1536,1024]{1,0:T(8,128)(2,1)S(1)} %local_rest.1.rest, bf16[1536,1024]{1,0:T(8,128)(2,1)S(1)} %cross_term.3.kept, bf16[1536,1024]{1,0:T(8,128)(2,1)S(1)} %collective-permute-done.29.arrived, ...), custom_call_target="tpu_custom_call", output_to_operand_aliasing={{}: (4, {})} | custom-call | flops 10000000 | bytes 10000 | tf_op jit(solution)/shard_map/closing_sum/pallas_call | solution.py:326
  (122 shorter events, 89.2 us)
Async XLA Ops:
  8.5 20.5 %collective-permute-start.2 = (bf16[1536,256]{1,0:T(8,128)(2,1)S(1)}, bf16[1536,256]{1,0:T(8,128)(2,1)S(1)}, u32[]{:S(2)}, u32[]{:S(2)}) collective-permute-start(bf16[1536,256]{1,0:T(8,128)(2,1)S(1)} %broadcast_select_fusion.4), channel_id=1, source_target_pairs={{0,8},{4,12},{8,0},{12,4},{1,9},{5,13},{9,1},{13,5},{2,10},{6,14},... | collective-permute-start | bytes 2359304 | tf_op jit(solution)/shard_map/ppermute | solution.py:38
  23.7 18.7 %collective-permute-start.5 = (bf16[256,1536]{1,0:T(8,128)(2,1)S(1)}, bf16[256,1536]{1,0:T(8,128)(2,1)S(1)}, u32[]{:S(2)}, u32[]{:S(2)}) collective-permute-start(bf16[256,1536]{1,0:T(8,128)(2,1)S(1)} %slab_product.6.left), channel_id=1, source_target_pairs={{0,1},{3,2},{4,5},{7,6},{8,9},{11,10},{12,13},{15,14},{16,17},{19,... | collective-permute-start | bytes 2359304 | tf_op jit(solution)/shard_map/ppermute | solution.py:38
  31.8 16.9 %collective-permute-start.4 = (bf16[1536,256]{1,0:T(8,128)(2,1)}, bf16[1536,256]{1,0:T(8,128)(2,1)S(1)}, u32[]{:S(2)}, u32[]{:S(2)}) collective-permute-start(bf16[1536,256]{1,0:T(8,128)(2,1)} %broadcast_select_fusion.3), channel_id=1, source_target_pairs={{0,8},{4,12},{8,0},{12,4},{1,9},{5,13},{9,1},{13,5},{2,10},{6,14},... | collective-permute-start | bytes 2359304 | tf_op jit(solution)/shard_map/ppermute | solution.py:38
  34.1 25.2 %collective-permute-start.3 = (bf16[256,1536]{1,0:T(8,128)(2,1)S(1)}, bf16[256,1536]{1,0:T(8,128)(2,1)}, u32[]{:S(2)}, u32[]{:S(2)}) collective-permute-start(bf16[256,1536]{1,0:T(8,128)(2,1)S(1)} %slab_product.7.left), channel_id=1, source_target_pairs={{0,1},{3,2},{4,5},{7,6},{8,9},{11,10},{12,13},{15,14},{16,17},{19,... | collective-permute-start | bytes 2359304 | tf_op jit(solution)/shard_map/ppermute | solution.py:38
  43.5 22.4 %collective-permute-start.9 = (bf16[256,1536]{1,0:T(8,128)(2,1)}, bf16[256,1536]{1,0:T(8,128)(2,1)}, u32[]{:S(2)}, u32[]{:S(2)}) collective-permute-start(bf16[256,1536]{1,0:T(8,128)(2,1)} %half_sum.6.left), channel_id=1, source_target_pairs={{1,2},{2,1},{5,6},{6,5},{9,10},{10,9},{13,14},{14,13},{17,18},{18,... | collective-permute-start | bytes 2359304 | tf_op jit(solution)/shard_map/ppermute | solution.py:38
  45.2 24.5 %collective-permute-start.8 = (bf16[1536,256]{1,0:T(8,128)(2,1)}, bf16[1536,256]{1,0:T(8,128)(2,1)S(1)}, u32[]{:S(2)}, u32[]{:S(2)}) collective-permute-start(bf16[1536,256]{1,0:T(8,128)(2,1)} %broadcast_select_fusion.2), channel_id=1, source_target_pairs={{0,8},{4,12},{8,0},{12,4},{1,9},{5,13},{9,1},{13,5},{2,10},{6,14},... | collective-permute-start | bytes 2359304 | tf_op jit(solution)/shard_map/ppermute | solution.py:38
  59.3 18.6 %collective-permute-start.7 = (bf16[256,1536]{1,0:T(8,128)(2,1)S(1)}, bf16[256,1536]{1,0:T(8,128)(2,1)S(1)}, u32[]{:S(2)}, u32[]{:S(2)}) collective-permute-start(bf16[256,1536]{1,0:T(8,128)(2,1)S(1)} %slab_product.8.left), channel_id=1, source_target_pairs={{0,1},{3,2},{4,5},{7,6},{8,9},{11,10},{12,13},{15,14},{16,17},{19,... | collective-permute-start | bytes 2359304 | tf_op jit(solution)/shard_map/ppermute | solution.py:38
  64.9 13.2 %collective-permute-start.6 = (bf16[256,1536]{1,0:T(8,128)(2,1)S(1)}, bf16[256,1536]{1,0:T(8,128)(2,1)S(1)}, u32[]{:S(2)}, u32[]{:S(2)}) collective-permute-start(bf16[256,1536]{1,0:T(8,128)(2,1)S(1)} %half_sum.7.left), channel_id=1, source_target_pairs={{1,2},{2,1},{5,6},{6,5},{9,10},{10,9},{13,14},{14,13},{17,18},{18,... | collective-permute-start | bytes 2359304 | tf_op jit(solution)/shard_map/ppermute | solution.py:38
  68.4 17.0 %collective-permute-start.13 = (bf16[256,1536]{1,0:T(8,128)(2,1)S(1)}, bf16[256,1536]{1,0:T(8,128)(2,1)S(1)}, u32[]{:S(2)}, u32[]{:S(2)}) collective-permute-start(bf16[256,1536]{1,0:T(8,128)(2,1)S(1)} %amplitude.6.left), channel_id=1, source_target_pairs={{1,0},{2,3},{5,4},{6,7},{9,8},{10,11},{13,12},{14,15},{17,16},{18,... | collective-permute-start | bytes 2359304 | tf_op jit(solution)/shard_map/ppermute | solution.py:38
  72.4 21.4 %collective-permute-start.12 = (bf16[256,1536]{1,0:T(8,128)(2,1)S(1)}, bf16[256,1536]{1,0:T(8,128)(2,1)S(1)}, u32[]{:S(2)}, u32[]{:S(2)}) collective-permute-start(bf16[256,1536]{1,0:T(8,128)(2,1)S(1)} %slab_product.9.left), channel_id=1, source_target_pairs={{0,1},{3,2},{4,5},{7,6},{8,9},{11,10},{12,13},{15,14},{16,17},{19,... | collective-permute-start | bytes 2359304 | tf_op jit(solution)/shard_map/ppermute | solution.py:38
  78.1 20.8 %collective-permute-start.11 = (bf16[256,1536]{1,0:T(8,128)(2,1)S(1)}, bf16[256,1536]{1,0:T(8,128)(2,1)S(1)}, u32[]{:S(2)}, u32[]{:S(2)}) collective-permute-start(bf16[256,1536]{1,0:T(8,128)(2,1)S(1)} %half_sum.8.left), channel_id=1, source_target_pairs={{1,2},{2,1},{5,6},{6,5},{9,10},{10,9},{13,14},{14,13},{17,18},{18,... | collective-permute-start | bytes 2359304 | tf_op jit(solution)/shard_map/ppermute | solution.py:38
  80.6 20.4 %collective-permute-start.10 = (bf16[256,1536]{1,0:T(8,128)(2,1)S(1)}, bf16[256,1536]{1,0:T(8,128)(2,1)S(1)}, u32[]{:S(2)}, u32[]{:S(2)}) collective-permute-start(bf16[256,1536]{1,0:T(8,128)(2,1)S(1)} %amplitude.7.left), channel_id=1, source_target_pairs={{1,0},{2,3},{5,4},{6,7},{9,8},{10,11},{13,12},{14,15},{17,16},{18,... | collective-permute-start | bytes 2359304 | tf_op jit(solution)/shard_map/ppermute | solution.py:38
  93.9 16.7 %collective-permute-start.17 = (bf16[256,1536]{1,0:T(8,128)(2,1)S(1)}, bf16[256,1536]{1,0:T(8,128)(2,1)S(1)}, u32[]{:S(2)}, u32[]{:S(2)}) collective-permute-start(bf16[256,1536]{1,0:T(8,128)(2,1)S(1)} %slab_product.10.left), channel_id=1, source_target_pairs={{0,1},{3,2},{4,5},{7,6},{8,9},{11,10},{12,13},{15,14},{16,17},{19,... | collective-permute-start | bytes 2359304 | tf_op jit(solution)/shard_map/ppermute | solution.py:38
  98.2 12.6 %collective-permute-start.16 = (bf16[256,1536]{1,0:T(8,128)(2,1)S(1)}, bf16[256,1536]{1,0:T(8,128)(2,1)S(1)}, u32[]{:S(2)}, u32[]{:S(2)}) collective-permute-start(bf16[256,1536]{1,0:T(8,128)(2,1)S(1)} %half_sum.9.left), channel_id=1, source_target_pairs={{1,2},{2,1},{5,6},{6,5},{9,10},{10,9},{13,14},{14,13},{17,18},{18,... | collective-permute-start | bytes 2359304 | tf_op jit(solution)/shard_map/ppermute | solution.py:38
  101.6 15.4 %collective-permute-start.15 = (bf16[256,1536]{1,0:T(8,128)(2,1)S(1)}, bf16[256,1536]{1,0:T(8,128)(2,1)S(1)}, u32[]{:S(2)}, u32[]{:S(2)}) collective-permute-start(bf16[256,1536]{1,0:T(8,128)(2,1)S(1)} %amplitude.8.left), channel_id=1, source_target_pairs={{1,0},{2,3},{5,4},{6,7},{9,8},{10,11},{13,12},{14,15},{17,16},{18,... | collective-permute-start | bytes 2359304 | tf_op jit(solution)/shard_map/ppermute | solution.py:38
  105.7 21.8 %collective-permute-start.14 = (bf16[256,1536]{1,0:T(8,128)(2,1)S(1)}, bf16[256,1536]{1,0:T(8,128)(2,1)S(1)}, u32[]{:S(2)}, u32[]{:S(2)}) collective-permute-start(bf16[256,1536]{1,0:T(8,128)(2,1)S(1)} %slab_product.11.left), channel_id=1, source_target_pairs={{0,1},{3,2},{4,5},{7,6},{8,9},{11,10},{12,13},{15,14},{16,17},{19,... | collective-permute-start | bytes 2359304 | tf_op jit(solution)/shard_map/ppermute | solution.py:38
  110.8 16.8 %collective-permute-start.19 = (bf16[256,1536]{1,0:T(8,128)(2,1)S(1)}, bf16[256,1536]{1,0:T(8,128)(2,1)S(1)}, u32[]{:S(2)}, u32[]{:S(2)}) collective-permute-start(bf16[256,1536]{1,0:T(8,128)(2,1)S(1)} %half_sum.10.left), channel_id=1, source_target_pairs={{1,2},{2,1},{5,6},{6,5},{9,10},{10,9},{13,14},{14,13},{17,18},{18,... | collective-permute-start | bytes 2359304 | tf_op jit(solution)/shard_map/ppermute | solution.py:38
  113.1 21.0 %collective-permute-start.21 = (bf16[256,1536]{1,0:T(8,128)(2,1)S(1)}, bf16[256,1536]{1,0:T(8,128)(2,1)S(1)}, u32[]{:S(2)}, u32[]{:S(2)}) collective-permute-start(bf16[256,1536]{1,0:T(8,128)(2,1)S(1)} %amplitude.9.left), channel_id=1, source_target_pairs={{1,0},{2,3},{5,4},{6,7},{9,8},{10,11},{13,12},{14,15},{17,16},{18,... | collective-permute-start | bytes 2359304 | tf_op jit(solution)/shard_map/ppermute | solution.py:38
  143.9 20.9 %collective-permute-start.20 = (bf16[256,1536]{1,0:T(8,128)(2,1)S(1)}, bf16[256,1536]{1,0:T(8,128)(2,1)S(1)}, u32[]{:S(2)}, u32[]{:S(2)}) collective-permute-start(bf16[256,1536]{1,0:T(8,128)(2,1)S(1)} %amplitude.10.left), channel_id=1, source_target_pairs={{1,0},{2,3},{5,4},{6,7},{9,8},{10,11},{13,12},{14,15},{17,16},{18,... | collective-permute-start | bytes 2359304 | tf_op jit(solution)/shard_map/ppermute | solution.py:38
  145.2 20.2 %collective-permute-start.18 = (bf16[256,1536]{1,0:T(8,128)(2,1)S(1)}, bf16[256,1536]{1,0:T(8,128)(2,1)S(1)}, u32[]{:S(2)}, u32[]{:S(2)}) collective-permute-start(bf16[256,1536]{1,0:T(8,128)(2,1)S(1)} %half_sum.11.left), channel_id=1, source_target_pairs={{1,2},{2,1},{5,6},{6,5},{9,10},{10,9},{13,14},{14,13},{17,18},{18,... | collective-permute-start | bytes 2359304 | tf_op jit(solution)/shard_map/ppermute | solution.py:38
  154.2 43.2 %collective-permute-start.25 = (bf16[1536,512]{1,0:T(8,128)(2,1)S(1)}, bf16[1536,512]{1,0:T(8,128)(2,1)S(1)}, u32[]{:S(2)}, u32[]{:S(2)}) collective-permute-start(bf16[1536,512]{1,0:T(8,128)(2,1)S(1)} %cross_term.2.kept), channel_id=1, source_target_pairs={{4,12},{12,4},{5,13},{13,5},{6,14},{14,6},{7,15},{15,7},{20,28},{2... | collective-permute-start | bytes 4718600 | tf_op jit(solution)/shard_map/ppermute | solution.py:38
  173.6 46.3 %collective-permute-start.29 = (bf16[1536,1024]{1,0:T(8,128)(2,1)S(1)}, bf16[1536,1024]{1,0:T(8,128)(2,1)S(1)}, u32[]{:S(2)}, u32[]{:S(2)}) collective-permute-start(bf16[1536,1024]{1,0:T(8,128)(2,1)S(1)} %cross_term.3.kept), channel_id=1, source_target_pairs={{4,12},{12,4},{5,13},{13,5},{6,14},{14,6},{7,15},{15,7},{20,28},{2... | collective-permute-start | bytes 9437192 | tf_op jit(solution)/shard_map/ppermute | solution.py:38
  176.7 20.6 %collective-permute-start.24 = (bf16[256,1536]{1,0:T(8,128)(2,1)S(1)}, bf16[256,1536]{1,0:T(8,128)(2,1)S(1)}, u32[]{:S(2)}, u32[]{:S(2)}) collective-permute-start(bf16[256,1536]{1,0:T(8,128)(2,1)S(1)} %amplitude.11.left), channel_id=1, source_target_pairs={{1,0},{2,3},{5,4},{6,7},{9,8},{10,11},{13,12},{14,15},{17,16},{18,... | collective-permute-start | bytes 2359304 | tf_op jit(solution)/shard_map/ppermute | solution.py:38
  208.0 15.7 %collective-permute-start.30 = (bf16[384,384]{1,0:T(8,128)(2,1)S(1)}, bf16[384,384]{1,0:T(8,128)(2,1)S(1)}, u32[]{:S(2)}, u32[]{:S(2)}) collective-permute-start(bf16[384,384]{1,0:T(8,128)(2,1)S(1)} %fusion), channel_id=1, source_target_pairs={{0,8},{4,12},{8,0},{12,4},{1,9},{5,13},{9,1},{13,5},{2,10},{6,14},... | collective-permute-start | bytes 884744 | tf_op jit(solution)/shard_map/ppermute | solution.py:38
  (21 other events, 188.6 us)

commit v5 on v4

--- a/solution.py
+++ b/solution.py
@@ -138,8 +138,9 @@
     )(place, energy, eps_rows, eps_cols, left, right)
 
 
-def mix_kernel(half, band, rows, cols, straight_core, place, *refs):
-    own, *other, mix, dens, amp_t, amp, sems = refs
+def mix_kernel(owned, half, band, rows, cols, straight_core, place, *refs):
+    *pieces, mix, dens, amp_t, amp, sems = refs
+    own, other = pieces[:owned], pieces[owned:]
     core, slab, chip = place[0], place[1], place[2]
     nvirt = 2 * half
     step = pl.program_id(0)
@@ -147,11 +148,12 @@
     @pl.when(step == 0)
     def _():
         copies = []
-        for i, piece in enumerate((own, *other)):
-            width = piece.shape[0]
-            start = core * half if i == 0 else (1 - core) * half + (i - 1) * width
-            rows_at = pl.ds(pl.multiple_of(start, 128), width)
-            copies.append(pltpu.make_async_copy(piece, amp_t.at[rows_at, :], sems.at[i]))
+        for side, group in ((core, own), (1 - core, other)):
+            start = side * half
+            for piece in group:
+                rows_at = pl.ds(pl.multiple_of(start, 128), piece.shape[0])
+                copies.append(pltpu.make_async_copy(piece, amp_t.at[rows_at, :], sems.at[len(copies)]))
+                start += piece.shape[0]
         for copy in copies:
             copy.start()
         for copy in copies:
@@ -178,15 +180,15 @@
 
 
 def mix(place, own, other, straight_core, slabs, count):
-    nvirt = own.shape[1]
+    nvirt = own[0].shape[1]
     rows, cols, chips = nvirt // slabs, nvirt // count, count // 2
     band = 256
     return pl.pallas_call(
-        functools.partial(mix_kernel, nvirt // 2, band, rows, cols, straight_core),
+        functools.partial(mix_kernel, len(own), nvirt // 2, band, rows, cols, straight_core),
         grid_spec=pltpu.PrefetchScalarGridSpec(
             num_scalar_prefetch=1,
             grid=(nvirt // band,),
-            in_specs=[pl.BlockSpec(memory_space=pl.ANY)] * (1 + len(other)),
+            in_specs=[pl.BlockSpec(memory_space=pl.ANY)] * (len(own) + len(other)),
             out_specs=[
                 pl.BlockSpec((band, nvirt), lambda i, p: (i, 0)),
                 pl.BlockSpec((chips, rows, cols), lambda i, p: (0, 0, 0)),
@@ -194,7 +196,7 @@
             scratch_shapes=[
                 pltpu.VMEM((nvirt, nvirt), BF16),
                 pltpu.VMEM((nvirt, nvirt), BF16),
-                pltpu.SemaphoreType.DMA((1 + len(other),)),
+                pltpu.SemaphoreType.DMA((len(own) + len(other),)),
             ],
         ),
         out_shape=[
@@ -204,7 +206,7 @@
         compiler_params=pltpu.CompilerParams(vmem_limit_bytes=LIMIT),
         cost_estimate=TINY,
         name="mix",
-    )(place, own, *other)
+    )(place, *own, *other)
 
 
 def block_of(rows):
@@ -264,20 +266,21 @@
 def final_columns(place, partner, weight, kept, arrived, start, step, gamma=None):
     rows, nvirt = partner.shape
     block = block_of(rows)
+    part = nvirt // 3
     before = [] if gamma is None else [gamma]
     return pl.pallas_call(
         final_kernel,
         grid_spec=pltpu.PrefetchScalarGridSpec(
             num_scalar_prefetch=1,
-            grid=(rows // block,),
+            grid=(step // part, rows // block),
             in_specs=[
-                pl.BlockSpec((block, nvirt), lambda i, p: (i, 0)),
-                pl.BlockSpec((nvirt, step), lambda i, p: (0, start // step)),
-                pl.BlockSpec((block, step), lambda i, p: (jnp.where(p[0] == 0, i, 0), 0)),
-                pl.BlockSpec((block, step), lambda i, p: (jnp.where(p[0] == 0, 0, i), 0)),
+                pl.BlockSpec((block, nvirt), lambda j, i, p: (i, 0)),
+                pl.BlockSpec((nvirt, part), lambda j, i, p: (0, start // part + j)),
+                pl.BlockSpec((block, part), lambda j, i, p: (jnp.where(p[0] == 0, i, 0), jnp.where(p[0] == 0, j, 0))),
+                pl.BlockSpec((block, part), lambda j, i, p: (jnp.where(p[0] == 0, 0, i), jnp.where(p[0] == 0, 0, j))),
             ]
             + [pl.BlockSpec(memory_space=pl.ANY)] * len(before),
-            out_specs=pl.BlockSpec((1, block, step), lambda i, p: (0, i, start // step)),
+            out_specs=pl.BlockSpec((1, block, part), lambda j, i, p: (0, i, start // part + j)),
         ),
         out_shape=jax.ShapeDtypeStruct((1, rows, nvirt), BF16),
         input_output_aliases={5: 0} if before else {},
@@ -305,7 +308,7 @@
         out_specs=pl.BlockSpec((block, part), lambda j, i: (i, j)),
         out_shape=jax.ShapeDtypeStruct((rows, step), BF16),
         compiler_params=pltpu.CompilerParams(vmem_limit_bytes=LIMIT),
-        cost_estimate=TINY,
+        cost_estimate=pl.CostEstimate(flops=5760000000, bytes_accessed=10**4, transcendentals=0),
         name="local_rest",
     )(partner, weight)
 
@@ -448,15 +451,20 @@
     def collect(s):
         if 0 <= s < n:
             kind, j = jobs[s]
-            own[kind] = [
-                order.step(
-                    lambda a, b, *c: picked(where, a, b, 0, slabs, j * width, half, c), amp[s], outward[s], *own[kind]
-                )
-            ]
+            together = kind == "cross"
+            start, rows = (j * width, half) if together else (0, width)
+            before = own[kind] if together else []
+            full = order.step(
+                lambda a, b, *c: picked(where, a, b, 0, slabs, start, rows, c), amp[s], outward[s], *before
+            )
+            own[kind] = [full] if together else own[kind] + [full]
             left[kind] -= 1
 
+    def swapped(value):
+        return order.send(value, "occ", swap_pairs)
+
     third = nvirt // 3
-    spans = [(0, third), (third, 2 * third)]
+    spans = [(0, 2 * third), (2 * third, third)]
     kept, arrived = [], []
 
     def cross_term():
@@ -470,7 +478,7 @@
             )
             arrived.append(order.send(kept[j], "occ", back_pairs))
 
-    cross_mix = []
+    cross_mix, other = [], []
     for s in range(-1, n + 2):
         if s + 1 < n:
             feed(s + 1)
@@ -479,28 +487,23 @@
             pass_out(s - 1)
             collect(s - 2)
         else:
-            if s == n + 1:
-                settle(arrived[0])
             collect(s - 2)
             pass_out(s - 1)
-            cross_term()
         if not left["cross"] and not cross_mix:
-            other = order.send(own["cross"][0], "occ", swap_pairs)
+            cross_other = swapped(own["cross"][0])
             received = order.step(lambda *v: jnp.concatenate(v, axis=1), *incoming.values())
             upper = order.send(received, "occ", down_pairs)
             cross_mix = order.step(
-                lambda a, b: mix(where, a, (b,), 0, slabs, count), own["cross"][0], other
+                lambda a, b: mix(where, (a,), (b,), 0, slabs, count), own["cross"][0], cross_other
             )
             cross_term()
+        elif s >= n:
+            other += [swapped(v) for v in own["local"][len(other):]]
     while len(kept) < len(spans):
         cross_term()
 
-    other = [
-        order.send(lax.slice_in_dim(own["local"][0], j * width, (j + 1) * width), "occ", swap_pairs)
-        for j in range(PIECES)
-    ]
     weight, dens = order.step(
-        lambda a, *b: mix(where, a, b, 1, slabs, count), own["local"][0], *other
+        lambda *v: mix(where, v[:PIECES], v[PIECES:], 1, slabs, count), *own["local"], *other
     )
     total = order.step(lambda a, b: (a + b) * nvirt ** (-0.5), cross_mix[1], dens)
     density = total[0]

time: 226 us -> 224 us (level)
    pallas_call x1, Pallas kernels: 4.58 us -> 8.17 us  [final_columns(): pl.pallas_call(final_kernel, grid_spec=pltpu.PrefetchScalarGridSpec(num_s...]
    pallas_call x1, Pallas kernels: 5.99 us -> 2.88 us  [local_columns(): pl.pallas_call(local_kernel, grid=(step // part, rows // block), in_specs...]
  transfers between devices with their start and end apart: 31 -> 31, of which waited for: 18 -> 17; matrix products, arithmetic and copies ran while one was open for 3% -> 3% of each run, Pallas kernels for 30% -> 30%
where the time goes in v5:
time: 224 us; the launch traced here: 223 us
  waiting for transfers between devices  74 us (33%)
  Pallas kernels  66.8 us (30%)
  starting transfers between devices  65.1 us (29%)
  local copies, waits for them, and re-layouts  8 us (4%)
  other arithmetic  7.38 us (3%)
    ppermute x31, waiting for transfers between devices, send(): return lax.ppermute(self.ready(value, *others)[0], axis, pairs)  74 us
    ppermute x31, starting transfers between devices, send(): return lax.ppermute(self.ready(value, *others)[0], axis, pairs)  65.1 us
    pallas_call x6, Pallas kernels, product_rows(): pl.pallas_call(product_kernel, grid_spec=pltpu.PrefetchScalarGridSpec(num...  16.6 us
    pallas_call x6, Pallas kernels, amplitude(): pl.pallas_call(amp_kernel, grid_spec=pltpu.PrefetchScalarGridSpec(num_sca...  10.2 us
    pallas_call x2, Pallas kernels, cross_columns(): pl.pallas_call(cross_kernel, grid_spec=pltpu.PrefetchScalarGridSpec(num_s...  10.2 us
    pallas_call x2, Pallas kernels, mix(): pl.pallas_call(functools.partial(mix_kernel, len(own), nvirt // 2, band,...  9.58 us
    pallas_call x1, Pallas kernels, final_columns(): pl.pallas_call(final_kernel, grid_spec=pltpu.PrefetchScalarGridSpec(num_s...  8.17 us
    unnamed x30, local copies, waits for them, and re-layouts  4.76 us
  transfers between devices with their start and end apart: 31, of which 17 were waited for; matrix products, arithmetic and copies ran while one was open for 3% of the time, Pallas kernels for 30%

profile of v5, /device:TPU:1, one launch (start us, length us, event | category | flops | bytes accessed | tf_op | source)
XLA Modules:
  0.0 222.7 jit_solution(14163026907645529036)
XLA Ops:
  11.2 5.1 %collective-permute-done.1.partner = bf16[1536,1536]{1,0:T(8,128)(2,1)S(1)} collective-permute-done((bf16[1536,1536]{1,0:T(8,128)(2,1)}, bf16[1536,1536]{1,0:T(8,128)(2,1)S(1)}, u32[]{:S(2)}, u32[]{:S(2)}) %collective-permute-start.1) | collective-permute-done | bytes 4718624 | tf_op jit(solution)/shard_map/ppermute | solution.py:38
  23.7 4.7 %collective-permute-start.2 = (bf16[256,1536]{1,0:T(8,128)(2,1)S(1)}, bf16[256,1536]{1,0:T(8,128)(2,1)S(1)}, u32[]{:S(2)}, u32[]{:S(2)}) collective-permute-start(bf16[256,1536]{1,0:T(8,128)(2,1)S(1)} %slab_product.6.left), channel_id=1, source_target_pairs={{0,1},{3,2},{4,5},{7,6},{8,9},{11,10},{12,13},{15,14},{16,17},{19,... | collective-permute-start | bytes 2359304 | tf_op jit(solution)/shard_map/ppermute | solution.py:38
  34.1 4.2 %collective-permute-start.5 = (bf16[256,1536]{1,0:T(8,128)(2,1)S(1)}, bf16[256,1536]{1,0:T(8,128)(2,1)}, u32[]{:S(2)}, u32[]{:S(2)}) collective-permute-start(bf16[256,1536]{1,0:T(8,128)(2,1)S(1)} %slab_product.7.left), channel_id=1, source_target_pairs={{0,1},{3,2},{4,5},{7,6},{8,9},{11,10},{12,13},{15,14},{16,17},{19,... | collective-permute-start | bytes 2359304 | tf_op jit(solution)/shard_map/ppermute | solution.py:38
  38.3 4.1 %collective-permute-done.2.right = bf16[256,1536]{1,0:T(8,128)(2,1)S(1)} collective-permute-done((bf16[256,1536]{1,0:T(8,128)(2,1)S(1)}, bf16[256,1536]{1,0:T(8,128)(2,1)S(1)}, u32[]{:S(2)}, u32[]{:S(2)}) %collective-permute-start.2) | collective-permute-done | bytes 786464 | tf_op jit(solution)/shard_map/ppermute | solution.py:38
  53.8 5.5 %collective-permute-done.5.right = bf16[256,1536]{1,0:T(8,128)(2,1)} collective-permute-done((bf16[256,1536]{1,0:T(8,128)(2,1)S(1)}, bf16[256,1536]{1,0:T(8,128)(2,1)}, u32[]{:S(2)}, u32[]{:S(2)}) %collective-permute-start.5) | collective-permute-done | bytes 786464 | tf_op jit(solution)/shard_map/ppermute | solution.py:38
  59.3 4.2 %collective-permute-start.9 = (bf16[256,1536]{1,0:T(8,128)(2,1)S(1)}, bf16[256,1536]{1,0:T(8,128)(2,1)S(1)}, u32[]{:S(2)}, u32[]{:S(2)}) collective-permute-start(bf16[256,1536]{1,0:T(8,128)(2,1)S(1)} %slab_product.8.left), channel_id=1, source_target_pairs={{0,1},{3,2},{4,5},{7,6},{8,9},{11,10},{12,13},{15,14},{16,17},{19,... | collective-permute-start | bytes 2359304 | tf_op jit(solution)/shard_map/ppermute | solution.py:38
  72.4 4.1 %collective-permute-start.14 = (bf16[256,1536]{1,0:T(8,128)(2,1)S(1)}, bf16[256,1536]{1,0:T(8,128)(2,1)S(1)}, u32[]{:S(2)}, u32[]{:S(2)}) collective-permute-start(bf16[256,1536]{1,0:T(8,128)(2,1)S(1)} %slab_product.9.left), channel_id=1, source_target_pairs={{0,1},{3,2},{4,5},{7,6},{8,9},{11,10},{12,13},{15,14},{16,17},{19,... | collective-permute-start | bytes 2359304 | tf_op jit(solution)/shard_map/ppermute | solution.py:38
  81.7 3.7 %collective-permute-done.7.right = bf16[256,1536]{1,0:T(8,128)(2,1)S(1)} collective-permute-done((bf16[256,1536]{1,0:T(8,128)(2,1)S(1)}, bf16[256,1536]{1,0:T(8,128)(2,1)S(1)}, u32[]{:S(2)}, u32[]{:S(2)}) %collective-permute-start.7) | collective-permute-done | bytes 786464 | tf_op jit(solution)/shard_map/ppermute | solution.py:38
  88.8 5.1 %collective-permute-done.14.right = bf16[256,1536]{1,0:T(8,128)(2,1)S(1)} collective-permute-done((bf16[256,1536]{1,0:T(8,128)(2,1)S(1)}, bf16[256,1536]{1,0:T(8,128)(2,1)S(1)}, u32[]{:S(2)}, u32[]{:S(2)}) %collective-permute-start.14) | collective-permute-done | bytes 786464 | tf_op jit(solution)/shard_map/ppermute | solution.py:38
  93.9 4.1 %collective-permute-start.11 = (bf16[256,1536]{1,0:T(8,128)(2,1)S(1)}, bf16[256,1536]{1,0:T(8,128)(2,1)S(1)}, u32[]{:S(2)}, u32[]{:S(2)}) collective-permute-start(bf16[256,1536]{1,0:T(8,128)(2,1)S(1)} %slab_product.10.left), channel_id=1, source_target_pairs={{0,1},{3,2},{4,5},{7,6},{8,9},{11,10},{12,13},{15,14},{16,17},{19,... | collective-permute-start | bytes 2359304 | tf_op jit(solution)/shard_map/ppermute | solution.py:38
  105.9 4.1 %collective-permute-start.16 = (bf16[256,1536]{1,0:T(8,128)(2,1)S(1)}, bf16[256,1536]{1,0:T(8,128)(2,1)S(1)}, u32[]{:S(2)}, u32[]{:S(2)}) collective-permute-start(bf16[256,1536]{1,0:T(8,128)(2,1)S(1)} %slab_product.11.left), channel_id=1, source_target_pairs={{0,1},{3,2},{4,5},{7,6},{8,9},{11,10},{12,13},{15,14},{16,17},{19,... | collective-permute-start | bytes 2359304 | tf_op jit(solution)/shard_map/ppermute | solution.py:38
  118.0 9.5 %collective-permute-done.16.right = bf16[256,1536]{1,0:T(8,128)(2,1)S(1)} collective-permute-done((bf16[256,1536]{1,0:T(8,128)(2,1)S(1)}, bf16[256,1536]{1,0:T(8,128)(2,1)S(1)}, u32[]{:S(2)}, u32[]{:S(2)}) %collective-permute-start.16) | collective-permute-done | bytes 786464 | tf_op jit(solution)/shard_map/ppermute | solution.py:38
  129.2 5.0 %collective-permute-done.20.right = bf16[256,1536]{1,0:T(8,128)(2,1)S(1)} collective-permute-done((bf16[256,1536]{1,0:T(8,128)(2,1)S(1)}, bf16[256,1536]{1,0:T(8,128)(2,1)S(1)}, u32[]{:S(2)}, u32[]{:S(2)}) %collective-permute-start.20) | collective-permute-done | bytes 786464 | tf_op jit(solution)/shard_map/ppermute | solution.py:38
  134.9 6.6 %collective-permute-start.21 = (bf16[768,1536]{1,0:T(8,128)(2,1)S(1)}, bf16[768,1536]{1,0:T(8,128)(2,1)S(1)}, u32[]{:S(2)}, u32[]{:S(2)}) collective-permute-start(bf16[768,1536]{1,0:T(8,128)(2,1)S(1)} %amp_of_slab.9.refs_0_), channel_id=1, source_target_pairs={{0,4},{4,0},{8,12},{12,8},{1,5},{5,1},{9,13},{13,9},{2,6},{6,2},{1... | collective-permute-start | bytes 7077896 | tf_op jit(solution)/shard_map/ppermute | solution.py:38
  145.9 4.8 %mix.2 = (bf16[1536,1536]{1,0:T(8,128)(2,1)S(1)}, f32[2,384,384]{2,1,0:T(8,128)S(1)}) custom-call(s32[3]{0:T(128)S(1)} %pad_add_fusion.place, bf16[768,1536]{1,0:T(8,128)(2,1)S(1)} %amp_of_slab.9.refs_0_, bf16[768,1536]{1,0:T(8,128)(2,1)S(1)} %collective-permute-done.21.refs_1_), custom_call_target="tpu_custom_call" | custom-call | flops 10000000 | bytes 10000 | tf_op jit(solution)/shard_map/mix/pallas_call | solution.py:186
  150.7 6.7 %cross_term.2.kept = bf16[1536,1024]{1,0:T(8,128)(2,1)S(1)} custom-call(s32[3]{0:T(128)S(1)} %pad_add_fusion.place, bf16[1536,768]{1,0:T(8,128)(2,1)S(1)} %constant_dynamic-update-slice_fusion.lower, bf16[1536,768]{1,0:T(8,128)(2,1)S(1)} %collective-permute-done.22.upper, bf16[1536,1536]{1,0:T(8,128)(2,1)S(1)} %bitcast.11, ...), custom_call_target="tpu_custom_call" | custom-call | flops 10000000 | bytes 10000 | tf_op jit(solution)/shard_map/cross_term/pallas_call | solution.py:233
  157.4 3.1 %collective-permute-start.28 = (bf16[1536,1024]{1,0:T(8,128)(2,1)S(1)}, bf16[1536,1024]{1,0:T(8,128)(2,1)S(1)}, u32[]{:S(2)}, u32[]{:S(2)}) collective-permute-start(bf16[1536,1024]{1,0:T(8,128)(2,1)S(1)} %cross_term.2.kept), channel_id=1, source_target_pairs={{4,12},{12,4},{5,13},{13,5},{6,14},{14,6},{7,15},{15,7},{20,28},{2... | collective-permute-start | bytes 9437192 | tf_op jit(solution)/shard_map/ppermute | solution.py:38
  160.5 4.2 %collective-permute-done.19.right = bf16[256,1536]{1,0:T(8,128)(2,1)S(1)} collective-permute-done((bf16[256,1536]{1,0:T(8,128)(2,1)S(1)}, bf16[256,1536]{1,0:T(8,128)(2,1)S(1)}, u32[]{:S(2)}, u32[]{:S(2)}) %collective-permute-start.19) | collective-permute-done | bytes 786464 | tf_op jit(solution)/shard_map/ppermute | solution.py:38
  168.7 20.5 %collective-permute-done.24.right = bf16[256,1536]{1,0:T(8,128)(2,1)S(1)} collective-permute-done((bf16[256,1536]{1,0:T(8,128)(2,1)S(1)}, bf16[256,1536]{1,0:T(8,128)(2,1)S(1)}, u32[]{:S(2)}, u32[]{:S(2)}) %collective-permute-start.24) | collective-permute-done | bytes 786464 | tf_op jit(solution)/shard_map/ppermute | solution.py:38
  190.8 3.5 %cross_term.3.kept = bf16[1536,512]{1,0:T(8,128)(2,1)S(1)} custom-call(s32[3]{0:T(128)S(1)} %pad_add_fusion.place, bf16[1536,768]{1,0:T(8,128)(2,1)S(1)} %constant_dynamic-update-slice_fusion.lower, bf16[1536,768]{1,0:T(8,128)(2,1)S(1)} %collective-permute-done.22.upper, bf16[1536,1536]{1,0:T(8,128)(2,1)S(1)} %bitcast.11, ...), custom_call_target="tpu_custom_call" | custom-call | flops 10000000 | bytes 10000 | tf_op jit(solution)/shard_map/cross_term/pallas_call | solution.py:233
  194.3 3.3 %collective-permute-start.29 = (bf16[1536,512]{1,0:T(8,128)(2,1)S(1)}, bf16[1536,512]{1,0:T(8,128)(2,1)S(1)}, u32[]{:S(2)}, u32[]{:S(2)}) collective-permute-start(bf16[1536,512]{1,0:T(8,128)(2,1)S(1)} %cross_term.3.kept), channel_id=1, source_target_pairs={{4,12},{12,4},{5,13},{13,5},{6,14},{14,6},{7,15},{15,7},{20,28},{2... | collective-permute-start | bytes 4718600 | tf_op jit(solution)/shard_map/ppermute | solution.py:38
  197.7 4.8 %mix.3 = (bf16[1536,1536]{1,0:T(8,128)(2,1)S(1)}, f32[2,384,384]{2,1,0:T(8,128)S(1)}) custom-call(s32[3]{0:T(128)S(1)} %pad_add_fusion.place, bf16[256,1536]{1,0:T(8,128)(2,1)S(1)} %amp_of_slab.6.refs_0_, bf16[256,1536]{1,0:T(8,128)(2,1)S(1)} %amp_of_slab.10.refs_1_, bf16[256,1536]{1,0:T(8,128)(2,1)S(1)} %amp_of_slab.11.refs_2_, ...), custom_call_target="tpu_custom_call" | custom-call | flops 10000000 | bytes 10000 | tf_op jit(solution)/shard_map/mix/pallas_call | solution.py:186
  203.1 8.2 %local_term.1.gamma = bf16[1,1536,1536]{2,1,0:T(8,128)(2,1)} custom-call(s32[3]{0:T(128)S(1)} %pad_add_fusion.place, bf16[1536,1536]{1,0:T(8,128)(2,1)S(1)} %bitcast.11, bf16[1536,1536]{1,0:T(8,128)(2,1)S(1)} %get-tuple-element.249.weight, bf16[1536,1024]{1,0:T(8,128)(2,1)S(1)} %cross_term.2.kept, bf16[1536,1024]{1,0:T(8,128)(2,1)S(1)} %collective-permute-done.28.arrived), custom_call_target="tpu_custom_call" | custom-call | flops 10000000 | bytes 10000 | tf_op jit(solution)/shard_map/local_term/pallas_call | solution.py:271
  214.2 4.4 %collective-permute-done.29.arrived = bf16[1536,512]{1,0:T(8,128)(2,1)S(1)} collective-permute-done((bf16[1536,512]{1,0:T(8,128)(2,1)S(1)}, bf16[1536,512]{1,0:T(8,128)(2,1)S(1)}, u32[]{:S(2)}, u32[]{:S(2)}) %collective-permute-start.29) | collective-permute-done | bytes 1572896 | tf_op jit(solution)/shard_map/ppermute | solution.py:38
  (121 shorter events, 87.9 us)
Async XLA Ops:
  8.5 20.5 %collective-permute-start.3 = (bf16[1536,256]{1,0:T(8,128)(2,1)S(1)}, bf16[1536,256]{1,0:T(8,128)(2,1)S(1)}, u32[]{:S(2)}, u32[]{:S(2)}) collective-permute-start(bf16[1536,256]{1,0:T(8,128)(2,1)S(1)} %broadcast_select_fusion.4), channel_id=1, source_target_pairs={{0,8},{4,12},{8,0},{12,4},{1,9},{5,13},{9,1},{13,5},{2,10},{6,14},... | collective-permute-start | bytes 2359304 | tf_op jit(solution)/shard_map/ppermute | solution.py:38
  23.7 18.7 %collective-permute-start.2 = (bf16[256,1536]{1,0:T(8,128)(2,1)S(1)}, bf16[256,1536]{1,0:T(8,128)(2,1)S(1)}, u32[]{:S(2)}, u32[]{:S(2)}) collective-permute-start(bf16[256,1536]{1,0:T(8,128)(2,1)S(1)} %slab_product.6.left), channel_id=1, source_target_pairs={{0,1},{3,2},{4,5},{7,6},{8,9},{11,10},{12,13},{15,14},{16,17},{19,... | collective-permute-start | bytes 2359304 | tf_op jit(solution)/shard_map/ppermute | solution.py:38
  31.8 16.9 %collective-permute-start.6 = (bf16[1536,256]{1,0:T(8,128)(2,1)}, bf16[1536,256]{1,0:T(8,128)(2,1)S(1)}, u32[]{:S(2)}, u32[]{:S(2)}) collective-permute-start(bf16[1536,256]{1,0:T(8,128)(2,1)} %broadcast_select_fusion.3), channel_id=1, source_target_pairs={{0,8},{4,12},{8,0},{12,4},{1,9},{5,13},{9,1},{13,5},{2,10},{6,14},... | collective-permute-start | bytes 2359304 | tf_op jit(solution)/shard_map/ppermute | solution.py:38
  34.1 25.1 %collective-permute-start.5 = (bf16[256,1536]{1,0:T(8,128)(2,1)S(1)}, bf16[256,1536]{1,0:T(8,128)(2,1)}, u32[]{:S(2)}, u32[]{:S(2)}) collective-permute-start(bf16[256,1536]{1,0:T(8,128)(2,1)S(1)} %slab_product.7.left), channel_id=1, source_target_pairs={{0,1},{3,2},{4,5},{7,6},{8,9},{11,10},{12,13},{15,14},{16,17},{19,... | collective-permute-start | bytes 2359304 | tf_op jit(solution)/shard_map/ppermute | solution.py:38
  43.5 22.4 %collective-permute-start.4 = (bf16[256,1536]{1,0:T(8,128)(2,1)}, bf16[256,1536]{1,0:T(8,128)(2,1)}, u32[]{:S(2)}, u32[]{:S(2)}) collective-permute-start(bf16[256,1536]{1,0:T(8,128)(2,1)} %half_sum.6.left), channel_id=1, source_target_pairs={{1,2},{2,1},{5,6},{6,5},{9,10},{10,9},{13,14},{14,13},{17,18},{18,... | collective-permute-start | bytes 2359304 | tf_op jit(solution)/shard_map/ppermute | solution.py:38
  45.1 24.5 %collective-permute-start.10 = (bf16[1536,256]{1,0:T(8,128)(2,1)}, bf16[1536,256]{1,0:T(8,128)(2,1)S(1)}, u32[]{:S(2)}, u32[]{:S(2)}) collective-permute-start(bf16[1536,256]{1,0:T(8,128)(2,1)} %broadcast_select_fusion.2), channel_id=1, source_target_pairs={{0,8},{4,12},{8,0},{12,4},{1,9},{5,13},{9,1},{13,5},{2,10},{6,14},... | collective-permute-start | bytes 2359304 | tf_op jit(solution)/shard_map/ppermute | solution.py:38
  59.3 18.6 %collective-permute-start.9 = (bf16[256,1536]{1,0:T(8,128)(2,1)S(1)}, bf16[256,1536]{1,0:T(8,128)(2,1)S(1)}, u32[]{:S(2)}, u32[]{:S(2)}) collective-permute-start(bf16[256,1536]{1,0:T(8,128)(2,1)S(1)} %slab_product.8.left), channel_id=1, source_target_pairs={{0,1},{3,2},{4,5},{7,6},{8,9},{11,10},{12,13},{15,14},{16,17},{19,... | collective-permute-start | bytes 2359304 | tf_op jit(solution)/shard_map/ppermute | solution.py:38
  68.3 17.0 %collective-permute-start.7 = (bf16[256,1536]{1,0:T(8,128)(2,1)S(1)}, bf16[256,1536]{1,0:T(8,128)(2,1)S(1)}, u32[]{:S(2)}, u32[]{:S(2)}) collective-permute-start(bf16[256,1536]{1,0:T(8,128)(2,1)S(1)} %amplitude.6.left), channel_id=1, source_target_pairs={{1,0},{2,3},{5,4},{6,7},{9,8},{10,11},{13,12},{14,15},{17,16},{18,... | collective-permute-start | bytes 2359304 | tf_op jit(solution)/shard_map/ppermute | solution.py:38
  72.4 21.4 %collective-permute-start.14 = (bf16[256,1536]{1,0:T(8,128)(2,1)S(1)}, bf16[256,1536]{1,0:T(8,128)(2,1)S(1)}, u32[]{:S(2)}, u32[]{:S(2)}) collective-permute-start(bf16[256,1536]{1,0:T(8,128)(2,1)S(1)} %slab_product.9.left), channel_id=1, source_target_pairs={{0,1},{3,2},{4,5},{7,6},{8,9},{11,10},{12,13},{15,14},{16,17},{19,... | collective-permute-start | bytes 2359304 | tf_op jit(solution)/shard_map/ppermute | solution.py:38
  78.1 20.9 %collective-permute-start.13 = (bf16[256,1536]{1,0:T(8,128)(2,1)S(1)}, bf16[256,1536]{1,0:T(8,128)(2,1)S(1)}, u32[]{:S(2)}, u32[]{:S(2)}) collective-permute-start(bf16[256,1536]{1,0:T(8,128)(2,1)S(1)} %half_sum.8.left), channel_id=1, source_target_pairs={{1,2},{2,1},{5,6},{6,5},{9,10},{10,9},{13,14},{14,13},{17,18},{18,... | collective-permute-start | bytes 2359304 | tf_op jit(solution)/shard_map/ppermute | solution.py:38
  80.4 20.8 %collective-permute-start.12 = (bf16[256,1536]{1,0:T(8,128)(2,1)S(1)}, bf16[256,1536]{1,0:T(8,128)(2,1)S(1)}, u32[]{:S(2)}, u32[]{:S(2)}) collective-permute-start(bf16[256,1536]{1,0:T(8,128)(2,1)S(1)} %amplitude.7.left), channel_id=1, source_target_pairs={{1,0},{2,3},{5,4},{6,7},{9,8},{10,11},{13,12},{14,15},{17,16},{18,... | collective-permute-start | bytes 2359304 | tf_op jit(solution)/shard_map/ppermute | solution.py:38
  93.9 16.7 %collective-permute-start.11 = (bf16[256,1536]{1,0:T(8,128)(2,1)S(1)}, bf16[256,1536]{1,0:T(8,128)(2,1)S(1)}, u32[]{:S(2)}, u32[]{:S(2)}) collective-permute-start(bf16[256,1536]{1,0:T(8,128)(2,1)S(1)} %slab_product.10.left), channel_id=1, source_target_pairs={{0,1},{3,2},{4,5},{7,6},{8,9},{11,10},{12,13},{15,14},{16,17},{19,... | collective-permute-start | bytes 2359304 | tf_op jit(solution)/shard_map/ppermute | solution.py:38
  101.8 15.4 %collective-permute-start.17 = (bf16[256,1536]{1,0:T(8,128)(2,1)S(1)}, bf16[256,1536]{1,0:T(8,128)(2,1)S(1)}, u32[]{:S(2)}, u32[]{:S(2)}) collective-permute-start(bf16[256,1536]{1,0:T(8,128)(2,1)S(1)} %amplitude.8.left), channel_id=1, source_target_pairs={{1,0},{2,3},{5,4},{6,7},{9,8},{10,11},{13,12},{14,15},{17,16},{18,... | collective-permute-start | bytes 2359304 | tf_op jit(solution)/shard_map/ppermute | solution.py:38
  105.9 21.5 %collective-permute-start.16 = (bf16[256,1536]{1,0:T(8,128)(2,1)S(1)}, bf16[256,1536]{1,0:T(8,128)(2,1)S(1)}, u32[]{:S(2)}, u32[]{:S(2)}) collective-permute-start(bf16[256,1536]{1,0:T(8,128)(2,1)S(1)} %slab_product.11.left), channel_id=1, source_target_pairs={{0,1},{3,2},{4,5},{7,6},{8,9},{11,10},{12,13},{15,14},{16,17},{19,... | collective-permute-start | bytes 2359304 | tf_op jit(solution)/shard_map/ppermute | solution.py:38
  110.8 16.8 %collective-permute-start.15 = (bf16[256,1536]{1,0:T(8,128)(2,1)S(1)}, bf16[256,1536]{1,0:T(8,128)(2,1)S(1)}, u32[]{:S(2)}, u32[]{:S(2)}) collective-permute-start(bf16[256,1536]{1,0:T(8,128)(2,1)S(1)} %half_sum.10.left), channel_id=1, source_target_pairs={{1,2},{2,1},{5,6},{6,5},{9,10},{10,9},{13,14},{14,13},{17,18},{18,... | collective-permute-start | bytes 2359304 | tf_op jit(solution)/shard_map/ppermute | solution.py:38
  113.1 21.2 %collective-permute-start.20 = (bf16[256,1536]{1,0:T(8,128)(2,1)S(1)}, bf16[256,1536]{1,0:T(8,128)(2,1)S(1)}, u32[]{:S(2)}, u32[]{:S(2)}) collective-permute-start(bf16[256,1536]{1,0:T(8,128)(2,1)S(1)} %amplitude.9.left), channel_id=1, source_target_pairs={{1,0},{2,3},{5,4},{6,7},{9,8},{10,11},{13,12},{14,15},{17,16},{18,... | collective-permute-start | bytes 2359304 | tf_op jit(solution)/shard_map/ppermute | solution.py:38
  143.8 20.9 %collective-permute-start.19 = (bf16[256,1536]{1,0:T(8,128)(2,1)S(1)}, bf16[256,1536]{1,0:T(8,128)(2,1)S(1)}, u32[]{:S(2)}, u32[]{:S(2)}) collective-permute-start(bf16[256,1536]{1,0:T(8,128)(2,1)S(1)} %amplitude.10.left), channel_id=1, source_target_pairs={{1,0},{2,3},{5,4},{6,7},{9,8},{10,11},{13,12},{14,15},{17,16},{18,... | collective-permute-start | bytes 2359304 | tf_op jit(solution)/shard_map/ppermute | solution.py:38
  145.1 20.2 %collective-permute-start.23 = (bf16[256,1536]{1,0:T(8,128)(2,1)S(1)}, bf16[256,1536]{1,0:T(8,128)(2,1)S(1)}, u32[]{:S(2)}, u32[]{:S(2)}) collective-permute-start(bf16[256,1536]{1,0:T(8,128)(2,1)S(1)} %half_sum.11.left), channel_id=1, source_target_pairs={{1,2},{2,1},{5,6},{6,5},{9,10},{10,9},{13,14},{14,13},{17,18},{18,... | collective-permute-start | bytes 2359304 | tf_op jit(solution)/shard_map/ppermute | solution.py:38
  157.4 45.8 %collective-permute-start.28 = (bf16[1536,1024]{1,0:T(8,128)(2,1)S(1)}, bf16[1536,1024]{1,0:T(8,128)(2,1)S(1)}, u32[]{:S(2)}, u32[]{:S(2)}) collective-permute-start(bf16[1536,1024]{1,0:T(8,128)(2,1)S(1)} %cross_term.2.kept), channel_id=1, source_target_pairs={{4,12},{12,4},{5,13},{13,5},{6,14},{14,6},{7,15},{15,7},{20,28},{2... | collective-permute-start | bytes 9437192 | tf_op jit(solution)/shard_map/ppermute | solution.py:38
  166.9 22.4 %collective-permute-start.24 = (bf16[256,1536]{1,0:T(8,128)(2,1)S(1)}, bf16[256,1536]{1,0:T(8,128)(2,1)S(1)}, u32[]{:S(2)}, u32[]{:S(2)}) collective-permute-start(bf16[256,1536]{1,0:T(8,128)(2,1)S(1)} %amplitude.11.left), channel_id=1, source_target_pairs={{1,0},{2,3},{5,4},{6,7},{9,8},{10,11},{13,12},{14,15},{17,16},{18,... | collective-permute-start | bytes 2359304 | tf_op jit(solution)/shard_map/ppermute | solution.py:38
  168.2 29.5 %collective-permute-start.26 = (bf16[256,1536]{1,0:T(8,128)(2,1)S(1)}, bf16[256,1536]{1,0:T(8,128)(2,1)S(1)}, u32[]{:S(2)}, u32[]{:S(2)}) collective-permute-start(bf16[256,1536]{1,0:T(8,128)(2,1)S(1)} %amp_of_slab.10.refs_1_), channel_id=1, source_target_pairs={{0,4},{4,0},{8,12},{12,8},{1,5},{5,1},{9,13},{13,9},{2,6},{6,2},{1... | collective-permute-start | bytes 2359304 | tf_op jit(solution)/shard_map/ppermute | solution.py:38
  168.6 29.1 %collective-permute-start.25 = (bf16[256,1536]{1,0:T(8,128)(2,1)S(1)}, bf16[256,1536]{1,0:T(8,128)(2,1)S(1)}, u32[]{:S(2)}, u32[]{:S(2)}) collective-permute-start(bf16[256,1536]{1,0:T(8,128)(2,1)S(1)} %amp_of_slab.6.refs_0_), channel_id=1, source_target_pairs={{0,4},{4,0},{8,12},{12,8},{1,5},{5,1},{9,13},{13,9},{2,6},{6,2},{1... | collective-permute-start | bytes 2359304 | tf_op jit(solution)/shard_map/ppermute | solution.py:38
  194.3 24.3 %collective-permute-start.29 = (bf16[1536,512]{1,0:T(8,128)(2,1)S(1)}, bf16[1536,512]{1,0:T(8,128)(2,1)S(1)}, u32[]{:S(2)}, u32[]{:S(2)}) collective-permute-start(bf16[1536,512]{1,0:T(8,128)(2,1)S(1)} %cross_term.3.kept), channel_id=1, source_target_pairs={{4,12},{12,4},{5,13},{13,5},{6,14},{14,6},{7,15},{15,7},{20,28},{2... | collective-permute-start | bytes 4718600 | tf_op jit(solution)/shard_map/ppermute | solution.py:38
  202.8 19.0 %collective-permute-start.30 = (bf16[384,384]{1,0:T(8,128)(2,1)S(1)}, bf16[384,384]{1,0:T(8,128)(2,1)S(1)}, u32[]{:S(2)}, u32[]{:S(2)}) collective-permute-start(bf16[384,384]{1,0:T(8,128)(2,1)S(1)} %fusion), channel_id=1, source_target_pairs={{0,8},{4,12},{8,0},{12,4},{1,9},{5,13},{9,1},{13,5},{2,10},{6,14},... | collective-permute-start | bytes 884744 | tf_op jit(solution)/shard_map/ppermute | solution.py:38
  (21 other events, 219.9 us)

commit v6 on v5

--- a/solution.py
+++ b/solution.py
@@ -61,7 +61,7 @@
         ),
         out_shape=jax.ShapeDtypeStruct((width, nvirt), BF16),
         compiler_params=pltpu.CompilerParams(vmem_limit_bytes=LIMIT),
-        cost_estimate=LIGHT,
+        cost_estimate=pl.CostEstimate(flops=300000000, bytes_accessed=10**4, transcendentals=0),
         name="slab_product",
     )(place, left, right)
 
@@ -75,7 +75,7 @@
         add_kernel,
         out_shape=jax.ShapeDtypeStruct(left.shape, BF16),
         compiler_params=pltpu.CompilerParams(vmem_limit_bytes=LIMIT),
-        cost_estimate=LIGHT,
+        cost_estimate=pl.CostEstimate(flops=2000000000, bytes_accessed=10**4, transcendentals=0),
         name="half_sum",
     )(left, right)
 
@@ -105,7 +105,7 @@
         out_shape=jax.ShapeDtypeStruct((rows, nvirt), BF16),
         input_output_aliases={3: 0} if before else {},
         compiler_params=pltpu.CompilerParams(vmem_limit_bytes=LIMIT),
-        cost_estimate=LIGHT,
+        cost_estimate=pl.CostEstimate(flops=10000000, bytes_accessed=10**4, transcendentals=0),
         name="amp_of_slab",
     )(place, left, right, *before)
 
@@ -133,7 +133,7 @@
         ),
         out_shape=jax.ShapeDtypeStruct(left.shape, BF16),
         compiler_params=pltpu.CompilerParams(vmem_limit_bytes=LIMIT),
-        cost_estimate=LIGHT,
+        cost_estimate=pl.CostEstimate(flops=1000000000, bytes_accessed=10**4, transcendentals=0),
         name="amplitude",
     )(place, energy, eps_rows, eps_cols, left, right)
 
@@ -204,7 +204,7 @@
             jax.ShapeDtypeStruct((chips, rows, cols), F32),
         ],
         compiler_params=pltpu.CompilerParams(vmem_limit_bytes=LIMIT),
-        cost_estimate=TINY,
+        cost_estimate=pl.CostEstimate(flops=10000000, bytes_accessed=10**4, transcendentals=0),
         name="mix",
     )(place, *own, *other)
 
@@ -245,7 +245,7 @@
         ),
         out_shape=jax.ShapeDtypeStruct((rows, step), BF16),
         compiler_params=pltpu.CompilerParams(vmem_limit_bytes=LIMIT),
-        cost_estimate=TINY,
+        cost_estimate=pl.CostEstimate(flops=4000000000, bytes_accessed=10**4, transcendentals=0),
         name="cross_term",
     )(place, lower, upper, partner, weight)
 
@@ -285,7 +285,7 @@
         out_shape=jax.ShapeDtypeStruct((1, rows, nvirt), BF16),
         input_output_aliases={5: 0} if before else {},
         compiler_params=pltpu.CompilerParams(vmem_limit_bytes=LIMIT),
-        cost_estimate=TINY,
+        cost_estimate=pl.CostEstimate(flops=4000000000, bytes_accessed=10**4, transcendentals=0),
         name="local_term",
     )(place, partner, weight, kept, arrived, *before)
 
@@ -476,7 +476,8 @@
                     cross_mix[0], partner, received, upper,
                 )
             )
-            arrived.append(order.send(kept[j], "occ", back_pairs))
+            if j == 0:
+                arrived.append(order.send(kept[j], "occ", back_pairs))
 
     cross_mix, other = [], []
     for s in range(-1, n + 2):
@@ -487,6 +488,8 @@
             pass_out(s - 1)
             collect(s - 2)
         else:
+            if s == n + 1:
+                cross_term()
             collect(s - 2)
             pass_out(s - 1)
         if not left["cross"] and not cross_mix:
@@ -499,8 +502,7 @@
             cross_term()
         elif s >= n:
             other += [swapped(v) for v in own["local"][len(other):]]
-    while len(kept) < len(spans):
-        cross_term()
+    arrived.append(order.send(kept[1], "occ", back_pairs))
 
     weight, dens = order.step(
         lambda *v: mix(where, v[:PIECES], v[PIECES:], 1, slabs, count), *own["local"], *other

time: 224 us -> 219 us (0.978)
  waiting for transfers between devices: 74 us -> 64.6 us
  starting transfers between devices: 65.1 us -> 69.5 us
    ppermute x31, waiting for transfers between devices: 74 us -> 64.6 us  [send(): return lax.ppermute(self.ready(value, *others)[0], axis, pairs)]
    ppermute x31, starting transfers between devices: 65.1 us -> 69.5 us  [send(): return lax.ppermute(self.ready(value, *others)[0], axis, pairs)]
  transfers between devices with their start and end apart: 31 -> 31, of which waited for: 17 -> 14; matrix products, arithmetic and copies ran while one was open for 3% -> 4% of each run, Pallas kernels for 30% -> 30%
where the time goes in v6:
time: 219 us; the launch traced here: 218 us
  starting transfers between devices  69.5 us (32%)
  Pallas kernels  66.8 us (31%)
  waiting for transfers between devices  64.6 us (29%)
  local copies, waits for them, and re-layouts  8.01 us (4%)
  other arithmetic  7.7 us (4%)
    ppermute x31, starting transfers between devices, send(): return lax.ppermute(self.ready(value, *others)[0], axis, pairs)  69.5 us
    ppermute x31, waiting for transfers between devices, send(): return lax.ppermute(self.ready(value, *others)[0], axis, pairs)  64.6 us
    pallas_call x6, Pallas kernels, product_rows(): pl.pallas_call(product_kernel, grid_spec=pltpu.PrefetchScalarGridSpec(num...  16.6 us
    pallas_call x6, Pallas kernels, amplitude(): pl.pallas_call(amp_kernel, grid_spec=pltpu.PrefetchScalarGridSpec(num_sca...  10.2 us
    pallas_call x2, Pallas kernels, cross_columns(): pl.pallas_call(cross_kernel, grid_spec=pltpu.PrefetchScalarGridSpec(num_s...  10.2 us
    pallas_call x2, Pallas kernels, mix(): pl.pallas_call(functools.partial(mix_kernel, len(own), nvirt // 2, band,...  9.58 us
    pallas_call x1, Pallas kernels, final_columns(): pl.pallas_call(final_kernel, grid_spec=pltpu.PrefetchScalarGridSpec(num_s...  8.18 us
    unnamed x30, local copies, waits for them, and re-layouts  4.77 us
  transfers between devices with their start and end apart: 31, of which 14 were waited for; matrix products, arithmetic and copies ran while one was open for 4% of the time, Pallas kernels for 30%

profile of v6, /device:TPU:1, one launch (start us, length us, event | category | flops | bytes accessed | tf_op | source)
XLA Modules:
  0.0 217.9 jit_solution(12945336576666768988)
XLA Ops:
  11.2 5.1 %collective-permute-done.1.partner = bf16[1536,1536]{1,0:T(8,128)(2,1)S(1)} collective-permute-done((bf16[1536,1536]{1,0:T(8,128)(2,1)}, bf16[1536,1536]{1,0:T(8,128)(2,1)S(1)}, u32[]{:S(2)}, u32[]{:S(2)}) %collective-permute-start.1) | collective-permute-done | bytes 4718624 | tf_op jit(solution)/shard_map/ppermute | solution.py:38
  23.7 4.7 %collective-permute-start.2 = (bf16[256,1536]{1,0:T(8,128)(2,1)S(1)}, bf16[256,1536]{1,0:T(8,128)(2,1)S(1)}, u32[]{:S(2)}, u32[]{:S(2)}) collective-permute-start(bf16[256,1536]{1,0:T(8,128)(2,1)S(1)} %slab_product.6.left), channel_id=1, source_target_pairs={{0,1},{3,2},{4,5},{7,6},{8,9},{11,10},{12,13},{15,14},{16,17},{19,... | collective-permute-start | bytes 2359304 | tf_op jit(solution)/shard_map/ppermute | solution.py:38
  33.4 3.6 %collective-permute-start.5 = (bf16[256,1536]{1,0:T(8,128)(2,1)S(1)}, bf16[256,1536]{1,0:T(8,128)(2,1)}, u32[]{:S(2)}, u32[]{:S(2)}) collective-permute-start(bf16[256,1536]{1,0:T(8,128)(2,1)S(1)} %slab_product.7.left), channel_id=1, source_target_pairs={{0,1},{3,2},{4,5},{7,6},{8,9},{11,10},{12,13},{15,14},{16,17},{19,... | collective-permute-start | bytes 2359304 | tf_op jit(solution)/shard_map/ppermute | solution.py:38
  37.1 5.4 %collective-permute-done.2.right = bf16[256,1536]{1,0:T(8,128)(2,1)S(1)} collective-permute-done((bf16[256,1536]{1,0:T(8,128)(2,1)S(1)}, bf16[256,1536]{1,0:T(8,128)(2,1)S(1)}, u32[]{:S(2)}, u32[]{:S(2)}) %collective-permute-start.2) | collective-permute-done | bytes 786464 | tf_op jit(solution)/shard_map/ppermute | solution.py:38
  53.6 6.0 %collective-permute-start.9 = (bf16[256,1536]{1,0:T(8,128)(2,1)S(1)}, bf16[256,1536]{1,0:T(8,128)(2,1)S(1)}, u32[]{:S(2)}, u32[]{:S(2)}) collective-permute-start(bf16[256,1536]{1,0:T(8,128)(2,1)S(1)} %slab_product.8.left), channel_id=1, source_target_pairs={{0,1},{3,2},{4,5},{7,6},{8,9},{11,10},{12,13},{15,14},{16,17},{19,... | collective-permute-start | bytes 2359304 | tf_op jit(solution)/shard_map/ppermute | solution.py:38
  68.5 6.5 %collective-permute-start.14 = (bf16[256,1536]{1,0:T(8,128)(2,1)S(1)}, bf16[256,1536]{1,0:T(8,128)(2,1)S(1)}, u32[]{:S(2)}, u32[]{:S(2)}) collective-permute-start(bf16[256,1536]{1,0:T(8,128)(2,1)S(1)} %slab_product.9.left), channel_id=1, source_target_pairs={{0,1},{3,2},{4,5},{7,6},{8,9},{11,10},{12,13},{15,14},{16,17},{19,... | collective-permute-start | bytes 2359304 | tf_op jit(solution)/shard_map/ppermute | solution.py:38
  84.3 4.7 %collective-permute-start.11 = (bf16[256,1536]{1,0:T(8,128)(2,1)S(1)}, bf16[256,1536]{1,0:T(8,128)(2,1)S(1)}, u32[]{:S(2)}, u32[]{:S(2)}) collective-permute-start(bf16[256,1536]{1,0:T(8,128)(2,1)S(1)} %slab_product.10.left), channel_id=1, source_target_pairs={{0,1},{3,2},{4,5},{7,6},{8,9},{11,10},{12,13},{15,14},{16,17},{19,... | collective-permute-start | bytes 2359304 | tf_op jit(solution)/shard_map/ppermute | solution.py:38
  89.0 3.4 %collective-permute-done.14.right = bf16[256,1536]{1,0:T(8,128)(2,1)S(1)} collective-permute-done((bf16[256,1536]{1,0:T(8,128)(2,1)S(1)}, bf16[256,1536]{1,0:T(8,128)(2,1)S(1)}, u32[]{:S(2)}, u32[]{:S(2)}) %collective-permute-start.14) | collective-permute-done | bytes 786464 | tf_op jit(solution)/shard_map/ppermute | solution.py:38
  94.8 4.2 %collective-permute-done.12.right = bf16[256,1536]{1,0:T(8,128)(2,1)S(1)} collective-permute-done((bf16[256,1536]{1,0:T(8,128)(2,1)S(1)}, bf16[256,1536]{1,0:T(8,128)(2,1)S(1)}, u32[]{:S(2)}, u32[]{:S(2)}) %collective-permute-start.12) | collective-permute-done | bytes 786464 | tf_op jit(solution)/shard_map/ppermute | solution.py:38
  103.7 4.1 %collective-permute-start.16 = (bf16[256,1536]{1,0:T(8,128)(2,1)S(1)}, bf16[256,1536]{1,0:T(8,128)(2,1)S(1)}, u32[]{:S(2)}, u32[]{:S(2)}) collective-permute-start(bf16[256,1536]{1,0:T(8,128)(2,1)S(1)} %slab_product.11.left), channel_id=1, source_target_pairs={{0,1},{3,2},{4,5},{7,6},{8,9},{11,10},{12,13},{15,14},{16,17},{19,... | collective-permute-start | bytes 2359304 | tf_op jit(solution)/shard_map/ppermute | solution.py:38
  115.8 10.3 %collective-permute-done.16.right = bf16[256,1536]{1,0:T(8,128)(2,1)S(1)} collective-permute-done((bf16[256,1536]{1,0:T(8,128)(2,1)S(1)}, bf16[256,1536]{1,0:T(8,128)(2,1)S(1)}, u32[]{:S(2)}, u32[]{:S(2)}) %collective-permute-start.16) | collective-permute-done | bytes 786464 | tf_op jit(solution)/shard_map/ppermute | solution.py:38
  127.8 4.9 %collective-permute-done.20.right = bf16[256,1536]{1,0:T(8,128)(2,1)S(1)} collective-permute-done((bf16[256,1536]{1,0:T(8,128)(2,1)S(1)}, bf16[256,1536]{1,0:T(8,128)(2,1)S(1)}, u32[]{:S(2)}, u32[]{:S(2)}) %collective-permute-start.20) | collective-permute-done | bytes 786464 | tf_op jit(solution)/shard_map/ppermute | solution.py:38
  133.4 6.6 %collective-permute-start.21 = (bf16[768,1536]{1,0:T(8,128)(2,1)S(1)}, bf16[768,1536]{1,0:T(8,128)(2,1)S(1)}, u32[]{:S(2)}, u32[]{:S(2)}) collective-permute-start(bf16[768,1536]{1,0:T(8,128)(2,1)S(1)} %amp_of_slab.9.refs_0_), channel_id=1, source_target_pairs={{0,4},{4,0},{8,12},{12,8},{1,5},{5,1},{9,13},{13,9},{2,6},{6,2},{1... | collective-permute-start | bytes 7077896 | tf_op jit(solution)/shard_map/ppermute | solution.py:38
  144.3 4.8 %mix.2 = (bf16[1536,1536]{1,0:T(8,128)(2,1)S(1)}, f32[2,384,384]{2,1,0:T(8,128)S(1)}) custom-call(s32[3]{0:T(128)S(1)} %pad_add_fusion.place, bf16[768,1536]{1,0:T(8,128)(2,1)S(1)} %amp_of_slab.9.refs_0_, bf16[768,1536]{1,0:T(8,128)(2,1)S(1)} %collective-permute-done.21.refs_1_), custom_call_target="tpu_custom_call" | custom-call | flops 10000000 | bytes 10000 | tf_op jit(solution)/shard_map/mix/pallas_call | solution.py:186
  149.1 6.7 %cross_term.2.kept = bf16[1536,1024]{1,0:T(8,128)(2,1)S(1)} custom-call(s32[3]{0:T(128)S(1)} %pad_add_fusion.place, bf16[1536,768]{1,0:T(8,128)(2,1)S(1)} %constant_dynamic-update-slice_fusion.lower, bf16[1536,768]{1,0:T(8,128)(2,1)S(1)} %collective-permute-done.22.upper, bf16[1536,1536]{1,0:T(8,128)(2,1)S(1)} %bitcast.11, ...), custom_call_target="tpu_custom_call" | custom-call | flops 4000000000 | bytes 10000 | tf_op jit(solution)/shard_map/cross_term/pallas_call | solution.py:233
  155.8 3.2 %collective-permute-start.28 = (bf16[1536,1024]{1,0:T(8,128)(2,1)S(1)}, bf16[1536,1024]{1,0:T(8,128)(2,1)S(1)}, u32[]{:S(2)}, u32[]{:S(2)}) collective-permute-start(bf16[1536,1024]{1,0:T(8,128)(2,1)S(1)} %cross_term.2.kept), channel_id=1, source_target_pairs={{4,12},{12,4},{5,13},{13,5},{6,14},{14,6},{7,15},{15,7},{20,28},{2... | collective-permute-start | bytes 9437192 | tf_op jit(solution)/shard_map/ppermute | solution.py:38
  159.0 4.9 %collective-permute-done.19.right = bf16[256,1536]{1,0:T(8,128)(2,1)S(1)} collective-permute-done((bf16[256,1536]{1,0:T(8,128)(2,1)S(1)}, bf16[256,1536]{1,0:T(8,128)(2,1)S(1)}, u32[]{:S(2)}, u32[]{:S(2)}) %collective-permute-start.19) | collective-permute-done | bytes 786464 | tf_op jit(solution)/shard_map/ppermute | solution.py:38
  167.9 3.5 %cross_term.3.kept = bf16[1536,512]{1,0:T(8,128)(2,1)S(1)} custom-call(s32[3]{0:T(128)S(1)} %pad_add_fusion.place, bf16[1536,768]{1,0:T(8,128)(2,1)S(1)} %constant_dynamic-update-slice_fusion.lower, bf16[1536,768]{1,0:T(8,128)(2,1)S(1)} %collective-permute-done.22.upper, bf16[1536,1536]{1,0:T(8,128)(2,1)S(1)} %bitcast.11, ...), custom_call_target="tpu_custom_call" | custom-call | flops 4000000000 | bytes 10000 | tf_op jit(solution)/shard_map/cross_term/pallas_call | solution.py:233
  171.4 15.3 %collective-permute-done.24.right = bf16[256,1536]{1,0:T(8,128)(2,1)S(1)} collective-permute-done((bf16[256,1536]{1,0:T(8,128)(2,1)S(1)}, bf16[256,1536]{1,0:T(8,128)(2,1)S(1)}, u32[]{:S(2)}, u32[]{:S(2)}) %collective-permute-start.24) | collective-permute-done | bytes 786464 | tf_op jit(solution)/shard_map/ppermute | solution.py:38
  188.6 3.4 %collective-permute-start.29 = (bf16[1536,512]{1,0:T(8,128)(2,1)S(1)}, bf16[1536,512]{1,0:T(8,128)(2,1)S(1)}, u32[]{:S(2)}, u32[]{:S(2)}) collective-permute-start(bf16[1536,512]{1,0:T(8,128)(2,1)S(1)} %cross_term.3.kept), channel_id=1, source_target_pairs={{4,12},{12,4},{5,13},{13,5},{6,14},{14,6},{7,15},{15,7},{20,28},{2... | collective-permute-start | bytes 4718600 | tf_op jit(solution)/shard_map/ppermute | solution.py:38
  192.0 4.8 %mix.3 = (bf16[1536,1536]{1,0:T(8,128)(2,1)S(1)}, f32[2,384,384]{2,1,0:T(8,128)S(1)}) custom-call(s32[3]{0:T(128)S(1)} %pad_add_fusion.place, bf16[256,1536]{1,0:T(8,128)(2,1)S(1)} %amp_of_slab.6.refs_0_, bf16[256,1536]{1,0:T(8,128)(2,1)S(1)} %amp_of_slab.10.refs_1_, bf16[256,1536]{1,0:T(8,128)(2,1)S(1)} %amp_of_slab.11.refs_2_, ...), custom_call_target="tpu_custom_call" | custom-call | flops 10000000 | bytes 10000 | tf_op jit(solution)/shard_map/mix/pallas_call | solution.py:186
  197.4 8.2 %local_term.1.gamma = bf16[1,1536,1536]{2,1,0:T(8,128)(2,1)} custom-call(s32[3]{0:T(128)S(1)} %pad_add_fusion.place, bf16[1536,1536]{1,0:T(8,128)(2,1)S(1)} %bitcast.11, bf16[1536,1536]{1,0:T(8,128)(2,1)S(1)} %get-tuple-element.249.weight, bf16[1536,1024]{1,0:T(8,128)(2,1)S(1)} %cross_term.2.kept, bf16[1536,1024]{1,0:T(8,128)(2,1)S(1)} %collective-permute-done.28.arrived), custom_call_target="tpu_custom_call" | custom-call | flops 4000000000 | bytes 10000 | tf_op jit(solution)/shard_map/local_term/pallas_call | solution.py:271
  205.6 2.9 %local_rest.1.rest = bf16[1536,512]{1,0:T(8,128)(2,1)S(1)} custom-call(bf16[1536,1536]{1,0:T(8,128)(2,1)S(1)} %bitcast.11, bf16[1536,1536]{1,0:T(8,128)(2,1)S(1)} %get-tuple-element.249.weight), custom_call_target="tpu_custom_call" | custom-call | flops 5760000000 | bytes 10000 | tf_op jit(solution)/shard_map/local_rest/pallas_call | solution.py:301
  208.5 5.4 %collective-permute-done.29.arrived = bf16[1536,512]{1,0:T(8,128)(2,1)S(1)} collective-permute-done((bf16[1536,512]{1,0:T(8,128)(2,1)S(1)}, bf16[1536,512]{1,0:T(8,128)(2,1)S(1)}, u32[]{:S(2)}, u32[]{:S(2)}) %collective-permute-start.29) | collective-permute-done | bytes 1572896 | tf_op jit(solution)/shard_map/ppermute | solution.py:38
  (121 shorter events, 84.5 us)
Async XLA Ops:
  8.5 21.1 %collective-permute-start.3 = (bf16[1536,256]{1,0:T(8,128)(2,1)S(1)}, bf16[1536,256]{1,0:T(8,128)(2,1)S(1)}, u32[]{:S(2)}, u32[]{:S(2)}) collective-permute-start(bf16[1536,256]{1,0:T(8,128)(2,1)S(1)} %broadcast_select_fusion.4), channel_id=1, source_target_pairs={{0,8},{4,12},{8,0},{12,4},{1,9},{5,13},{9,1},{13,5},{2,10},{6,14},... | collective-permute-start | bytes 2359304 | tf_op jit(solution)/shard_map/ppermute | solution.py:38
  23.7 18.7 %collective-permute-start.2 = (bf16[256,1536]{1,0:T(8,128)(2,1)S(1)}, bf16[256,1536]{1,0:T(8,128)(2,1)S(1)}, u32[]{:S(2)}, u32[]{:S(2)}) collective-permute-start(bf16[256,1536]{1,0:T(8,128)(2,1)S(1)} %slab_product.6.left), channel_id=1, source_target_pairs={{0,1},{3,2},{4,5},{7,6},{8,9},{11,10},{12,13},{15,14},{16,17},{19,... | collective-permute-start | bytes 2359304 | tf_op jit(solution)/shard_map/ppermute | solution.py:38
  28.4 20.1 %collective-permute-start.6 = (bf16[1536,256]{1,0:T(8,128)(2,1)}, bf16[1536,256]{1,0:T(8,128)(2,1)S(1)}, u32[]{:S(2)}, u32[]{:S(2)}) collective-permute-start(bf16[1536,256]{1,0:T(8,128)(2,1)} %broadcast_select_fusion.3), channel_id=1, source_target_pairs={{0,8},{4,12},{8,0},{12,4},{1,9},{5,13},{9,1},{13,5},{2,10},{6,14},... | collective-permute-start | bytes 2359304 | tf_op jit(solution)/shard_map/ppermute | solution.py:38
  33.4 26.2 %collective-permute-start.5 = (bf16[256,1536]{1,0:T(8,128)(2,1)S(1)}, bf16[256,1536]{1,0:T(8,128)(2,1)}, u32[]{:S(2)}, u32[]{:S(2)}) collective-permute-start(bf16[256,1536]{1,0:T(8,128)(2,1)S(1)} %slab_product.7.left), channel_id=1, source_target_pairs={{0,1},{3,2},{4,5},{7,6},{8,9},{11,10},{12,13},{15,14},{16,17},{19,... | collective-permute-start | bytes 2359304 | tf_op jit(solution)/shard_map/ppermute | solution.py:38
  43.5 18.5 %collective-permute-start.4 = (bf16[256,1536]{1,0:T(8,128)(2,1)}, bf16[256,1536]{1,0:T(8,128)(2,1)}, u32[]{:S(2)}, u32[]{:S(2)}) collective-permute-start(bf16[256,1536]{1,0:T(8,128)(2,1)} %half_sum.6.left), channel_id=1, source_target_pairs={{1,2},{2,1},{5,6},{6,5},{9,10},{10,9},{13,14},{14,13},{17,18},{18,... | collective-permute-start | bytes 2359304 | tf_op jit(solution)/shard_map/ppermute | solution.py:38
  45.1 20.6 %collective-permute-start.10 = (bf16[1536,256]{1,0:T(8,128)(2,1)}, bf16[1536,256]{1,0:T(8,128)(2,1)S(1)}, u32[]{:S(2)}, u32[]{:S(2)}) collective-permute-start(bf16[1536,256]{1,0:T(8,128)(2,1)} %broadcast_select_fusion.2), channel_id=1, source_target_pairs={{0,8},{4,12},{8,0},{12,4},{1,9},{5,13},{9,1},{13,5},{2,10},{6,14},... | collective-permute-start | bytes 2359304 | tf_op jit(solution)/shard_map/ppermute | solution.py:38
  53.6 23.0 %collective-permute-start.9 = (bf16[256,1536]{1,0:T(8,128)(2,1)S(1)}, bf16[256,1536]{1,0:T(8,128)(2,1)S(1)}, u32[]{:S(2)}, u32[]{:S(2)}) collective-permute-start(bf16[256,1536]{1,0:T(8,128)(2,1)S(1)} %slab_product.8.left), channel_id=1, source_target_pairs={{0,1},{3,2},{4,5},{7,6},{8,9},{11,10},{12,13},{15,14},{16,17},{19,... | collective-permute-start | bytes 2359304 | tf_op jit(solution)/shard_map/ppermute | solution.py:38
  61.0 16.6 %collective-permute-start.8 = (bf16[256,1536]{1,0:T(8,128)(2,1)S(1)}, bf16[256,1536]{1,0:T(8,128)(2,1)S(1)}, u32[]{:S(2)}, u32[]{:S(2)}) collective-permute-start(bf16[256,1536]{1,0:T(8,128)(2,1)S(1)} %half_sum.7.left), channel_id=1, source_target_pairs={{1,2},{2,1},{5,6},{6,5},{9,10},{10,9},{13,14},{14,13},{17,18},{18,... | collective-permute-start | bytes 2359304 | tf_op jit(solution)/shard_map/ppermute | solution.py:38
  68.5 23.8 %collective-permute-start.14 = (bf16[256,1536]{1,0:T(8,128)(2,1)S(1)}, bf16[256,1536]{1,0:T(8,128)(2,1)S(1)}, u32[]{:S(2)}, u32[]{:S(2)}) collective-permute-start(bf16[256,1536]{1,0:T(8,128)(2,1)S(1)} %slab_product.9.left), channel_id=1, source_target_pairs={{0,1},{3,2},{4,5},{7,6},{8,9},{11,10},{12,13},{15,14},{16,17},{19,... | collective-permute-start | bytes 2359304 | tf_op jit(solution)/shard_map/ppermute | solution.py:38
  76.8 16.4 %collective-permute-start.13 = (bf16[256,1536]{1,0:T(8,128)(2,1)S(1)}, bf16[256,1536]{1,0:T(8,128)(2,1)S(1)}, u32[]{:S(2)}, u32[]{:S(2)}) collective-permute-start(bf16[256,1536]{1,0:T(8,128)(2,1)S(1)} %half_sum.8.left), channel_id=1, source_target_pairs={{1,2},{2,1},{5,6},{6,5},{9,10},{10,9},{13,14},{14,13},{17,18},{18,... | collective-permute-start | bytes 2359304 | tf_op jit(solution)/shard_map/ppermute | solution.py:38
  79.1 19.9 %collective-permute-start.12 = (bf16[256,1536]{1,0:T(8,128)(2,1)S(1)}, bf16[256,1536]{1,0:T(8,128)(2,1)S(1)}, u32[]{:S(2)}, u32[]{:S(2)}) collective-permute-start(bf16[256,1536]{1,0:T(8,128)(2,1)S(1)} %amplitude.7.left), channel_id=1, source_target_pairs={{1,0},{2,3},{5,4},{6,7},{9,8},{10,11},{13,12},{14,15},{17,16},{18,... | collective-permute-start | bytes 2359304 | tf_op jit(solution)/shard_map/ppermute | solution.py:38
  84.3 24.9 %collective-permute-start.11 = (bf16[256,1536]{1,0:T(8,128)(2,1)S(1)}, bf16[256,1536]{1,0:T(8,128)(2,1)S(1)}, u32[]{:S(2)}, u32[]{:S(2)}) collective-permute-start(bf16[256,1536]{1,0:T(8,128)(2,1)S(1)} %slab_product.10.left), channel_id=1, source_target_pairs={{0,1},{3,2},{4,5},{7,6},{8,9},{11,10},{12,13},{15,14},{16,17},{19,... | collective-permute-start | bytes 2359304 | tf_op jit(solution)/shard_map/ppermute | solution.py:38
  92.5 17.6 %collective-permute-start.18 = (bf16[256,1536]{1,0:T(8,128)(2,1)S(1)}, bf16[256,1536]{1,0:T(8,128)(2,1)S(1)}, u32[]{:S(2)}, u32[]{:S(2)}) collective-permute-start(bf16[256,1536]{1,0:T(8,128)(2,1)S(1)} %half_sum.9.left), channel_id=1, source_target_pairs={{1,2},{2,1},{5,6},{6,5},{9,10},{10,9},{13,14},{14,13},{17,18},{18,... | collective-permute-start | bytes 2359304 | tf_op jit(solution)/shard_map/ppermute | solution.py:38
  103.7 22.3 %collective-permute-start.16 = (bf16[256,1536]{1,0:T(8,128)(2,1)S(1)}, bf16[256,1536]{1,0:T(8,128)(2,1)S(1)}, u32[]{:S(2)}, u32[]{:S(2)}) collective-permute-start(bf16[256,1536]{1,0:T(8,128)(2,1)S(1)} %slab_product.11.left), channel_id=1, source_target_pairs={{0,1},{3,2},{4,5},{7,6},{8,9},{11,10},{12,13},{15,14},{16,17},{19,... | collective-permute-start | bytes 2359304 | tf_op jit(solution)/shard_map/ppermute | solution.py:38
  109.4 16.9 %collective-permute-start.15 = (bf16[256,1536]{1,0:T(8,128)(2,1)S(1)}, bf16[256,1536]{1,0:T(8,128)(2,1)S(1)}, u32[]{:S(2)}, u32[]{:S(2)}) collective-permute-start(bf16[256,1536]{1,0:T(8,128)(2,1)S(1)} %half_sum.10.left), channel_id=1, source_target_pairs={{1,2},{2,1},{5,6},{6,5},{9,10},{10,9},{13,14},{14,13},{17,18},{18,... | collective-permute-start | bytes 2359304 | tf_op jit(solution)/shard_map/ppermute | solution.py:38
  111.7 21.0 %collective-permute-start.20 = (bf16[256,1536]{1,0:T(8,128)(2,1)S(1)}, bf16[256,1536]{1,0:T(8,128)(2,1)S(1)}, u32[]{:S(2)}, u32[]{:S(2)}) collective-permute-start(bf16[256,1536]{1,0:T(8,128)(2,1)S(1)} %amplitude.9.left), channel_id=1, source_target_pairs={{1,0},{2,3},{5,4},{6,7},{9,8},{10,11},{13,12},{14,15},{17,16},{18,... | collective-permute-start | bytes 2359304 | tf_op jit(solution)/shard_map/ppermute | solution.py:38
  142.3 22.2 %collective-permute-start.23 = (bf16[256,1536]{1,0:T(8,128)(2,1)S(1)}, bf16[256,1536]{1,0:T(8,128)(2,1)S(1)}, u32[]{:S(2)}, u32[]{:S(2)}) collective-permute-start(bf16[256,1536]{1,0:T(8,128)(2,1)S(1)} %half_sum.11.left), channel_id=1, source_target_pairs={{1,2},{2,1},{5,6},{6,5},{9,10},{10,9},{13,14},{14,13},{17,18},{18,... | collective-permute-start | bytes 2359304 | tf_op jit(solution)/shard_map/ppermute | solution.py:38
  143.0 20.9 %collective-permute-start.19 = (bf16[256,1536]{1,0:T(8,128)(2,1)S(1)}, bf16[256,1536]{1,0:T(8,128)(2,1)S(1)}, u32[]{:S(2)}, u32[]{:S(2)}) collective-permute-start(bf16[256,1536]{1,0:T(8,128)(2,1)S(1)} %amplitude.10.left), channel_id=1, source_target_pairs={{1,0},{2,3},{5,4},{6,7},{9,8},{10,11},{13,12},{14,15},{17,16},{18,... | collective-permute-start | bytes 2359304 | tf_op jit(solution)/shard_map/ppermute | solution.py:38
  155.8 41.6 %collective-permute-start.28 = (bf16[1536,1024]{1,0:T(8,128)(2,1)S(1)}, bf16[1536,1024]{1,0:T(8,128)(2,1)S(1)}, u32[]{:S(2)}, u32[]{:S(2)}) collective-permute-start(bf16[1536,1024]{1,0:T(8,128)(2,1)S(1)} %cross_term.2.kept), channel_id=1, source_target_pairs={{4,12},{12,4},{5,13},{13,5},{6,14},{14,6},{7,15},{15,7},{20,28},{2... | collective-permute-start | bytes 9437192 | tf_op jit(solution)/shard_map/ppermute | solution.py:38
  166.1 20.6 %collective-permute-start.24 = (bf16[256,1536]{1,0:T(8,128)(2,1)S(1)}, bf16[256,1536]{1,0:T(8,128)(2,1)S(1)}, u32[]{:S(2)}, u32[]{:S(2)}) collective-permute-start(bf16[256,1536]{1,0:T(8,128)(2,1)S(1)} %amplitude.11.left), channel_id=1, source_target_pairs={{1,0},{2,3},{5,4},{6,7},{9,8},{10,11},{13,12},{14,15},{17,16},{18,... | collective-permute-start | bytes 2359304 | tf_op jit(solution)/shard_map/ppermute | solution.py:38
  167.4 24.6 %collective-permute-start.25 = (bf16[256,1536]{1,0:T(8,128)(2,1)S(1)}, bf16[256,1536]{1,0:T(8,128)(2,1)S(1)}, u32[]{:S(2)}, u32[]{:S(2)}) collective-permute-start(bf16[256,1536]{1,0:T(8,128)(2,1)S(1)} %amp_of_slab.6.refs_0_), channel_id=1, source_target_pairs={{0,4},{4,0},{8,12},{12,8},{1,5},{5,1},{9,13},{13,9},{2,6},{6,2},{1... | collective-permute-start | bytes 2359304 | tf_op jit(solution)/shard_map/ppermute | solution.py:38
  167.8 24.2 %collective-permute-start.26 = (bf16[256,1536]{1,0:T(8,128)(2,1)S(1)}, bf16[256,1536]{1,0:T(8,128)(2,1)S(1)}, u32[]{:S(2)}, u32[]{:S(2)}) collective-permute-start(bf16[256,1536]{1,0:T(8,128)(2,1)S(1)} %amp_of_slab.10.refs_1_), channel_id=1, source_target_pairs={{0,4},{4,0},{8,12},{12,8},{1,5},{5,1},{9,13},{13,9},{2,6},{6,2},{1... | collective-permute-start | bytes 2359304 | tf_op jit(solution)/shard_map/ppermute | solution.py:38
  188.6 25.3 %collective-permute-start.29 = (bf16[1536,512]{1,0:T(8,128)(2,1)S(1)}, bf16[1536,512]{1,0:T(8,128)(2,1)S(1)}, u32[]{:S(2)}, u32[]{:S(2)}) collective-permute-start(bf16[1536,512]{1,0:T(8,128)(2,1)S(1)} %cross_term.3.kept), channel_id=1, source_target_pairs={{4,12},{12,4},{5,13},{13,5},{6,14},{14,6},{7,15},{15,7},{20,28},{2... | collective-permute-start | bytes 4718600 | tf_op jit(solution)/shard_map/ppermute | solution.py:38
  197.1 20.0 %collective-permute-start.30 = (bf16[384,384]{1,0:T(8,128)(2,1)S(1)}, bf16[384,384]{1,0:T(8,128)(2,1)S(1)}, u32[]{:S(2)}, u32[]{:S(2)}) collective-permute-start(bf16[384,384]{1,0:T(8,128)(2,1)S(1)} %fusion), channel_id=1, source_target_pairs={{0,8},{4,12},{8,0},{12,4},{1,9},{5,13},{9,1},{13,5},{2,10},{6,14},... | collective-permute-start | bytes 884744 | tf_op jit(solution)/shard_map/ppermute | solution.py:38
  (21 other events, 200.4 us)

commit v7 on v6

--- a/solution.py
+++ b/solution.py
@@ -165,9 +165,9 @@
     start = pl.multiple_of(step * band, band)
     for j in range(nvirt // band):
         tile = amp_t[pl.ds(start, band), j * band : (j + 1) * band].astype(F32)
-        turned = amp_t[j * band : (j + 1) * band, pl.ds(start, band)].astype(F32).T
-        amp[pl.ds(start, band), j * band : (j + 1) * band] = turned.astype(BF16)
-        mix[:, j * band : (j + 1) * band] = (here * tile + there * turned).astype(BF16)
+        turned = amp_t[j * band : (j + 1) * band, pl.ds(start, band)].T
+        amp[pl.ds(start, band), j * band : (j + 1) * band] = turned
+        mix[:, j * band : (j + 1) * band] = (here * tile + there * turned.astype(F32)).astype(BF16)
 
     @pl.when(step == nvirt // band - 1)
     def _():

time: 219 us -> 218 us (level)
  no operation moved by 1% of the time
where the time goes in v7:
time: 218 us
  starting transfers between devices  69.5 us (32%)
  Pallas kernels  66.2 us (30%)
  waiting for transfers between devices  64.9 us (30%)
  local copies, waits for them, and re-layouts  8.01 us (4%)
  other arithmetic  7.7 us (4%)
    ppermute x31, starting transfers between devices, send(): return lax.ppermute(self.ready(value, *others)[0], axis, pairs)  69.5 us
    ppermute x31, waiting for transfers between devices, send(): return lax.ppermute(self.ready(value, *others)[0], axis, pairs)  64.9 us
    pallas_call x6, Pallas kernels, product_rows(): pl.pallas_call(product_kernel, grid_spec=pltpu.PrefetchScalarGridSpec(num...  16.6 us
    pallas_call x6, Pallas kernels, amplitude(): pl.pallas_call(amp_kernel, grid_spec=pltpu.PrefetchScalarGridSpec(num_sca...  10.2 us
    pallas_call x2, Pallas kernels, cross_columns(): pl.pallas_call(cross_kernel, grid_spec=pltpu.PrefetchScalarGridSpec(num_s...  10.2 us
    pallas_call x2, Pallas kernels, mix(): pl.pallas_call(functools.partial(mix_kernel, len(own), nvirt // 2, band,...  8.96 us
    pallas_call x1, Pallas kernels, final_columns(): pl.pallas_call(final_kernel, grid_spec=pltpu.PrefetchScalarGridSpec(num_s...  8.18 us
    unnamed x30, local copies, waits for them, and re-layouts  4.77 us
  transfers between devices with their start and end apart: 31, of which 14 were waited for; matrix products, arithmetic and copies ran while one was open for 4% of the time, Pallas kernels for 30%

profile of v7, /device:TPU:1, one launch (start us, length us, event | category | flops | bytes accessed | tf_op | source)
XLA Modules:
  0.0 217.6 jit_solution(5723230671685782875)
XLA Ops:
  11.2 5.1 %collective-permute-done.1.partner = bf16[1536,1536]{1,0:T(8,128)(2,1)S(1)} collective-permute-done((bf16[1536,1536]{1,0:T(8,128)(2,1)}, bf16[1536,1536]{1,0:T(8,128)(2,1)S(1)}, u32[]{:S(2)}, u32[]{:S(2)}) %collective-permute-start.1) | collective-permute-done | bytes 4718624 | tf_op jit(solution)/shard_map/ppermute | solution.py:38
  23.7 4.7 %collective-permute-start.2 = (bf16[256,1536]{1,0:T(8,128)(2,1)S(1)}, bf16[256,1536]{1,0:T(8,128)(2,1)S(1)}, u32[]{:S(2)}, u32[]{:S(2)}) collective-permute-start(bf16[256,1536]{1,0:T(8,128)(2,1)S(1)} %slab_product.6.left), channel_id=1, source_target_pairs={{0,1},{3,2},{4,5},{7,6},{8,9},{11,10},{12,13},{15,14},{16,17},{19,... | collective-permute-start | bytes 2359304 | tf_op jit(solution)/shard_map/ppermute | solution.py:38
  33.4 3.6 %collective-permute-start.5 = (bf16[256,1536]{1,0:T(8,128)(2,1)S(1)}, bf16[256,1536]{1,0:T(8,128)(2,1)}, u32[]{:S(2)}, u32[]{:S(2)}) collective-permute-start(bf16[256,1536]{1,0:T(8,128)(2,1)S(1)} %slab_product.7.left), channel_id=1, source_target_pairs={{0,1},{3,2},{4,5},{7,6},{8,9},{11,10},{12,13},{15,14},{16,17},{19,... | collective-permute-start | bytes 2359304 | tf_op jit(solution)/shard_map/ppermute | solution.py:38
  37.1 5.4 %collective-permute-done.2.right = bf16[256,1536]{1,0:T(8,128)(2,1)S(1)} collective-permute-done((bf16[256,1536]{1,0:T(8,128)(2,1)S(1)}, bf16[256,1536]{1,0:T(8,128)(2,1)S(1)}, u32[]{:S(2)}, u32[]{:S(2)}) %collective-permute-start.2) | collective-permute-done | bytes 786464 | tf_op jit(solution)/shard_map/ppermute | solution.py:38
  53.6 6.0 %collective-permute-start.9 = (bf16[256,1536]{1,0:T(8,128)(2,1)S(1)}, bf16[256,1536]{1,0:T(8,128)(2,1)S(1)}, u32[]{:S(2)}, u32[]{:S(2)}) collective-permute-start(bf16[256,1536]{1,0:T(8,128)(2,1)S(1)} %slab_product.8.left), channel_id=1, source_target_pairs={{0,1},{3,2},{4,5},{7,6},{8,9},{11,10},{12,13},{15,14},{16,17},{19,... | collective-permute-start | bytes 2359304 | tf_op jit(solution)/shard_map/ppermute | solution.py:38
  68.5 6.5 %collective-permute-start.14 = (bf16[256,1536]{1,0:T(8,128)(2,1)S(1)}, bf16[256,1536]{1,0:T(8,128)(2,1)S(1)}, u32[]{:S(2)}, u32[]{:S(2)}) collective-permute-start(bf16[256,1536]{1,0:T(8,128)(2,1)S(1)} %slab_product.9.left), channel_id=1, source_target_pairs={{0,1},{3,2},{4,5},{7,6},{8,9},{11,10},{12,13},{15,14},{16,17},{19,... | collective-permute-start | bytes 2359304 | tf_op jit(solution)/shard_map/ppermute | solution.py:38
  84.3 4.7 %collective-permute-start.11 = (bf16[256,1536]{1,0:T(8,128)(2,1)S(1)}, bf16[256,1536]{1,0:T(8,128)(2,1)S(1)}, u32[]{:S(2)}, u32[]{:S(2)}) collective-permute-start(bf16[256,1536]{1,0:T(8,128)(2,1)S(1)} %slab_product.10.left), channel_id=1, source_target_pairs={{0,1},{3,2},{4,5},{7,6},{8,9},{11,10},{12,13},{15,14},{16,17},{19,... | collective-permute-start | bytes 2359304 | tf_op jit(solution)/shard_map/ppermute | solution.py:38
  89.0 3.4 %collective-permute-done.14.right = bf16[256,1536]{1,0:T(8,128)(2,1)S(1)} collective-permute-done((bf16[256,1536]{1,0:T(8,128)(2,1)S(1)}, bf16[256,1536]{1,0:T(8,128)(2,1)S(1)}, u32[]{:S(2)}, u32[]{:S(2)}) %collective-permute-start.14) | collective-permute-done | bytes 786464 | tf_op jit(solution)/shard_map/ppermute | solution.py:38
  94.8 4.2 %collective-permute-done.12.right = bf16[256,1536]{1,0:T(8,128)(2,1)S(1)} collective-permute-done((bf16[256,1536]{1,0:T(8,128)(2,1)S(1)}, bf16[256,1536]{1,0:T(8,128)(2,1)S(1)}, u32[]{:S(2)}, u32[]{:S(2)}) %collective-permute-start.12) | collective-permute-done | bytes 786464 | tf_op jit(solution)/shard_map/ppermute | solution.py:38
  103.7 4.1 %collective-permute-start.16 = (bf16[256,1536]{1,0:T(8,128)(2,1)S(1)}, bf16[256,1536]{1,0:T(8,128)(2,1)S(1)}, u32[]{:S(2)}, u32[]{:S(2)}) collective-permute-start(bf16[256,1536]{1,0:T(8,128)(2,1)S(1)} %slab_product.11.left), channel_id=1, source_target_pairs={{0,1},{3,2},{4,5},{7,6},{8,9},{11,10},{12,13},{15,14},{16,17},{19,... | collective-permute-start | bytes 2359304 | tf_op jit(solution)/shard_map/ppermute | solution.py:38
  115.8 10.3 %collective-permute-done.16.right = bf16[256,1536]{1,0:T(8,128)(2,1)S(1)} collective-permute-done((bf16[256,1536]{1,0:T(8,128)(2,1)S(1)}, bf16[256,1536]{1,0:T(8,128)(2,1)S(1)}, u32[]{:S(2)}, u32[]{:S(2)}) %collective-permute-start.16) | collective-permute-done | bytes 786464 | tf_op jit(solution)/shard_map/ppermute | solution.py:38
  127.8 4.9 %collective-permute-done.20.right = bf16[256,1536]{1,0:T(8,128)(2,1)S(1)} collective-permute-done((bf16[256,1536]{1,0:T(8,128)(2,1)S(1)}, bf16[256,1536]{1,0:T(8,128)(2,1)S(1)}, u32[]{:S(2)}, u32[]{:S(2)}) %collective-permute-start.20) | collective-permute-done | bytes 786464 | tf_op jit(solution)/shard_map/ppermute | solution.py:38
  133.4 6.6 %collective-permute-start.21 = (bf16[768,1536]{1,0:T(8,128)(2,1)S(1)}, bf16[768,1536]{1,0:T(8,128)(2,1)S(1)}, u32[]{:S(2)}, u32[]{:S(2)}) collective-permute-start(bf16[768,1536]{1,0:T(8,128)(2,1)S(1)} %amp_of_slab.9.refs_0_), channel_id=1, source_target_pairs={{0,4},{4,0},{8,12},{12,8},{1,5},{5,1},{9,13},{13,9},{2,6},{6,2},{1... | collective-permute-start | bytes 7077896 | tf_op jit(solution)/shard_map/ppermute | solution.py:38
  144.3 4.5 %mix.2 = (bf16[1536,1536]{1,0:T(8,128)(2,1)S(1)}, f32[2,384,384]{2,1,0:T(8,128)S(1)}) custom-call(s32[3]{0:T(128)S(1)} %pad_add_fusion.place, bf16[768,1536]{1,0:T(8,128)(2,1)S(1)} %amp_of_slab.9.refs_0_, bf16[768,1536]{1,0:T(8,128)(2,1)S(1)} %collective-permute-done.21.refs_1_), custom_call_target="tpu_custom_call" | custom-call | flops 10000000 | bytes 10000 | tf_op jit(solution)/shard_map/mix/pallas_call | solution.py:186
  148.8 6.7 %cross_term.2.kept = bf16[1536,1024]{1,0:T(8,128)(2,1)S(1)} custom-call(s32[3]{0:T(128)S(1)} %pad_add_fusion.place, bf16[1536,768]{1,0:T(8,128)(2,1)S(1)} %constant_dynamic-update-slice_fusion.lower, bf16[1536,768]{1,0:T(8,128)(2,1)S(1)} %collective-permute-done.22.upper, bf16[1536,1536]{1,0:T(8,128)(2,1)S(1)} %bitcast.11, ...), custom_call_target="tpu_custom_call" | custom-call | flops 4000000000 | bytes 10000 | tf_op jit(solution)/shard_map/cross_term/pallas_call | solution.py:233
  155.5 3.2 %collective-permute-start.28 = (bf16[1536,1024]{1,0:T(8,128)(2,1)S(1)}, bf16[1536,1024]{1,0:T(8,128)(2,1)S(1)}, u32[]{:S(2)}, u32[]{:S(2)}) collective-permute-start(bf16[1536,1024]{1,0:T(8,128)(2,1)S(1)} %cross_term.2.kept), channel_id=1, source_target_pairs={{4,12},{12,4},{5,13},{13,5},{6,14},{14,6},{7,15},{15,7},{20,28},{2... | collective-permute-start | bytes 9437192 | tf_op jit(solution)/shard_map/ppermute | solution.py:38
  158.7 5.2 %collective-permute-done.19.right = bf16[256,1536]{1,0:T(8,128)(2,1)S(1)} collective-permute-done((bf16[256,1536]{1,0:T(8,128)(2,1)S(1)}, bf16[256,1536]{1,0:T(8,128)(2,1)S(1)}, u32[]{:S(2)}, u32[]{:S(2)}) %collective-permute-start.19) | collective-permute-done | bytes 786464 | tf_op jit(solution)/shard_map/ppermute | solution.py:38
  167.9 3.5 %cross_term.3.kept = bf16[1536,512]{1,0:T(8,128)(2,1)S(1)} custom-call(s32[3]{0:T(128)S(1)} %pad_add_fusion.place, bf16[1536,768]{1,0:T(8,128)(2,1)S(1)} %constant_dynamic-update-slice_fusion.lower, bf16[1536,768]{1,0:T(8,128)(2,1)S(1)} %collective-permute-done.22.upper, bf16[1536,1536]{1,0:T(8,128)(2,1)S(1)} %bitcast.11, ...), custom_call_target="tpu_custom_call" | custom-call | flops 4000000000 | bytes 10000 | tf_op jit(solution)/shard_map/cross_term/pallas_call | solution.py:233
  171.4 15.3 %collective-permute-done.24.right = bf16[256,1536]{1,0:T(8,128)(2,1)S(1)} collective-permute-done((bf16[256,1536]{1,0:T(8,128)(2,1)S(1)}, bf16[256,1536]{1,0:T(8,128)(2,1)S(1)}, u32[]{:S(2)}, u32[]{:S(2)}) %collective-permute-start.24) | collective-permute-done | bytes 786464 | tf_op jit(solution)/shard_map/ppermute | solution.py:38
  188.6 3.4 %collective-permute-start.29 = (bf16[1536,512]{1,0:T(8,128)(2,1)S(1)}, bf16[1536,512]{1,0:T(8,128)(2,1)S(1)}, u32[]{:S(2)}, u32[]{:S(2)}) collective-permute-start(bf16[1536,512]{1,0:T(8,128)(2,1)S(1)} %cross_term.3.kept), channel_id=1, source_target_pairs={{4,12},{12,4},{5,13},{13,5},{6,14},{14,6},{7,15},{15,7},{20,28},{2... | collective-permute-start | bytes 4718600 | tf_op jit(solution)/shard_map/ppermute | solution.py:38
  192.0 4.5 %mix.3 = (bf16[1536,1536]{1,0:T(8,128)(2,1)S(1)}, f32[2,384,384]{2,1,0:T(8,128)S(1)}) custom-call(s32[3]{0:T(128)S(1)} %pad_add_fusion.place, bf16[256,1536]{1,0:T(8,128)(2,1)S(1)} %amp_of_slab.6.refs_0_, bf16[256,1536]{1,0:T(8,128)(2,1)S(1)} %amp_of_slab.10.refs_1_, bf16[256,1536]{1,0:T(8,128)(2,1)S(1)} %amp_of_slab.11.refs_2_, ...), custom_call_target="tpu_custom_call" | custom-call | flops 10000000 | bytes 10000 | tf_op jit(solution)/shard_map/mix/pallas_call | solution.py:186
  197.1 8.2 %local_term.1.gamma = bf16[1,1536,1536]{2,1,0:T(8,128)(2,1)} custom-call(s32[3]{0:T(128)S(1)} %pad_add_fusion.place, bf16[1536,1536]{1,0:T(8,128)(2,1)S(1)} %bitcast.11, bf16[1536,1536]{1,0:T(8,128)(2,1)S(1)} %get-tuple-element.249.weight, bf16[1536,1024]{1,0:T(8,128)(2,1)S(1)} %cross_term.2.kept, bf16[1536,1024]{1,0:T(8,128)(2,1)S(1)} %collective-permute-done.28.arrived), custom_call_target="tpu_custom_call" | custom-call | flops 4000000000 | bytes 10000 | tf_op jit(solution)/shard_map/local_term/pallas_call | solution.py:271
  205.3 2.9 %local_rest.1.rest = bf16[1536,512]{1,0:T(8,128)(2,1)S(1)} custom-call(bf16[1536,1536]{1,0:T(8,128)(2,1)S(1)} %bitcast.11, bf16[1536,1536]{1,0:T(8,128)(2,1)S(1)} %get-tuple-element.249.weight), custom_call_target="tpu_custom_call" | custom-call | flops 5760000000 | bytes 10000 | tf_op jit(solution)/shard_map/local_rest/pallas_call | solution.py:301
  208.2 5.4 %collective-permute-done.29.arrived = bf16[1536,512]{1,0:T(8,128)(2,1)S(1)} collective-permute-done((bf16[1536,512]{1,0:T(8,128)(2,1)S(1)}, bf16[1536,512]{1,0:T(8,128)(2,1)S(1)}, u32[]{:S(2)}, u32[]{:S(2)}) %collective-permute-start.29) | collective-permute-done | bytes 1572896 | tf_op jit(solution)/shard_map/ppermute | solution.py:38
  (121 shorter events, 84.5 us)
Async XLA Ops:
  8.5 21.1 %collective-permute-start.3 = (bf16[1536,256]{1,0:T(8,128)(2,1)S(1)}, bf16[1536,256]{1,0:T(8,128)(2,1)S(1)}, u32[]{:S(2)}, u32[]{:S(2)}) collective-permute-start(bf16[1536,256]{1,0:T(8,128)(2,1)S(1)} %broadcast_select_fusion.4), channel_id=1, source_target_pairs={{0,8},{4,12},{8,0},{12,4},{1,9},{5,13},{9,1},{13,5},{2,10},{6,14},... | collective-permute-start | bytes 2359304 | tf_op jit(solution)/shard_map/ppermute | solution.py:38
  23.7 18.7 %collective-permute-start.2 = (bf16[256,1536]{1,0:T(8,128)(2,1)S(1)}, bf16[256,1536]{1,0:T(8,128)(2,1)S(1)}, u32[]{:S(2)}, u32[]{:S(2)}) collective-permute-start(bf16[256,1536]{1,0:T(8,128)(2,1)S(1)} %slab_product.6.left), channel_id=1, source_target_pairs={{0,1},{3,2},{4,5},{7,6},{8,9},{11,10},{12,13},{15,14},{16,17},{19,... | collective-permute-start | bytes 2359304 | tf_op jit(solution)/shard_map/ppermute | solution.py:38
  28.4 20.1 %collective-permute-start.6 = (bf16[1536,256]{1,0:T(8,128)(2,1)}, bf16[1536,256]{1,0:T(8,128)(2,1)S(1)}, u32[]{:S(2)}, u32[]{:S(2)}) collective-permute-start(bf16[1536,256]{1,0:T(8,128)(2,1)} %broadcast_select_fusion.3), channel_id=1, source_target_pairs={{0,8},{4,12},{8,0},{12,4},{1,9},{5,13},{9,1},{13,5},{2,10},{6,14},... | collective-permute-start | bytes 2359304 | tf_op jit(solution)/shard_map/ppermute | solution.py:38
  33.4 26.2 %collective-permute-start.5 = (bf16[256,1536]{1,0:T(8,128)(2,1)S(1)}, bf16[256,1536]{1,0:T(8,128)(2,1)}, u32[]{:S(2)}, u32[]{:S(2)}) collective-permute-start(bf16[256,1536]{1,0:T(8,128)(2,1)S(1)} %slab_product.7.left), channel_id=1, source_target_pairs={{0,1},{3,2},{4,5},{7,6},{8,9},{11,10},{12,13},{15,14},{16,17},{19,... | collective-permute-start | bytes 2359304 | tf_op jit(solution)/shard_map/ppermute | solution.py:38
  43.5 18.5 %collective-permute-start.4 = (bf16[256,1536]{1,0:T(8,128)(2,1)}, bf16[256,1536]{1,0:T(8,128)(2,1)}, u32[]{:S(2)}, u32[]{:S(2)}) collective-permute-start(bf16[256,1536]{1,0:T(8,128)(2,1)} %half_sum.6.left), channel_id=1, source_target_pairs={{1,2},{2,1},{5,6},{6,5},{9,10},{10,9},{13,14},{14,13},{17,18},{18,... | collective-permute-start | bytes 2359304 | tf_op jit(solution)/shard_map/ppermute | solution.py:38
  45.1 20.6 %collective-permute-start.10 = (bf16[1536,256]{1,0:T(8,128)(2,1)}, bf16[1536,256]{1,0:T(8,128)(2,1)S(1)}, u32[]{:S(2)}, u32[]{:S(2)}) collective-permute-start(bf16[1536,256]{1,0:T(8,128)(2,1)} %broadcast_select_fusion.2), channel_id=1, source_target_pairs={{0,8},{4,12},{8,0},{12,4},{1,9},{5,13},{9,1},{13,5},{2,10},{6,14},... | collective-permute-start | bytes 2359304 | tf_op jit(solution)/shard_map/ppermute | solution.py:38
  53.6 23.0 %collective-permute-start.9 = (bf16[256,1536]{1,0:T(8,128)(2,1)S(1)}, bf16[256,1536]{1,0:T(8,128)(2,1)S(1)}, u32[]{:S(2)}, u32[]{:S(2)}) collective-permute-start(bf16[256,1536]{1,0:T(8,128)(2,1)S(1)} %slab_product.8.left), channel_id=1, source_target_pairs={{0,1},{3,2},{4,5},{7,6},{8,9},{11,10},{12,13},{15,14},{16,17},{19,... | collective-permute-start | bytes 2359304 | tf_op jit(solution)/shard_map/ppermute | solution.py:38
  61.0 16.6 %collective-permute-start.8 = (bf16[256,1536]{1,0:T(8,128)(2,1)S(1)}, bf16[256,1536]{1,0:T(8,128)(2,1)S(1)}, u32[]{:S(2)}, u32[]{:S(2)}) collective-permute-start(bf16[256,1536]{1,0:T(8,128)(2,1)S(1)} %half_sum.7.left), channel_id=1, source_target_pairs={{1,2},{2,1},{5,6},{6,5},{9,10},{10,9},{13,14},{14,13},{17,18},{18,... | collective-permute-start | bytes 2359304 | tf_op jit(solution)/shard_map/ppermute | solution.py:38
  68.5 23.8 %collective-permute-start.14 = (bf16[256,1536]{1,0:T(8,128)(2,1)S(1)}, bf16[256,1536]{1,0:T(8,128)(2,1)S(1)}, u32[]{:S(2)}, u32[]{:S(2)}) collective-permute-start(bf16[256,1536]{1,0:T(8,128)(2,1)S(1)} %slab_product.9.left), channel_id=1, source_target_pairs={{0,1},{3,2},{4,5},{7,6},{8,9},{11,10},{12,13},{15,14},{16,17},{19,... | collective-permute-start | bytes 2359304 | tf_op jit(solution)/shard_map/ppermute | solution.py:38
  76.8 16.4 %collective-permute-start.13 = (bf16[256,1536]{1,0:T(8,128)(2,1)S(1)}, bf16[256,1536]{1,0:T(8,128)(2,1)S(1)}, u32[]{:S(2)}, u32[]{:S(2)}) collective-permute-start(bf16[256,1536]{1,0:T(8,128)(2,1)S(1)} %half_sum.8.left), channel_id=1, source_target_pairs={{1,2},{2,1},{5,6},{6,5},{9,10},{10,9},{13,14},{14,13},{17,18},{18,... | collective-permute-start | bytes 2359304 | tf_op jit(solution)/shard_map/ppermute | solution.py:38
  79.1 19.9 %collective-permute-start.12 = (bf16[256,1536]{1,0:T(8,128)(2,1)S(1)}, bf16[256,1536]{1,0:T(8,128)(2,1)S(1)}, u32[]{:S(2)}, u32[]{:S(2)}) collective-permute-start(bf16[256,1536]{1,0:T(8,128)(2,1)S(1)} %amplitude.7.left), channel_id=1, source_target_pairs={{1,0},{2,3},{5,4},{6,7},{9,8},{10,11},{13,12},{14,15},{17,16},{18,... | collective-permute-start | bytes 2359304 | tf_op jit(solution)/shard_map/ppermute | solution.py:38
  84.3 24.9 %collective-permute-start.11 = (bf16[256,1536]{1,0:T(8,128)(2,1)S(1)}, bf16[256,1536]{1,0:T(8,128)(2,1)S(1)}, u32[]{:S(2)}, u32[]{:S(2)}) collective-permute-start(bf16[256,1536]{1,0:T(8,128)(2,1)S(1)} %slab_product.10.left), channel_id=1, source_target_pairs={{0,1},{3,2},{4,5},{7,6},{8,9},{11,10},{12,13},{15,14},{16,17},{19,... | collective-permute-start | bytes 2359304 | tf_op jit(solution)/shard_map/ppermute | solution.py:38
  92.5 17.6 %collective-permute-start.18 = (bf16[256,1536]{1,0:T(8,128)(2,1)S(1)}, bf16[256,1536]{1,0:T(8,128)(2,1)S(1)}, u32[]{:S(2)}, u32[]{:S(2)}) collective-permute-start(bf16[256,1536]{1,0:T(8,128)(2,1)S(1)} %half_sum.9.left), channel_id=1, source_target_pairs={{1,2},{2,1},{5,6},{6,5},{9,10},{10,9},{13,14},{14,13},{17,18},{18,... | collective-permute-start | bytes 2359304 | tf_op jit(solution)/shard_map/ppermute | solution.py:38
  103.7 22.3 %collective-permute-start.16 = (bf16[256,1536]{1,0:T(8,128)(2,1)S(1)}, bf16[256,1536]{1,0:T(8,128)(2,1)S(1)}, u32[]{:S(2)}, u32[]{:S(2)}) collective-permute-start(bf16[256,1536]{1,0:T(8,128)(2,1)S(1)} %slab_product.11.left), channel_id=1, source_target_pairs={{0,1},{3,2},{4,5},{7,6},{8,9},{11,10},{12,13},{15,14},{16,17},{19,... | collective-permute-start | bytes 2359304 | tf_op jit(solution)/shard_map/ppermute | solution.py:38
  109.4 16.9 %collective-permute-start.15 = (bf16[256,1536]{1,0:T(8,128)(2,1)S(1)}, bf16[256,1536]{1,0:T(8,128)(2,1)S(1)}, u32[]{:S(2)}, u32[]{:S(2)}) collective-permute-start(bf16[256,1536]{1,0:T(8,128)(2,1)S(1)} %half_sum.10.left), channel_id=1, source_target_pairs={{1,2},{2,1},{5,6},{6,5},{9,10},{10,9},{13,14},{14,13},{17,18},{18,... | collective-permute-start | bytes 2359304 | tf_op jit(solution)/shard_map/ppermute | solution.py:38
  111.7 21.0 %collective-permute-start.20 = (bf16[256,1536]{1,0:T(8,128)(2,1)S(1)}, bf16[256,1536]{1,0:T(8,128)(2,1)S(1)}, u32[]{:S(2)}, u32[]{:S(2)}) collective-permute-start(bf16[256,1536]{1,0:T(8,128)(2,1)S(1)} %amplitude.9.left), channel_id=1, source_target_pairs={{1,0},{2,3},{5,4},{6,7},{9,8},{10,11},{13,12},{14,15},{17,16},{18,... | collective-permute-start | bytes 2359304 | tf_op jit(solution)/shard_map/ppermute | solution.py:38
  142.3 22.2 %collective-permute-start.23 = (bf16[256,1536]{1,0:T(8,128)(2,1)S(1)}, bf16[256,1536]{1,0:T(8,128)(2,1)S(1)}, u32[]{:S(2)}, u32[]{:S(2)}) collective-permute-start(bf16[256,1536]{1,0:T(8,128)(2,1)S(1)} %half_sum.11.left), channel_id=1, source_target_pairs={{1,2},{2,1},{5,6},{6,5},{9,10},{10,9},{13,14},{14,13},{17,18},{18,... | collective-permute-start | bytes 2359304 | tf_op jit(solution)/shard_map/ppermute | solution.py:38
  143.0 20.9 %collective-permute-start.19 = (bf16[256,1536]{1,0:T(8,128)(2,1)S(1)}, bf16[256,1536]{1,0:T(8,128)(2,1)S(1)}, u32[]{:S(2)}, u32[]{:S(2)}) collective-permute-start(bf16[256,1536]{1,0:T(8,128)(2,1)S(1)} %amplitude.10.left), channel_id=1, source_target_pairs={{1,0},{2,3},{5,4},{6,7},{9,8},{10,11},{13,12},{14,15},{17,16},{18,... | collective-permute-start | bytes 2359304 | tf_op jit(solution)/shard_map/ppermute | solution.py:38
  155.5 41.6 %collective-permute-start.28 = (bf16[1536,1024]{1,0:T(8,128)(2,1)S(1)}, bf16[1536,1024]{1,0:T(8,128)(2,1)S(1)}, u32[]{:S(2)}, u32[]{:S(2)}) collective-permute-start(bf16[1536,1024]{1,0:T(8,128)(2,1)S(1)} %cross_term.2.kept), channel_id=1, source_target_pairs={{4,12},{12,4},{5,13},{13,5},{6,14},{14,6},{7,15},{15,7},{20,28},{2... | collective-permute-start | bytes 9437192 | tf_op jit(solution)/shard_map/ppermute | solution.py:38
  166.1 20.6 %collective-permute-start.24 = (bf16[256,1536]{1,0:T(8,128)(2,1)S(1)}, bf16[256,1536]{1,0:T(8,128)(2,1)S(1)}, u32[]{:S(2)}, u32[]{:S(2)}) collective-permute-start(bf16[256,1536]{1,0:T(8,128)(2,1)S(1)} %amplitude.11.left), channel_id=1, source_target_pairs={{1,0},{2,3},{5,4},{6,7},{9,8},{10,11},{13,12},{14,15},{17,16},{18,... | collective-permute-start | bytes 2359304 | tf_op jit(solution)/shard_map/ppermute | solution.py:38
  167.4 24.6 %collective-permute-start.25 = (bf16[256,1536]{1,0:T(8,128)(2,1)S(1)}, bf16[256,1536]{1,0:T(8,128)(2,1)S(1)}, u32[]{:S(2)}, u32[]{:S(2)}) collective-permute-start(bf16[256,1536]{1,0:T(8,128)(2,1)S(1)} %amp_of_slab.6.refs_0_), channel_id=1, source_target_pairs={{0,4},{4,0},{8,12},{12,8},{1,5},{5,1},{9,13},{13,9},{2,6},{6,2},{1... | collective-permute-start | bytes 2359304 | tf_op jit(solution)/shard_map/ppermute | solution.py:38
  167.8 24.2 %collective-permute-start.26 = (bf16[256,1536]{1,0:T(8,128)(2,1)S(1)}, bf16[256,1536]{1,0:T(8,128)(2,1)S(1)}, u32[]{:S(2)}, u32[]{:S(2)}) collective-permute-start(bf16[256,1536]{1,0:T(8,128)(2,1)S(1)} %amp_of_slab.10.refs_1_), channel_id=1, source_target_pairs={{0,4},{4,0},{8,12},{12,8},{1,5},{5,1},{9,13},{13,9},{2,6},{6,2},{1... | collective-permute-start | bytes 2359304 | tf_op jit(solution)/shard_map/ppermute | solution.py:38
  188.6 25.0 %collective-permute-start.29 = (bf16[1536,512]{1,0:T(8,128)(2,1)S(1)}, bf16[1536,512]{1,0:T(8,128)(2,1)S(1)}, u32[]{:S(2)}, u32[]{:S(2)}) collective-permute-start(bf16[1536,512]{1,0:T(8,128)(2,1)S(1)} %cross_term.3.kept), channel_id=1, source_target_pairs={{4,12},{12,4},{5,13},{13,5},{6,14},{14,6},{7,15},{15,7},{20,28},{2... | collective-permute-start | bytes 4718600 | tf_op jit(solution)/shard_map/ppermute | solution.py:38
  196.7 20.0 %collective-permute-start.30 = (bf16[384,384]{1,0:T(8,128)(2,1)S(1)}, bf16[384,384]{1,0:T(8,128)(2,1)S(1)}, u32[]{:S(2)}, u32[]{:S(2)}) collective-permute-start(bf16[384,384]{1,0:T(8,128)(2,1)S(1)} %fusion), channel_id=1, source_target_pairs={{0,8},{4,12},{8,0},{12,4},{1,9},{5,13},{9,1},{13,5},{2,10},{6,14},... | collective-permute-start | bytes 884744 | tf_op jit(solution)/shard_map/ppermute | solution.py:38
  (21 other events, 199.5 us)

commit v8 on v7

--- a/solution.py
+++ b/solution.py
@@ -182,7 +182,7 @@
 def mix(place, own, other, straight_core, slabs, count):
     nvirt = own[0].shape[1]
     rows, cols, chips = nvirt // slabs, nvirt // count, count // 2
-    band = 256
+    band = 512
     return pl.pallas_call(
         functools.partial(mix_kernel, len(own), nvirt // 2, band, rows, cols, straight_core),
         grid_spec=pltpu.PrefetchScalarGridSpec(

time: 218 us -> 218 us (level)
  no operation moved by 1% of the time
where the time goes in v8:
time: 218 us
  starting transfers between devices  69.5 us (32%)
  Pallas kernels  66 us (30%)
  waiting for transfers between devices  65 us (30%)
  local copies, waits for them, and re-layouts  8.01 us (4%)
  other arithmetic  7.7 us (4%)
    ppermute x31, starting transfers between devices, send(): return lax.ppermute(self.ready(value, *others)[0], axis, pairs)  69.5 us
    ppermute x31, waiting for transfers between devices, send(): return lax.ppermute(self.ready(value, *others)[0], axis, pairs)  65 us
    pallas_call x6, Pallas kernels, product_rows(): pl.pallas_call(product_kernel, grid_spec=pltpu.PrefetchScalarGridSpec(num...  16.6 us
    pallas_call x6, Pallas kernels, amplitude(): pl.pallas_call(amp_kernel, grid_spec=pltpu.PrefetchScalarGridSpec(num_sca...  10.2 us
    pallas_call x2, Pallas kernels, cross_columns(): pl.pallas_call(cross_kernel, grid_spec=pltpu.PrefetchScalarGridSpec(num_s...  10.2 us
    pallas_call x2, Pallas kernels, mix(): pl.pallas_call(functools.partial(mix_kernel, len(own), nvirt // 2, band,...  8.82 us
    pallas_call x1, Pallas kernels, final_columns(): pl.pallas_call(final_kernel, grid_spec=pltpu.PrefetchScalarGridSpec(num_s...  8.17 us
    unnamed x30, local copies, waits for them, and re-layouts  4.77 us
  transfers between devices with their start and end apart: 31, of which 14 were waited for; matrix products, arithmetic and copies ran while one was open for 4% of the time, Pallas kernels for 30%

profile of v8, /device:TPU:1, one launch (start us, length us, event | category | flops | bytes accessed | tf_op | source)
XLA Modules:
  0.0 217.5 jit_solution(1371510281632819898)
XLA Ops:
  11.2 5.1 %collective-permute-done.1.partner = bf16[1536,1536]{1,0:T(8,128)(2,1)S(1)} collective-permute-done((bf16[1536,1536]{1,0:T(8,128)(2,1)}, bf16[1536,1536]{1,0:T(8,128)(2,1)S(1)}, u32[]{:S(2)}, u32[]{:S(2)}) %collective-permute-start.1) | collective-permute-done | bytes 4718624 | tf_op jit(solution)/shard_map/ppermute | solution.py:38
  23.7 4.7 %collective-permute-start.2 = (bf16[256,1536]{1,0:T(8,128)(2,1)S(1)}, bf16[256,1536]{1,0:T(8,128)(2,1)S(1)}, u32[]{:S(2)}, u32[]{:S(2)}) collective-permute-start(bf16[256,1536]{1,0:T(8,128)(2,1)S(1)} %slab_product.6.left), channel_id=1, source_target_pairs={{0,1},{3,2},{4,5},{7,6},{8,9},{11,10},{12,13},{15,14},{16,17},{19,... | collective-permute-start | bytes 2359304 | tf_op jit(solution)/shard_map/ppermute | solution.py:38
  33.4 3.6 %collective-permute-start.5 = (bf16[256,1536]{1,0:T(8,128)(2,1)S(1)}, bf16[256,1536]{1,0:T(8,128)(2,1)}, u32[]{:S(2)}, u32[]{:S(2)}) collective-permute-start(bf16[256,1536]{1,0:T(8,128)(2,1)S(1)} %slab_product.7.left), channel_id=1, source_target_pairs={{0,1},{3,2},{4,5},{7,6},{8,9},{11,10},{12,13},{15,14},{16,17},{19,... | collective-permute-start | bytes 2359304 | tf_op jit(solution)/shard_map/ppermute | solution.py:38
  37.1 5.4 %collective-permute-done.2.right = bf16[256,1536]{1,0:T(8,128)(2,1)S(1)} collective-permute-done((bf16[256,1536]{1,0:T(8,128)(2,1)S(1)}, bf16[256,1536]{1,0:T(8,128)(2,1)S(1)}, u32[]{:S(2)}, u32[]{:S(2)}) %collective-permute-start.2) | collective-permute-done | bytes 786464 | tf_op jit(solution)/shard_map/ppermute | solution.py:38
  53.6 6.0 %collective-permute-start.9 = (bf16[256,1536]{1,0:T(8,128)(2,1)S(1)}, bf16[256,1536]{1,0:T(8,128)(2,1)S(1)}, u32[]{:S(2)}, u32[]{:S(2)}) collective-permute-start(bf16[256,1536]{1,0:T(8,128)(2,1)S(1)} %slab_product.8.left), channel_id=1, source_target_pairs={{0,1},{3,2},{4,5},{7,6},{8,9},{11,10},{12,13},{15,14},{16,17},{19,... | collective-permute-start | bytes 2359304 | tf_op jit(solution)/shard_map/ppermute | solution.py:38
  68.5 6.5 %collective-permute-start.14 = (bf16[256,1536]{1,0:T(8,128)(2,1)S(1)}, bf16[256,1536]{1,0:T(8,128)(2,1)S(1)}, u32[]{:S(2)}, u32[]{:S(2)}) collective-permute-start(bf16[256,1536]{1,0:T(8,128)(2,1)S(1)} %slab_product.9.left), channel_id=1, source_target_pairs={{0,1},{3,2},{4,5},{7,6},{8,9},{11,10},{12,13},{15,14},{16,17},{19,... | collective-permute-start | bytes 2359304 | tf_op jit(solution)/shard_map/ppermute | solution.py:38
  84.3 4.7 %collective-permute-start.11 = (bf16[256,1536]{1,0:T(8,128)(2,1)S(1)}, bf16[256,1536]{1,0:T(8,128)(2,1)S(1)}, u32[]{:S(2)}, u32[]{:S(2)}) collective-permute-start(bf16[256,1536]{1,0:T(8,128)(2,1)S(1)} %slab_product.10.left), channel_id=1, source_target_pairs={{0,1},{3,2},{4,5},{7,6},{8,9},{11,10},{12,13},{15,14},{16,17},{19,... | collective-permute-start | bytes 2359304 | tf_op jit(solution)/shard_map/ppermute | solution.py:38
  89.0 3.4 %collective-permute-done.14.right = bf16[256,1536]{1,0:T(8,128)(2,1)S(1)} collective-permute-done((bf16[256,1536]{1,0:T(8,128)(2,1)S(1)}, bf16[256,1536]{1,0:T(8,128)(2,1)S(1)}, u32[]{:S(2)}, u32[]{:S(2)}) %collective-permute-start.14) | collective-permute-done | bytes 786464 | tf_op jit(solution)/shard_map/ppermute | solution.py:38
  94.8 4.2 %collective-permute-done.12.right = bf16[256,1536]{1,0:T(8,128)(2,1)S(1)} collective-permute-done((bf16[256,1536]{1,0:T(8,128)(2,1)S(1)}, bf16[256,1536]{1,0:T(8,128)(2,1)S(1)}, u32[]{:S(2)}, u32[]{:S(2)}) %collective-permute-start.12) | collective-permute-done | bytes 786464 | tf_op jit(solution)/shard_map/ppermute | solution.py:38
  103.7 4.1 %collective-permute-start.16 = (bf16[256,1536]{1,0:T(8,128)(2,1)S(1)}, bf16[256,1536]{1,0:T(8,128)(2,1)S(1)}, u32[]{:S(2)}, u32[]{:S(2)}) collective-permute-start(bf16[256,1536]{1,0:T(8,128)(2,1)S(1)} %slab_product.11.left), channel_id=1, source_target_pairs={{0,1},{3,2},{4,5},{7,6},{8,9},{11,10},{12,13},{15,14},{16,17},{19,... | collective-permute-start | bytes 2359304 | tf_op jit(solution)/shard_map/ppermute | solution.py:38
  115.8 10.3 %collective-permute-done.16.right = bf16[256,1536]{1,0:T(8,128)(2,1)S(1)} collective-permute-done((bf16[256,1536]{1,0:T(8,128)(2,1)S(1)}, bf16[256,1536]{1,0:T(8,128)(2,1)S(1)}, u32[]{:S(2)}, u32[]{:S(2)}) %collective-permute-start.16) | collective-permute-done | bytes 786464 | tf_op jit(solution)/shard_map/ppermute | solution.py:38
  127.8 4.9 %collective-permute-done.20.right = bf16[256,1536]{1,0:T(8,128)(2,1)S(1)} collective-permute-done((bf16[256,1536]{1,0:T(8,128)(2,1)S(1)}, bf16[256,1536]{1,0:T(8,128)(2,1)S(1)}, u32[]{:S(2)}, u32[]{:S(2)}) %collective-permute-start.20) | collective-permute-done | bytes 786464 | tf_op jit(solution)/shard_map/ppermute | solution.py:38
  133.4 6.6 %collective-permute-start.21 = (bf16[768,1536]{1,0:T(8,128)(2,1)S(1)}, bf16[768,1536]{1,0:T(8,128)(2,1)S(1)}, u32[]{:S(2)}, u32[]{:S(2)}) collective-permute-start(bf16[768,1536]{1,0:T(8,128)(2,1)S(1)} %amp_of_slab.9.refs_0_), channel_id=1, source_target_pairs={{0,4},{4,0},{8,12},{12,8},{1,5},{5,1},{9,13},{13,9},{2,6},{6,2},{1... | collective-permute-start | bytes 7077896 | tf_op jit(solution)/shard_map/ppermute | solution.py:38
  144.3 4.4 %mix.2 = (bf16[1536,1536]{1,0:T(8,128)(2,1)S(1)}, f32[2,384,384]{2,1,0:T(8,128)S(1)}) custom-call(s32[3]{0:T(128)S(1)} %pad_add_fusion.place, bf16[768,1536]{1,0:T(8,128)(2,1)S(1)} %amp_of_slab.9.refs_0_, bf16[768,1536]{1,0:T(8,128)(2,1)S(1)} %collective-permute-done.21.refs_1_), custom_call_target="tpu_custom_call" | custom-call | flops 10000000 | bytes 10000 | tf_op jit(solution)/shard_map/mix/pallas_call | solution.py:186
  148.8 6.7 %cross_term.2.kept = bf16[1536,1024]{1,0:T(8,128)(2,1)S(1)} custom-call(s32[3]{0:T(128)S(1)} %pad_add_fusion.place, bf16[1536,768]{1,0:T(8,128)(2,1)S(1)} %constant_dynamic-update-slice_fusion.lower, bf16[1536,768]{1,0:T(8,128)(2,1)S(1)} %collective-permute-done.22.upper, bf16[1536,1536]{1,0:T(8,128)(2,1)S(1)} %bitcast.11, ...), custom_call_target="tpu_custom_call" | custom-call | flops 4000000000 | bytes 10000 | tf_op jit(solution)/shard_map/cross_term/pallas_call | solution.py:233
  155.5 3.2 %collective-permute-start.28 = (bf16[1536,1024]{1,0:T(8,128)(2,1)S(1)}, bf16[1536,1024]{1,0:T(8,128)(2,1)S(1)}, u32[]{:S(2)}, u32[]{:S(2)}) collective-permute-start(bf16[1536,1024]{1,0:T(8,128)(2,1)S(1)} %cross_term.2.kept), channel_id=1, source_target_pairs={{4,12},{12,4},{5,13},{13,5},{6,14},{14,6},{7,15},{15,7},{20,28},{2... | collective-permute-start | bytes 9437192 | tf_op jit(solution)/shard_map/ppermute | solution.py:38
  158.6 5.3 %collective-permute-done.19.right = bf16[256,1536]{1,0:T(8,128)(2,1)S(1)} collective-permute-done((bf16[256,1536]{1,0:T(8,128)(2,1)S(1)}, bf16[256,1536]{1,0:T(8,128)(2,1)S(1)}, u32[]{:S(2)}, u32[]{:S(2)}) %collective-permute-start.19) | collective-permute-done | bytes 786464 | tf_op jit(solution)/shard_map/ppermute | solution.py:38
  167.9 3.5 %cross_term.3.kept = bf16[1536,512]{1,0:T(8,128)(2,1)S(1)} custom-call(s32[3]{0:T(128)S(1)} %pad_add_fusion.place, bf16[1536,768]{1,0:T(8,128)(2,1)S(1)} %constant_dynamic-update-slice_fusion.lower, bf16[1536,768]{1,0:T(8,128)(2,1)S(1)} %collective-permute-done.22.upper, bf16[1536,1536]{1,0:T(8,128)(2,1)S(1)} %bitcast.11, ...), custom_call_target="tpu_custom_call" | custom-call | flops 4000000000 | bytes 10000 | tf_op jit(solution)/shard_map/cross_term/pallas_call | solution.py:233
  171.4 15.3 %collective-permute-done.24.right = bf16[256,1536]{1,0:T(8,128)(2,1)S(1)} collective-permute-done((bf16[256,1536]{1,0:T(8,128)(2,1)S(1)}, bf16[256,1536]{1,0:T(8,128)(2,1)S(1)}, u32[]{:S(2)}, u32[]{:S(2)}) %collective-permute-start.24) | collective-permute-done | bytes 786464 | tf_op jit(solution)/shard_map/ppermute | solution.py:38
  188.6 3.4 %collective-permute-start.29 = (bf16[1536,512]{1,0:T(8,128)(2,1)S(1)}, bf16[1536,512]{1,0:T(8,128)(2,1)S(1)}, u32[]{:S(2)}, u32[]{:S(2)}) collective-permute-start(bf16[1536,512]{1,0:T(8,128)(2,1)S(1)} %cross_term.3.kept), channel_id=1, source_target_pairs={{4,12},{12,4},{5,13},{13,5},{6,14},{14,6},{7,15},{15,7},{20,28},{2... | collective-permute-start | bytes 4718600 | tf_op jit(solution)/shard_map/ppermute | solution.py:38
  192.0 4.4 %mix.3 = (bf16[1536,1536]{1,0:T(8,128)(2,1)S(1)}, f32[2,384,384]{2,1,0:T(8,128)S(1)}) custom-call(s32[3]{0:T(128)S(1)} %pad_add_fusion.place, bf16[256,1536]{1,0:T(8,128)(2,1)S(1)} %amp_of_slab.6.refs_0_, bf16[256,1536]{1,0:T(8,128)(2,1)S(1)} %amp_of_slab.10.refs_1_, bf16[256,1536]{1,0:T(8,128)(2,1)S(1)} %amp_of_slab.11.refs_2_, ...), custom_call_target="tpu_custom_call" | custom-call | flops 10000000 | bytes 10000 | tf_op jit(solution)/shard_map/mix/pallas_call | solution.py:186
  197.0 8.2 %local_term.1.gamma = bf16[1,1536,1536]{2,1,0:T(8,128)(2,1)} custom-call(s32[3]{0:T(128)S(1)} %pad_add_fusion.place, bf16[1536,1536]{1,0:T(8,128)(2,1)S(1)} %bitcast.11, bf16[1536,1536]{1,0:T(8,128)(2,1)S(1)} %get-tuple-element.249.weight, bf16[1536,1024]{1,0:T(8,128)(2,1)S(1)} %cross_term.2.kept, bf16[1536,1024]{1,0:T(8,128)(2,1)S(1)} %collective-permute-done.28.arrived), custom_call_target="tpu_custom_call" | custom-call | flops 4000000000 | bytes 10000 | tf_op jit(solution)/shard_map/local_term/pallas_call | solution.py:271
  205.2 2.9 %local_rest.1.rest = bf16[1536,512]{1,0:T(8,128)(2,1)S(1)} custom-call(bf16[1536,1536]{1,0:T(8,128)(2,1)S(1)} %bitcast.11, bf16[1536,1536]{1,0:T(8,128)(2,1)S(1)} %get-tuple-element.249.weight), custom_call_target="tpu_custom_call" | custom-call | flops 5760000000 | bytes 10000 | tf_op jit(solution)/shard_map/local_rest/pallas_call | solution.py:301
  208.1 5.4 %collective-permute-done.29.arrived = bf16[1536,512]{1,0:T(8,128)(2,1)S(1)} collective-permute-done((bf16[1536,512]{1,0:T(8,128)(2,1)S(1)}, bf16[1536,512]{1,0:T(8,128)(2,1)S(1)}, u32[]{:S(2)}, u32[]{:S(2)}) %collective-permute-start.29) | collective-permute-done | bytes 1572896 | tf_op jit(solution)/shard_map/ppermute | solution.py:38
  (121 shorter events, 84.5 us)
Async XLA Ops:
  8.5 21.1 %collective-permute-start.3 = (bf16[1536,256]{1,0:T(8,128)(2,1)S(1)}, bf16[1536,256]{1,0:T(8,128)(2,1)S(1)}, u32[]{:S(2)}, u32[]{:S(2)}) collective-permute-start(bf16[1536,256]{1,0:T(8,128)(2,1)S(1)} %broadcast_select_fusion.4), channel_id=1, source_target_pairs={{0,8},{4,12},{8,0},{12,4},{1,9},{5,13},{9,1},{13,5},{2,10},{6,14},... | collective-permute-start | bytes 2359304 | tf_op jit(solution)/shard_map/ppermute | solution.py:38
  23.7 18.7 %collective-permute-start.2 = (bf16[256,1536]{1,0:T(8,128)(2,1)S(1)}, bf16[256,1536]{1,0:T(8,128)(2,1)S(1)}, u32[]{:S(2)}, u32[]{:S(2)}) collective-permute-start(bf16[256,1536]{1,0:T(8,128)(2,1)S(1)} %slab_product.6.left), channel_id=1, source_target_pairs={{0,1},{3,2},{4,5},{7,6},{8,9},{11,10},{12,13},{15,14},{16,17},{19,... | collective-permute-start | bytes 2359304 | tf_op jit(solution)/shard_map/ppermute | solution.py:38
  28.4 20.1 %collective-permute-start.6 = (bf16[1536,256]{1,0:T(8,128)(2,1)}, bf16[1536,256]{1,0:T(8,128)(2,1)S(1)}, u32[]{:S(2)}, u32[]{:S(2)}) collective-permute-start(bf16[1536,256]{1,0:T(8,128)(2,1)} %broadcast_select_fusion.3), channel_id=1, source_target_pairs={{0,8},{4,12},{8,0},{12,4},{1,9},{5,13},{9,1},{13,5},{2,10},{6,14},... | collective-permute-start | bytes 2359304 | tf_op jit(solution)/shard_map/ppermute | solution.py:38
  33.4 26.2 %collective-permute-start.5 = (bf16[256,1536]{1,0:T(8,128)(2,1)S(1)}, bf16[256,1536]{1,0:T(8,128)(2,1)}, u32[]{:S(2)}, u32[]{:S(2)}) collective-permute-start(bf16[256,1536]{1,0:T(8,128)(2,1)S(1)} %slab_product.7.left), channel_id=1, source_target_pairs={{0,1},{3,2},{4,5},{7,6},{8,9},{11,10},{12,13},{15,14},{16,17},{19,... | collective-permute-start | bytes 2359304 | tf_op jit(solution)/shard_map/ppermute | solution.py:38
  43.5 18.5 %collective-permute-start.4 = (bf16[256,1536]{1,0:T(8,128)(2,1)}, bf16[256,1536]{1,0:T(8,128)(2,1)}, u32[]{:S(2)}, u32[]{:S(2)}) collective-permute-start(bf16[256,1536]{1,0:T(8,128)(2,1)} %half_sum.6.left), channel_id=1, source_target_pairs={{1,2},{2,1},{5,6},{6,5},{9,10},{10,9},{13,14},{14,13},{17,18},{18,... | collective-permute-start | bytes 2359304 | tf_op jit(solution)/shard_map/ppermute | solution.py:38
  45.1 20.6 %collective-permute-start.10 = (bf16[1536,256]{1,0:T(8,128)(2,1)}, bf16[1536,256]{1,0:T(8,128)(2,1)S(1)}, u32[]{:S(2)}, u32[]{:S(2)}) collective-permute-start(bf16[1536,256]{1,0:T(8,128)(2,1)} %broadcast_select_fusion.2), channel_id=1, source_target_pairs={{0,8},{4,12},{8,0},{12,4},{1,9},{5,13},{9,1},{13,5},{2,10},{6,14},... | collective-permute-start | bytes 2359304 | tf_op jit(solution)/shard_map/ppermute | solution.py:38
  53.6 23.0 %collective-permute-start.9 = (bf16[256,1536]{1,0:T(8,128)(2,1)S(1)}, bf16[256,1536]{1,0:T(8,128)(2,1)S(1)}, u32[]{:S(2)}, u32[]{:S(2)}) collective-permute-start(bf16[256,1536]{1,0:T(8,128)(2,1)S(1)} %slab_product.8.left), channel_id=1, source_target_pairs={{0,1},{3,2},{4,5},{7,6},{8,9},{11,10},{12,13},{15,14},{16,17},{19,... | collective-permute-start | bytes 2359304 | tf_op jit(solution)/shard_map/ppermute | solution.py:38
  61.0 16.6 %collective-permute-start.8 = (bf16[256,1536]{1,0:T(8,128)(2,1)S(1)}, bf16[256,1536]{1,0:T(8,128)(2,1)S(1)}, u32[]{:S(2)}, u32[]{:S(2)}) collective-permute-start(bf16[256,1536]{1,0:T(8,128)(2,1)S(1)} %half_sum.7.left), channel_id=1, source_target_pairs={{1,2},{2,1},{5,6},{6,5},{9,10},{10,9},{13,14},{14,13},{17,18},{18,... | collective-permute-start | bytes 2359304 | tf_op jit(solution)/shard_map/ppermute | solution.py:38
  68.5 23.8 %collective-permute-start.14 = (bf16[256,1536]{1,0:T(8,128)(2,1)S(1)}, bf16[256,1536]{1,0:T(8,128)(2,1)S(1)}, u32[]{:S(2)}, u32[]{:S(2)}) collective-permute-start(bf16[256,1536]{1,0:T(8,128)(2,1)S(1)} %slab_product.9.left), channel_id=1, source_target_pairs={{0,1},{3,2},{4,5},{7,6},{8,9},{11,10},{12,13},{15,14},{16,17},{19,... | collective-permute-start | bytes 2359304 | tf_op jit(solution)/shard_map/ppermute | solution.py:38
  76.8 16.4 %collective-permute-start.13 = (bf16[256,1536]{1,0:T(8,128)(2,1)S(1)}, bf16[256,1536]{1,0:T(8,128)(2,1)S(1)}, u32[]{:S(2)}, u32[]{:S(2)}) collective-permute-start(bf16[256,1536]{1,0:T(8,128)(2,1)S(1)} %half_sum.8.left), channel_id=1, source_target_pairs={{1,2},{2,1},{5,6},{6,5},{9,10},{10,9},{13,14},{14,13},{17,18},{18,... | collective-permute-start | bytes 2359304 | tf_op jit(solution)/shard_map/ppermute | solution.py:38
  79.1 19.9 %collective-permute-start.12 = (bf16[256,1536]{1,0:T(8,128)(2,1)S(1)}, bf16[256,1536]{1,0:T(8,128)(2,1)S(1)}, u32[]{:S(2)}, u32[]{:S(2)}) collective-permute-start(bf16[256,1536]{1,0:T(8,128)(2,1)S(1)} %amplitude.7.left), channel_id=1, source_target_pairs={{1,0},{2,3},{5,4},{6,7},{9,8},{10,11},{13,12},{14,15},{17,16},{18,... | collective-permute-start | bytes 2359304 | tf_op jit(solution)/shard_map/ppermute | solution.py:38
  84.3 24.9 %collective-permute-start.11 = (bf16[256,1536]{1,0:T(8,128)(2,1)S(1)}, bf16[256,1536]{1,0:T(8,128)(2,1)S(1)}, u32[]{:S(2)}, u32[]{:S(2)}) collective-permute-start(bf16[256,1536]{1,0:T(8,128)(2,1)S(1)} %slab_product.10.left), channel_id=1, source_target_pairs={{0,1},{3,2},{4,5},{7,6},{8,9},{11,10},{12,13},{15,14},{16,17},{19,... | collective-permute-start | bytes 2359304 | tf_op jit(solution)/shard_map/ppermute | solution.py:38
  92.5 17.6 %collective-permute-start.18 = (bf16[256,1536]{1,0:T(8,128)(2,1)S(1)}, bf16[256,1536]{1,0:T(8,128)(2,1)S(1)}, u32[]{:S(2)}, u32[]{:S(2)}) collective-permute-start(bf16[256,1536]{1,0:T(8,128)(2,1)S(1)} %half_sum.9.left), channel_id=1, source_target_pairs={{1,2},{2,1},{5,6},{6,5},{9,10},{10,9},{13,14},{14,13},{17,18},{18,... | collective-permute-start | bytes 2359304 | tf_op jit(solution)/shard_map/ppermute | solution.py:38
  103.7 22.3 %collective-permute-start.16 = (bf16[256,1536]{1,0:T(8,128)(2,1)S(1)}, bf16[256,1536]{1,0:T(8,128)(2,1)S(1)}, u32[]{:S(2)}, u32[]{:S(2)}) collective-permute-start(bf16[256,1536]{1,0:T(8,128)(2,1)S(1)} %slab_product.11.left), channel_id=1, source_target_pairs={{0,1},{3,2},{4,5},{7,6},{8,9},{11,10},{12,13},{15,14},{16,17},{19,... | collective-permute-start | bytes 2359304 | tf_op jit(solution)/shard_map/ppermute | solution.py:38
  109.4 16.9 %collective-permute-start.15 = (bf16[256,1536]{1,0:T(8,128)(2,1)S(1)}, bf16[256,1536]{1,0:T(8,128)(2,1)S(1)}, u32[]{:S(2)}, u32[]{:S(2)}) collective-permute-start(bf16[256,1536]{1,0:T(8,128)(2,1)S(1)} %half_sum.10.left), channel_id=1, source_target_pairs={{1,2},{2,1},{5,6},{6,5},{9,10},{10,9},{13,14},{14,13},{17,18},{18,... | collective-permute-start | bytes 2359304 | tf_op jit(solution)/shard_map/ppermute | solution.py:38
  111.7 21.0 %collective-permute-start.20 = (bf16[256,1536]{1,0:T(8,128)(2,1)S(1)}, bf16[256,1536]{1,0:T(8,128)(2,1)S(1)}, u32[]{:S(2)}, u32[]{:S(2)}) collective-permute-start(bf16[256,1536]{1,0:T(8,128)(2,1)S(1)} %amplitude.9.left), channel_id=1, source_target_pairs={{1,0},{2,3},{5,4},{6,7},{9,8},{10,11},{13,12},{14,15},{17,16},{18,... | collective-permute-start | bytes 2359304 | tf_op jit(solution)/shard_map/ppermute | solution.py:38
  142.3 22.2 %collective-permute-start.23 = (bf16[256,1536]{1,0:T(8,128)(2,1)S(1)}, bf16[256,1536]{1,0:T(8,128)(2,1)S(1)}, u32[]{:S(2)}, u32[]{:S(2)}) collective-permute-start(bf16[256,1536]{1,0:T(8,128)(2,1)S(1)} %half_sum.11.left), channel_id=1, source_target_pairs={{1,2},{2,1},{5,6},{6,5},{9,10},{10,9},{13,14},{14,13},{17,18},{18,... | collective-permute-start | bytes 2359304 | tf_op jit(solution)/shard_map/ppermute | solution.py:38
  143.0 20.9 %collective-permute-start.19 = (bf16[256,1536]{1,0:T(8,128)(2,1)S(1)}, bf16[256,1536]{1,0:T(8,128)(2,1)S(1)}, u32[]{:S(2)}, u32[]{:S(2)}) collective-permute-start(bf16[256,1536]{1,0:T(8,128)(2,1)S(1)} %amplitude.10.left), channel_id=1, source_target_pairs={{1,0},{2,3},{5,4},{6,7},{9,8},{10,11},{13,12},{14,15},{17,16},{18,... | collective-permute-start | bytes 2359304 | tf_op jit(solution)/shard_map/ppermute | solution.py:38
  155.5 41.6 %collective-permute-start.28 = (bf16[1536,1024]{1,0:T(8,128)(2,1)S(1)}, bf16[1536,1024]{1,0:T(8,128)(2,1)S(1)}, u32[]{:S(2)}, u32[]{:S(2)}) collective-permute-start(bf16[1536,1024]{1,0:T(8,128)(2,1)S(1)} %cross_term.2.kept), channel_id=1, source_target_pairs={{4,12},{12,4},{5,13},{13,5},{6,14},{14,6},{7,15},{15,7},{20,28},{2... | collective-permute-start | bytes 9437192 | tf_op jit(solution)/shard_map/ppermute | solution.py:38
  166.1 20.6 %collective-permute-start.24 = (bf16[256,1536]{1,0:T(8,128)(2,1)S(1)}, bf16[256,1536]{1,0:T(8,128)(2,1)S(1)}, u32[]{:S(2)}, u32[]{:S(2)}) collective-permute-start(bf16[256,1536]{1,0:T(8,128)(2,1)S(1)} %amplitude.11.left), channel_id=1, source_target_pairs={{1,0},{2,3},{5,4},{6,7},{9,8},{10,11},{13,12},{14,15},{17,16},{18,... | collective-permute-start | bytes 2359304 | tf_op jit(solution)/shard_map/ppermute | solution.py:38
  167.4 24.6 %collective-permute-start.25 = (bf16[256,1536]{1,0:T(8,128)(2,1)S(1)}, bf16[256,1536]{1,0:T(8,128)(2,1)S(1)}, u32[]{:S(2)}, u32[]{:S(2)}) collective-permute-start(bf16[256,1536]{1,0:T(8,128)(2,1)S(1)} %amp_of_slab.6.refs_0_), channel_id=1, source_target_pairs={{0,4},{4,0},{8,12},{12,8},{1,5},{5,1},{9,13},{13,9},{2,6},{6,2},{1... | collective-permute-start | bytes 2359304 | tf_op jit(solution)/shard_map/ppermute | solution.py:38
  167.8 24.2 %collective-permute-start.26 = (bf16[256,1536]{1,0:T(8,128)(2,1)S(1)}, bf16[256,1536]{1,0:T(8,128)(2,1)S(1)}, u32[]{:S(2)}, u32[]{:S(2)}) collective-permute-start(bf16[256,1536]{1,0:T(8,128)(2,1)S(1)} %amp_of_slab.10.refs_1_), channel_id=1, source_target_pairs={{0,4},{4,0},{8,12},{12,8},{1,5},{5,1},{9,13},{13,9},{2,6},{6,2},{1... | collective-permute-start | bytes 2359304 | tf_op jit(solution)/shard_map/ppermute | solution.py:38
  188.6 24.9 %collective-permute-start.29 = (bf16[1536,512]{1,0:T(8,128)(2,1)S(1)}, bf16[1536,512]{1,0:T(8,128)(2,1)S(1)}, u32[]{:S(2)}, u32[]{:S(2)}) collective-permute-start(bf16[1536,512]{1,0:T(8,128)(2,1)S(1)} %cross_term.3.kept), channel_id=1, source_target_pairs={{4,12},{12,4},{5,13},{13,5},{6,14},{14,6},{7,15},{15,7},{20,28},{2... | collective-permute-start | bytes 4718600 | tf_op jit(solution)/shard_map/ppermute | solution.py:38
  196.7 20.0 %collective-permute-start.30 = (bf16[384,384]{1,0:T(8,128)(2,1)S(1)}, bf16[384,384]{1,0:T(8,128)(2,1)S(1)}, u32[]{:S(2)}, u32[]{:S(2)}) collective-permute-start(bf16[384,384]{1,0:T(8,128)(2,1)S(1)} %fusion), channel_id=1, source_target_pairs={{0,8},{4,12},{8,0},{12,4},{1,9},{5,13},{9,1},{13,5},{2,10},{6,14},... | collective-permute-start | bytes 884744 | tf_op jit(solution)/shard_map/ppermute | solution.py:38
  (21 other events, 199.3 us)
